TPU v7x, 256 devices: a whole 4x4x8 slice. The times are simulated.
256 devices in a mesh: gx: 8 (over y, core), gy: 4 (over x), gz: 8 (over z).
Axes of the slice: x: 4, y: 4, z: 8, core: 2. Of those that a mesh axis runs over, the one named last changes fastest.
Arguments:
- right_side: float32 [128, 128, 512], P('gx', 'gz', 'gy'), may hold values from -8 to 8
- sigma: float32 [128, 128, 512], P('gx', 'gz', 'gy'), may hold values from 0.25 to 4
Outputs:
- solution_field: float32 [128, 128, 512], P('gx', 'gz', 'gy')
- residual: float32 [128, 128, 512], P('gx', 'gz', 'gy')
All inputs are finite; a program needn't handle non-finite values.
Results may differ from a plain program's by a relative error of at most 0.0003.
Values sent between devices are 32-bit elements; how exact they have to be, the bound alone decides.
No kernel may reach another device: no remote copies, remote signals or barrier semaphores. Data moves between devices by JAX's collectives and lax.ppermute only.
A program may use at most 128 MiB of HBM per device.

v0:
```python
import functools

import jax
import jax.numpy as jnp
from jax import lax
from jax.experimental import pallas as pl
from jax.experimental.pallas import tpu as pltpu
from jax.sharding import PartitionSpec as P

NU = 2
BOTTOM = 8
F32 = jnp.float32
LANES = 128
STRIP = 8
PER = LANES // STRIP

H0, X0, Z0 = 5, 26, 32
H1, X1, Z1 = 7, 22, 24


def roll(v, shift, axis):
    return pltpu.roll(v, shift % v.shape[axis], axis)


def iota(shape, axis):
    return lax.broadcasted_iota(jnp.int32, shape, axis)


def exact_dot(a, b):
    return jnp.dot(a, b, precision=lax.Precision.HIGHEST, preferred_element_type=F32)


def halving(width):
    k, l = iota((width, LANES), 0), iota((width, LANES), 1)
    return jnp.where(k // 2 == l, 0.125, 0.0).astype(F32)


def doubling(width):
    k, l = iota((LANES, width), 0), iota((LANES, width), 1)
    return jnp.where(l // 2 == k, 1.0, 0.0).astype(F32)


def reds(shape, parity):
    return (iota(shape, 0) + iota(shape, 1)) % 2 == parity % 2


def couplings(s_ref, f_ref, c_ref, g_ref, w_ref, first, last, scale, so=0, fo=0, edges=False):
    shape = s_ref.shape[1:]
    if edges:
        z, y = iota(shape, 0), iota(shape, 1)
        walls = (None, None, z == shape[0] - 1, z == 0, y == shape[1] - 1, y == 0)

    def body(x, carry):
        centre = s_ref[x + so]
        near = [
            s_ref[x + so + 1],
            s_ref[x + so - 1],
            roll(centre, -1, 0),
            roll(centre, 1, 0),
            roll(centre, -1, 1),
            roll(centre, 1, 1),
        ]
        if edges:
            near = [v if wall is None else jnp.where(wall, 0.0, v) for v, wall in zip(near, walls)]
        betas = [0.5 * (centre + v) for v in near]
        total = ((betas[0] + betas[1]) + (betas[2] + betas[3])) + (betas[4] + betas[5])
        inverse = jnp.where(centre > 0.0, 1.0 / total, 0.0)
        for d in range(6):
            c = betas[d] * inverse
            if edges and walls[d] is not None:
                c = jnp.where(walls[d], 0.0, c)
            c_ref[d, x] = c
        g_ref[x] = f_ref[x + fo] * (inverse * scale)
        w_ref[x] = total * (1.0 / scale)
        return carry

    lax.fori_loop(first, last, body, 0)


def relaxed(u, c_ref, g_ref, x):
    low, centre, high = u
    a = c_ref[0, x] * high + c_ref[1, x] * low
    b = c_ref[2, x] * roll(centre, -1, 0) + c_ref[3, x] * roll(centre, 1, 0)
    d = c_ref[4, x] * roll(centre, -1, 1) + c_ref[5, x] * roll(centre, 1, 1)
    return g_ref[x] + ((a + b) + d)


def half_sweep(u_ref, c_ref, g_ref, first, last, parity, uo=0):
    shape = u_ref.shape[1:]

    def body(i, carry):
        x = first + 2 * i
        masks = (reds(shape, parity + first), reds(shape, parity + first + 1))
        u = [u_ref[x + uo + k] for k in (-1, 0, 1, 2)]
        u_ref[x + uo] = jnp.where(masks[0], relaxed(u[0:3], c_ref, g_ref, x), u[1])
        u_ref[x + uo + 1] = jnp.where(masks[1], relaxed(u[1:4], c_ref, g_ref, x + 1), u[2])
        return carry

    lax.fori_loop(0, (last - first) // 2, body, 0)


def first_half_sweep(u_ref, g_ref, first, last, parity, uo=0):
    shape = u_ref.shape[1:]

    def body(i, carry):
        x = first + 2 * i
        for k in range(2):
            u_ref[x + uo + k] = jnp.where(reds(shape, parity + first + k), g_ref[x + k], 0.0)
        return carry

    lax.fori_loop(0, (last - first) // 2, body, 0)


def residual_plane(u_ref, c_ref, g_ref, w_ref, x, uo=0):
    u = [u_ref[x + uo + k] for k in (-1, 0, 1)]
    return w_ref[x] * (relaxed(u, c_ref, g_ref, x) - u[1])


def pack_body(width, e_ref, lo_ref, hi_ref):
    planes, rows, _ = e_ref.shape
    group = iota((rows, LANES), 1) // STRIP
    for q in range(lo_ref.shape[0]):
        lo = hi = jnp.zeros((rows, LANES), F32)
        for k in range(min(PER, planes - q * PER)):
            v = e_ref[q * PER + k]
            lo = jnp.where(group == k, roll(v, STRIP * k, 1), lo)
            hi = jnp.where(group == k, roll(v, STRIP * (k + 1) - width, 1), hi)
        lo_ref[q] = lo
        hi_ref[q] = hi


def pack(width, *fields):
    shapes = [jax.ShapeDtypeStruct((-(-f.shape[0] // PER),) + f.shape[1:], F32) for f in fields]

    def kernel(*refs):
        n = len(fields)
        for i in range(n):
            pack_body(width[i], refs[i], refs[n + 2 * i], refs[n + 2 * i + 1])

    return call(kernel, [s for s in shapes for _ in range(2)], [])(*fields)


def unpacked(lo_ref, hi_ref, p, high_at):
    q, k = p // PER, p % PER
    lane = iota(lo_ref.shape[1:], 1)
    high = roll(hi_ref[q], high_at - STRIP * k, 1)
    low = roll(lo_ref[q], LANES - STRIP - STRIP * k, 1)
    inside = jnp.logical_and(lane >= high_at, lane < high_at + STRIP)
    return jnp.where(inside, high, jnp.where(lane >= LANES - STRIP, low, 0.0))


def fill_wide(out_ref, e_ref, lo_ref, hi_ref, base, planes):
    for x in range(planes):
        out_ref[x, :, :LANES] = e_ref[base + x]
        out_ref[x, :, LANES:] = unpacked(lo_ref, hi_ref, base + x, 0)


def fill_narrow(out_ref, e_ref, lo_ref, hi_ref, base, planes):
    half = LANES // 2
    lane = iota(e_ref.shape[1:], 1)
    for x in range(planes):
        out_ref[x] = jnp.where(lane < half, e_ref[base + x], unpacked(lo_ref, hi_ref, base + x, half))


def call(kernel, out_shape, scratch, smem=0):
    def run(*args):
        specs = [pl.BlockSpec(memory_space=pltpu.SMEM)] * smem
        specs += [pl.BlockSpec(memory_space=pltpu.VMEM)] * (len(args) - smem)
        return pl.pallas_call(
            kernel,
            out_shape=out_shape,
            in_specs=specs,
            out_specs=jax.tree.map(lambda _: pl.BlockSpec(memory_space=pltpu.VMEM), out_shape),
            scratch_shapes=scratch,
            compiler_params=pltpu.CompilerParams(vmem_limit_bytes=40 * 2**20),
        )(*args)

    return run


def vmem(*shape):
    return pltpu.VMEM(shape, F32)


def descend0(e_ref, lo_ref, hi_ref, u_out, next_out, s, f, c, g, w, u, q):
    fill_wide(f, e_ref, lo_ref, hi_ref, 0, X0)
    fill_wide(s, e_ref, lo_ref, hi_ref, X0, X0)
    couplings(s, f, c, g, w, 1, X0 - 1, 1.0)
    first_half_sweep(u, g, 1, X0 - 1, H0)
    half_sweep(u, c, g, 2, X0 - 2, H0 + 1)
    half_sweep(u, c, g, 3, X0 - 3, H0)
    half_sweep(u, c, g, 4, X0 - 4, H0 + 1)

    def body(i, carry):
        x = H0 + 2 * i
        r = residual_plane(u, c, g, w, x) + residual_plane(u, c, g, w, x + 1)
        q[0, i] = r[8:24, :LANES]
        q[1, i] = s[x, 8:24, :LANES] + s[x + 1, 8:24, :LANES]
        u_out[2 * i] = u[x, 8:24, :LANES]
        u_out[2 * i + 1] = u[x + 1, 8:24, :LANES]
        return carry

    lax.fori_loop(0, 8, body, 0)
    pairs = q[:, :, pl.ds(0, 8, stride=2), :] + q[:, :, pl.ds(1, 8, stride=2), :]
    next_out[...] = exact_dot(pairs.reshape(128, LANES), halving(LANES)).reshape(2, 8, 8, LANES)


def descend1(e_ref, lo_ref, hi_ref, u_out, tile_out, s, f, c, g, w, u, q, t):
    fill_narrow(f, e_ref, lo_ref, hi_ref, 0, X1)
    fill_narrow(s, e_ref, lo_ref, hi_ref, X1, X1)
    couplings(s, f, c, g, w, 3, X1 - 3, 4.0)
    first_half_sweep(u, g, 3, X1 - 3, H1)
    half_sweep(u, c, g, 4, X1 - 4, H1 + 1)
    half_sweep(u, c, g, 5, X1 - 5, H1)
    half_sweep(u, c, g, 6, X1 - 6, H1 + 1)
    k, l = iota((LANES, LANES), 0), iota((LANES, LANES), 1)
    total = jnp.zeros((8, LANES), F32)
    for i in range(4):
        x = H1 + 2 * i
        r = residual_plane(u, c, g, w, x) + residual_plane(u, c, g, w, x + 1)
        q[0] = r[8:16]
        q[1] = s[x, 8:16] + s[x + 1, 8:16]
        u_out[2 * i] = u[x, 8:16]
        u_out[2 * i + 1] = u[x + 1, 8:16]
        for b in range(2):
            t[4 * b : 4 * b + 4] = q[b, pl.ds(0, 4, stride=2), :] + q[b, pl.ds(1, 4, stride=2), :]
        place = jnp.where(jnp.logical_and(k < 64, l == 32 * i + k // 2), 0.125, 0.0).astype(F32)
        total = total + exact_dot(t[...], place)
    tile_out[...] = total


def coarse(where_ref, all_ref, out_ref, s2, f2, c2, g2, w2, u2, q2, d2, s3, f3, c3, g3, w3, u3, q3, d3, s4, f4, c4, g4, w4, u4):
    lane = iota((8, LANES), 1)
    row = iota((8, LANES), 0)
    zero2 = jnp.zeros((32, LANES), F32)

    def assemble(ix, carry):
        for zt in range(4):
            sides = []
            for iz in (2 * zt, 2 * zt + 1):
                tiles = [all_ref[(ix * 4 + iy) * 8 + iz] for iy in range(4)]
                merged = []
                for xl in range(4):
                    v = roll(tiles[0], -32 * xl, 1)
                    for iy in range(1, 4):
                        v = jnp.where(lane // 32 == iy, roll(tiles[iy], 32 * (iy - xl), 1), v)
                    merged.append(v)
                sides.append(merged)
            for xl in range(4):
                even, odd = sides[0][xl], sides[1][xl]
                f2[ix * 4 + xl, 8 * zt : 8 * zt + 8] = jnp.where(row < 4, even, roll(odd, 4, 0))
                s2[ix * 4 + xl + 1, 8 * zt : 8 * zt + 8] = jnp.where(row < 4, roll(even, 4, 0), odd)
        return carry

    lax.fori_loop(0, 8, assemble, 0)
    s2[0] = zero2
    s2[33] = zero2
    for x in (0, 1, 2, 3, 36, 37, 38, 39):
        u2[x] = zero2
    for x in (0, 17):
        s3[x] = zero2[:16]
        u3[x] = zero2[:16]
    for x in (0, 9):
        s4[x] = zero2[:8]
        u4[x] = zero2[:8]

    def down(s, f, c, g, w, u, uo, n, scale, q, s_next, f_next):
        couplings(s, f, c, g, w, 0, n, scale, so=1, edges=True)
        first_half_sweep(u, g, 0, n, 0, uo)
        half_sweep(u, c, g, 0, n, 1, uo)
        half_sweep(u, c, g, 0, n, 0, uo)
        half_sweep(u, c, g, 0, n, 1, uo)
        half = n // 2

        def body(i, carry):
            x = 2 * i
            q[0, i] = residual_plane(u, c, g, w, x, uo) + residual_plane(u, c, g, w, x + 1, uo)
            q[1, i] = s[x + 1] + s[x + 2]
            return carry

        lax.fori_loop(0, half, body, 0)
        pairs = q[:, :, pl.ds(0, half, stride=2), :] + q[:, :, pl.ds(1, half, stride=2), :]
        fine = exact_dot(pairs.reshape(2 * half * half, LANES), halving(LANES)).reshape(2, half, half, LANES)
        f_next[...] = fine[0]
        s_next[1 : half + 1] = fine[1]

    def up(c, g, u, uo, n, u_next, no, d):
        half = n // 2
        twice = exact_dot(u_next[no : no + half].reshape(half * half, LANES), doubling(LANES))
        twice = twice.reshape(half, half, LANES)
        d[:, pl.ds(0, half, stride=2), :] = twice
        d[:, pl.ds(1, half, stride=2), :] = twice

        def body(i, carry):
            for k in range(2):
                u[2 * i + k + uo] = u[2 * i + k + uo] + d[i]
            return carry

        lax.fori_loop(0, half, body, 0)
        for _ in range(NU):
            half_sweep(u, c, g, 0, n, 0, uo)
            half_sweep(u, c, g, 0, n, 1, uo)

    down(s2, f2, c2, g2, w2, u2, 4, 32, 16.0, q2, s3, f3)
    down(s3, f3, c3, g3, w3, u3, 1, 16, 64.0, q3, s4, f4)
    couplings(s4, f4, c4, g4, w4, 0, 8, 256.0, so=1, edges=True)
    first_half_sweep(u4, g4, 0, 8, 0, 1)
    half_sweep(u4, c4, g4, 0, 8, 1, 1)

    def more(i, carry):
        half_sweep(u4, c4, g4, 0, 8, 0, 1)
        half_sweep(u4, c4, g4, 0, 8, 1, 1)
        return carry

    lax.fori_loop(0, BOTTOM - 1, more, 0)
    up(c3, g3, u3, 1, 16, u4, 1, d3)
    up(c2, g2, u2, 4, 32, u3, 1, d2)
    ix, iy, iz = where_ref[0], where_ref[1], where_ref[2]
    down_z = lax.rem(36 - 4 * iz, 32)
    down_y = lax.rem(LANES - 32 * iy, LANES)
    for x in range(12):
        v = pltpu.roll(u2[ix * 4 + x], down_z, 0)
        out_ref[x] = pltpu.roll(v[:16], down_y, 1)


def ascend(e0, lo0, hi0, e1, lo1, hi1, v0, vlo0, vhi0, v1, vlo1, vhi1, win, u_out, r_out, s, f, c, g, w, u, t0, d0, sl, fl, cl, gl, wl, ul, t1, d1):
    fill_narrow(fl, e1, lo1, hi1, 0, X1)
    fill_narrow(sl, e1, lo1, hi1, X1, X1)
    fill_narrow(ul, v1, vlo1, vhi1, 0, X1)
    couplings(sl, fl, cl, gl, wl, 1, X1 - 1, 4.0)
    k, l = iota((LANES, LANES), 0), iota((LANES, LANES), 1)
    widen = jnp.where(k == jnp.where(l < 96, l // 2, 64 + l // 2), 1.0, 0.0).astype(F32)
    t1[...] = exact_dot(win[...].reshape(192, LANES), widen).reshape(12, 16, LANES)
    d1[:, pl.ds(0, 12, stride=2), :] = t1[:, :12]
    d1[:, pl.ds(1, 12, stride=2), :] = t1[:, :12]
    for x in range(X1):
        ul[x] = jnp.where(sl[x] > 0.0, ul[x] + d1[(x + 1) // 2], 0.0)
    half_sweep(ul, cl, gl, 1, X1 - 1, H1)
    half_sweep(ul, cl, gl, 2, X1 - 2, H1 + 1)
    half_sweep(ul, cl, gl, 3, X1 - 3, H1)
    half_sweep(ul, cl, gl, 4, X1 - 4, H1 + 1)
    fill_wide(f, e0, lo0, hi0, 0, X0)
    fill_wide(s, e0, lo0, hi0, X0, X0)
    fill_wide(u, v0, vlo0, vhi0, 0, X0)
    couplings(s, f, c, g, w, 1, X0 - 1, 1.0)
    t0[...] = exact_dot(ul[4:18].reshape(14 * Z1, LANES), doubling(2 * LANES)).reshape(14, Z1, 2 * LANES)
    for half in range(2):
        lanes = slice(half * LANES, half * LANES + LANES)
        d0[half, :, pl.ds(0, 16, stride=2), :] = t0[:, 4:20, lanes]
        d0[half, :, pl.ds(1, 16, stride=2), :] = t0[:, 4:20, lanes]
    for x in range(X0):
        for half in range(2):
            lanes = slice(half * LANES, half * LANES + LANES)
            u[x, :, lanes] = jnp.where(s[x, :, lanes] > 0.0, u[x, :, lanes] + d0[half, (x + 1) // 2], 0.0)
    half_sweep(u, c, g, 1, X0 - 1, H0)
    half_sweep(u, c, g, 2, X0 - 2, H0 + 1)
    half_sweep(u, c, g, 3, X0 - 3, H0)
    half_sweep(u, c, g, 4, X0 - 4, H0 + 1)

    def body(i, carry):
        x = H0 + i
        u_out[i] = u[x, 8:24, :LANES]
        r_out[i] = residual_plane(u, c, g, w, x)[8:24, :LANES]
        return carry

    lax.fori_loop(0, 16, body, 0)


def swap(low, high, axis):
    count = lax.axis_size(axis)
    even = lax.axis_index(axis) % 2 == 0
    first = [(i, i ^ 1) for i in range(count)]
    second = [(i, i + 1) for i in range(1, count - 1, 2)]
    second += [(j, i) for i, j in second]
    a = lax.ppermute(jnp.where(even, high, low), axis, first)
    b = lax.ppermute(jnp.where(even, low, high), axis, second)
    return jnp.where(even, b, a), jnp.where(even, a, b)


def join(pieces):
    return jnp.concatenate([p.reshape(-1, 8, LANES) for p in pieces], 0)


def split(joined, like):
    out, at = [], 0
    for p in like:
        n = p.size // (8 * LANES)
        out.append(joined[at : at + n].reshape(p.shape))
        at += n
    return out


def swap_many(lows, highs, axis):
    low, high = swap(join(lows), join(highs), axis)
    return split(low, lows), split(high, highs)


def extend(fields, rows, planes, widths):
    lows = [f[:, :, :8] for f in fields]
    highs = [f[:, :, -8:] for f in fields]
    lows, highs = swap_many(lows, highs, "gz")
    fields = [jnp.concatenate([a, f, b], 2) for a, f, b in zip(lows, fields, highs)]
    lows = [f[:, :h] for f, h in zip(fields, planes)]
    highs = [f[:, -h:] for f, h in zip(fields, planes)]
    lows, highs = swap_many(lows, highs, "gx")
    fields = [jnp.concatenate([a, f, b], 1) for a, f, b in zip(lows, fields, highs)]
    fields = [f.reshape((-1,) + f.shape[2:]) for f in fields]
    strips = pack(widths, *fields)
    lows, highs = swap_many(strips[0::2], strips[1::2], "gy")
    return [(f, a, b) for f, a, b in zip(fields, lows, highs)]


def level_scratch(planes, rows, lanes):
    p = (planes, rows, lanes)
    return [vmem(*p), vmem(*p), vmem(6, *p), vmem(*p), vmem(*p), vmem(*p)]


def full_scratch(n, uo):
    p = (n, LANES)
    return [vmem(n + 2, *p), vmem(n, *p), vmem(6, n, *p), vmem(n, *p), vmem(n, *p), vmem(n + 2 * uo, *p)]


def shape(*dims):
    return jax.ShapeDtypeStruct(dims, F32)


def on_device(right_side, sigma):
    ((e0, lo0, hi0),) = extend([jnp.stack([right_side, sigma])], None, [H0], [LANES])
    u0, next1 = call(descend0, [shape(16, 16, LANES), shape(2, 8, 8, LANES)], level_scratch(X0, Z0, 2 * LANES) + [vmem(2, 8, 16, LANES)])(e0, lo0, hi0)
    ((e1, lo1, hi1),) = extend([next1], None, [H1], [LANES // 2])
    u1, tile = call(descend1, [shape(8, 8, LANES), shape(8, LANES)], level_scratch(X1, Z1, LANES) + [vmem(2, 8, LANES), vmem(8, LANES)])(e1, lo1, hi1)
    (v0, vlo0, vhi0), (v1, vlo1, vhi1) = extend([u0[None], u1[None]], None, [H0, H1], [LANES, LANES // 2])
    every = lax.all_to_all(jnp.broadcast_to(tile[None], (256, 8, LANES)), ("gx", "gy", "gz"), 0, 0)
    place = jnp.stack([lax.axis_index("gx"), lax.axis_index("gy"), lax.axis_index("gz")]).astype(jnp.int32)
    window = call(
        coarse,
        shape(12, 16, LANES),
        full_scratch(32, 4)
        + [vmem(2, 16, 32, LANES), vmem(16, 32, LANES)]
        + full_scratch(16, 1)
        + [vmem(2, 8, 16, LANES), vmem(8, 16, LANES)]
        + full_scratch(8, 1),
        smem=1,
    )(place, every)
    return call(
        ascend,
        (shape(16, 16, LANES), shape(16, 16, LANES)),
        level_scratch(X0, Z0, 2 * LANES)
        + [vmem(14, Z1, 2 * LANES), vmem(2, 14, Z0, LANES)]
        + level_scratch(X1, Z1, LANES)
        + [vmem(12, 16, LANES), vmem(12, Z1, LANES)],
    )(e0, lo0, hi0, e1, lo1, hi1, v0, vlo0, vhi0, v1, vlo1, vhi1, window)


def solution(mesh):
    placed = (P("gx", "gz", "gy"), P("gx", "gz", "gy"))
    return jax.shard_map(
        on_device,
        mesh=mesh,
        in_specs=placed,
        out_specs=(P("gx", "gz", "gy"), P("gx", "gz", "gy")),
        check_vma=False,
    )
```

profile of v0, /device:TPU:1, one launch (start us, length us, event | category | flops | bytes accessed | tf_op | source)
XLA Modules:
  0.0 158.3 jit_solution(7617334281627137414)
XLA Ops:
  0.6 1.0 broadcast_select_fusion.9
  1.7 2.6 %collective-permute-start.1 = (f32[32,8,128]{2,1,0:T(8,128)S(1)}, f32[32,8,128]{2,1,0:T(8,128)S(1)}, u32[]{:S(2)}, u32[]{:S(2)}) collective-permute-start(f32[32,8,128]{2,1,0:T(8,128)S(1)} %bitcast.124), channel_id=1, source_target_pairs={{0,1},{1,0},{2,3},{3,2},{4,5},{5,4},{6,7},{7,6},{8,9},{9,8},{10,11... | collective-permute-start | bytes 393224 | tf_op jit(solution)/shard_map/ppermute | solution.py:375
  4.2 0.7 collective-permute-start
  4.9 0.0 copy-start.1
  4.9 0.0 copy-start.2
  4.9 1.7 %collective-permute-done.1 = f32[32,8,128]{2,1,0:T(8,128)S(1)} collective-permute-done((f32[32,8,128]{2,1,0:T(8,128)S(1)}, f32[32,8,128]{2,1,0:T(8,128)S(1)}, u32[]{:S(2)}, u32[]{:S(2)}) %collective-permute-start.1) | collective-permute-done | bytes 131104 | tf_op jit(solution)/shard_map/ppermute | solution.py:375
  6.6 0.0 collective-permute-done
  6.6 0.0 copy-done.1
  6.6 0.0 copy-done.2
  6.7 3.5 %collective-permute-start.3 = (f32[40,8,128]{2,1,0:T(8,128)S(1)}, f32[40,8,128]{2,1,0:T(8,128)S(1)}, u32[]{:S(2)}, u32[]{:S(2)}) collective-permute-start(f32[40,8,128]{2,1,0:T(8,128)S(1)} %bitcast.122), channel_id=1, source_target_pairs={{0,32},{32,0},{64,96},{96,64},{128,160},{160,128},{192,224},{224,1... | collective-permute-start | bytes 491528 | tf_op jit(solution)/shard_map/ppermute | solution.py:375
  10.2 1.9 %collective-permute-start.2 = (f32[40,8,128]{2,1,0:T(8,128)S(1)}, f32[40,8,128]{2,1,0:T(8,128)S(1)}, u32[]{:S(2)}, u32[]{:S(2)}) collective-permute-start(f32[40,8,128]{2,1,0:T(8,128)S(1)} %bitcast.121), channel_id=1, source_target_pairs={{32,64},{96,128},{160,192},{64,32},{128,96},{192,160},{33,65},{97,... | collective-permute-start | bytes 491528 | tf_op jit(solution)/shard_map/ppermute | solution.py:376
  12.1 0.0 collective-permute-done.3
  12.1 5.0 %collective-permute-done.2 = f32[40,8,128]{2,1,0:T(8,128)S(1)} collective-permute-done((f32[40,8,128]{2,1,0:T(8,128)S(1)}, f32[40,8,128]{2,1,0:T(8,128)S(1)}, u32[]{:S(2)}, u32[]{:S(2)}) %collective-permute-start.2) | collective-permute-done | bytes 163872 | tf_op jit(solution)/shard_map/ppermute | solution.py:376
  17.1 0.1 pad_maximum_fusion
  17.2 0.5 shard_map.41
  17.7 0.7 collective-permute-start.4
  18.4 2.2 %collective-permute-start.5 = (f32[16,8,128]{2,1,0:T(8,128)S(1)}, f32[16,8,128]{2,1,0:T(8,128)S(1)}, u32[]{:S(2)}, u32[]{:S(2)}) collective-permute-start(f32[16,8,128]{2,1,0:T(8,128)S(1)} %bitcast.125), channel_id=1, source_target_pairs={{0,8},{8,0},{16,24},{24,16},{1,9},{9,1},{17,25},{25,17},{2,10},{10... | collective-permute-start | bytes 196616 | tf_op jit(solution)/shard_map/ppermute | solution.py:375
  20.6 0.0 collective-permute-done.4
  20.6 1.7 %collective-permute-done.5 = f32[16,8,128]{2,1,0:T(8,128)S(1)} collective-permute-done((f32[16,8,128]{2,1,0:T(8,128)S(1)}, f32[16,8,128]{2,1,0:T(8,128)S(1)}, u32[]{:S(2)}, u32[]{:S(2)}) %collective-permute-start.5) | collective-permute-done | bytes 65568 | tf_op jit(solution)/shard_map/ppermute | solution.py:375
  22.2 7.7 %shard_map.42 = (f32[16,16,128]{2,1,0:T(8,128)S(1)}, f32[2,8,8,128]{3,2,1,0:T(8,128)S(1)}) custom-call(f32[52,32,128]{2,1,0:T(8,128)S(1)} %bitcast.65, f32[4,32,128]{2,1,0:T(8,128)S(1)} %bitcast.75, f32[4,32,128]{2,1,0:T(8,128)S(1)} %bitcast.73), custom_call_target="tpu_custom_call" | custom-call | tf_op jit(solution)/shard_map/pallas_call | solution.py:169
  29.9 5.2 %collective-permute-start.7 = (f32[16,8,128]{2,1,0:T(8,128)S(1)}, f32[16,8,128]{2,1,0:T(8,128)S(1)}, u32[]{:S(2)}, u32[]{:S(2)}) collective-permute-start(f32[16,8,128]{2,1,0:T(8,128)S(1)} %bitcast.83), channel_id=1, source_target_pairs={{0,1},{1,0},{2,3},{3,2},{4,5},{5,4},{6,7},{7,6},{8,9},{9,8},{10,11... | collective-permute-start | bytes 196616 | tf_op jit(solution)/shard_map/ppermute | solution.py:375
  35.2 0.7 collective-permute-start.6
  35.8 1.0 collective-permute-done.7
  36.8 0.0 collective-permute-done.6
  36.9 0.1 collective-permute-start.9
  37.0 5.4 %collective-permute-start.8 = (f32[42,8,128]{2,1,0:T(8,128)S(1)}, f32[42,8,128]{2,1,0:T(8,128)S(1)}, u32[]{:S(2)}, u32[]{:S(2)}) collective-permute-start(f32[42,8,128]{2,1,0:T(8,128)S(1)} %bitcast.119), channel_id=1, source_target_pairs={{32,64},{96,128},{160,192},{64,32},{128,96},{192,160},{33,65},{97,... | collective-permute-start | bytes 516104 | tf_op jit(solution)/shard_map/ppermute | solution.py:376
  42.4 0.0 collective-permute-done.9
  42.4 3.1 %collective-permute-done.8 = f32[42,8,128]{2,1,0:T(8,128)S(1)} collective-permute-done((f32[42,8,128]{2,1,0:T(8,128)S(1)}, f32[42,8,128]{2,1,0:T(8,128)S(1)}, u32[]{:S(2)}, u32[]{:S(2)}) %collective-permute-start.8) | collective-permute-done | bytes 172064 | tf_op jit(solution)/shard_map/ppermute | solution.py:376
  45.5 0.3 shard_map.43
  45.9 0.7 collective-permute-start.10
  46.5 3.4 %collective-permute-start.11 = (f32[9,8,128]{2,1,0:T(8,128)S(1)}, f32[9,8,128]{2,1,0:T(8,128)S(1)}, u32[]{:S(2)}, u32[]{:S(2)}) collective-permute-start(f32[9,8,128]{2,1,0:T(8,128)S(1)} %bitcast.127), channel_id=1, source_target_pairs={{0,8},{8,0},{16,24},{24,16},{1,9},{9,1},{17,25},{25,17},{2,10},{10... | collective-permute-start | bytes 110600 | tf_op jit(solution)/shard_map/ppermute | solution.py:375
  49.9 0.0 collective-permute-done.10
  50.0 1.3 collective-permute-done.11
  51.3 3.7 %shard_map.44 = (f32[8,8,128]{2,1,0:T(8,128)S(1)}, f32[8,128]{1,0:T(8,128)S(1)}) custom-call(f32[44,24,128]{2,1,0:T(8,128)S(1)} %bitcast.68, f32[3,24,128]{2,1,0:T(8,128)S(1)} %bitcast.79, f32[3,24,128]{2,1,0:T(8,128)S(1)} %bitcast.77), custom_call_target="tpu_custom_call" | custom-call | tf_op jit(solution)/shard_map/pallas_call | solution.py:169
  55.0 0.7 collective-permute-start.12
  55.7 8.5 %collective-permute-start.13 = (f32[24,8,128]{2,1,0:T(8,128)S(1)}, f32[24,8,128]{2,1,0:T(8,128)S(1)}, u32[]{:S(2)}, u32[]{:S(2)}) collective-permute-start(f32[24,8,128]{2,1,0:T(8,128)S(1)} %get-tuple-element.48), channel_id=1, source_target_pairs={{0,1},{1,0},{2,3},{3,2},{4,5},{5,4},{6,7},{7,6},{8,9},{9,8},{10,11... | collective-permute-start | bytes 294920 | tf_op jit(solution)/shard_map/ppermute | solution.py:375
  64.2 1.1 broadcast_in_dim.14
  65.2 13.4 %all-to-all-start = ((f32[256,8,128]{2,1,0:T(8,128)}), f32[256,8,128]{2,1,0:T(8,128)S(1)}, u32[]{:S(2)}, u32[]{:S(2)}) async-start(f32[256,8,128]{2,1,0:T(8,128)} %broadcast_in_dim.14), calls=%async_computation | async-start | bytes 2097152 | tf_op jit(solution)/shard_map/all_to_all | solution.py:433
  78.6 0.0 collective-permute-done.12
  78.6 0.0 collective-permute-done.13
  78.8 3.5 %collective-permute-start.14 = (f32[41,8,128]{2,1,0:T(8,128)S(1)}, f32[41,8,128]{2,1,0:T(8,128)S(1)}, u32[]{:S(2)}, u32[]{:S(2)}) collective-permute-start(f32[41,8,128]{2,1,0:T(8,128)S(1)} %get-tuple-element.33), channel_id=1, source_target_pairs={{32,64},{96,128},{160,192},{64,32},{128,96},{192,160},{33,65},{97,... | collective-permute-start | bytes 503816 | tf_op jit(solution)/shard_map/ppermute | solution.py:376
  82.4 0.1 collective-permute-start.15
  82.5 4.3 %collective-permute-done.14 = f32[41,8,128]{2,1,0:T(8,128)S(1)} collective-permute-done((f32[41,8,128]{2,1,0:T(8,128)S(1)}, f32[41,8,128]{2,1,0:T(8,128)S(1)}, u32[]{:S(2)}, u32[]{:S(2)}) %collective-permute-start.14) | collective-permute-done | bytes 167968 | tf_op jit(solution)/shard_map/ppermute | solution.py:376
  86.8 0.0 collective-permute-done.15
  87.0 0.4 shard_map.45
  87.4 1.6 collective-permute-start.17
  89.0 0.8 collective-permute-start.16
  89.8 0.6 pad_add_fusion.where_ref
  90.5 0.9 collective-permute-done.17
  91.3 0.0 collective-permute-done.16
  91.4 19.6 %all-to-all-done.all_ref = f32[256,8,128]{2,1,0:T(8,128)S(1)} async-done(((f32[256,8,128]{2,1,0:T(8,128)}), f32[256,8,128]{2,1,0:T(8,128)S(1)}, u32[]{:S(2)}, u32[]{:S(2)}) %all-to-all-start) | async-done | bytes 1048608 | tf_op jit(solution)/shard_map/all_to_all | solution.py:433
  111.0 0.0 copy-start
  111.0 0.7 copy-done
  111.6 30.4 %shard_map.46.win = f32[12,16,128]{2,1,0:T(8,128)S(1)} custom-call(s32[3]{0:T(128)S(1)} %copy-done, f32[256,8,128]{2,1,0:T(8,128)S(1)} %all-to-all-done.all_ref), custom_call_target="tpu_custom_call" | custom-call | tf_op jit(solution)/shard_map/pallas_call | solution.py:169
  142.0 16.3 %shard_map.47 = (f32[16,16,128]{2,1,0:T(8,128)}, f32[16,16,128]{2,1,0:T(8,128)}) custom-call(f32[52,32,128]{2,1,0:T(8,128)S(1)} %bitcast.66, f32[4,32,128]{2,1,0:T(8,128)S(1)} %bitcast.76, f32[4,32,128]{2,1,0:T(8,128)S(1)} %bitcast.74, f32[44,24,128]{2,1,0:T(8,128)S(1)} %bitcast.69, f32[3,24,128]{2,1,0:T(8,128)S(1)} %bitcast.80, f32[3,24,128]{2,1,0:T(8,128)S(1)} %bitcast.78, ...), custom_call_target="tpu_custom_call" | custom-call | tf_op jit(solution)/shard_map/pallas_call | solution.py:169
  (35 shorter events, 0.6 us)
Async XLA Ops:
  1.7 4.9 %collective-permute-start.1 = (f32[32,8,128]{2,1,0:T(8,128)S(1)}, f32[32,8,128]{2,1,0:T(8,128)S(1)}, u32[]{:S(2)}, u32[]{:S(2)}) collective-permute-start(f32[32,8,128]{2,1,0:T(8,128)S(1)} %bitcast.124), channel_id=1, source_target_pairs={{0,1},{1,0},{2,3},{3,2},{4,5},{5,4},{6,7},{7,6},{8,9},{9,8},{10,11... | collective-permute-start | bytes 393224 | tf_op jit(solution)/shard_map/ppermute | solution.py:375
  4.2 2.4 %collective-permute-start = (f32[32,8,128]{2,1,0:T(8,128)S(1)}, f32[32,8,128]{2,1,0:T(8,128)S(1)}, u32[]{:S(2)}, u32[]{:S(2)}) collective-permute-start(f32[32,8,128]{2,1,0:T(8,128)S(1)} %bitcast.123), channel_id=1, source_target_pairs={{1,2},{3,4},{5,6},{2,1},{4,3},{6,5},{9,10},{11,12},{13,14},{10,9},... | collective-permute-start | bytes 393224 | tf_op jit(solution)/shard_map/ppermute | solution.py:376
  4.9 1.7 %copy-start.1 = (f32[16,16,128]{2,1,0:T(8,128)S(1)}, f32[16,16,128]{2,1,0:T(8,128)}, u32[]{:S(2)}) copy-start(f32[16,16,128]{2,1,0:T(8,128)} %param.3) | copy-start | bytes 393220
  4.9 1.7 %copy-start.2 = (f32[16,16,128]{2,1,0:T(8,128)S(1)}, f32[16,16,128]{2,1,0:T(8,128)}, u32[]{:S(2)}) copy-start(f32[16,16,128]{2,1,0:T(8,128)} %param.2) | copy-start | bytes 393220
  6.7 5.4 %collective-permute-start.3 = (f32[40,8,128]{2,1,0:T(8,128)S(1)}, f32[40,8,128]{2,1,0:T(8,128)S(1)}, u32[]{:S(2)}, u32[]{:S(2)}) collective-permute-start(f32[40,8,128]{2,1,0:T(8,128)S(1)} %bitcast.122), channel_id=1, source_target_pairs={{0,32},{32,0},{64,96},{96,64},{128,160},{160,128},{192,224},{224,1... | collective-permute-start | bytes 491528 | tf_op jit(solution)/shard_map/ppermute | solution.py:375
  10.2 6.9 %collective-permute-start.2 = (f32[40,8,128]{2,1,0:T(8,128)S(1)}, f32[40,8,128]{2,1,0:T(8,128)S(1)}, u32[]{:S(2)}, u32[]{:S(2)}) collective-permute-start(f32[40,8,128]{2,1,0:T(8,128)S(1)} %bitcast.121), channel_id=1, source_target_pairs={{32,64},{96,128},{160,192},{64,32},{128,96},{192,160},{33,65},{97,... | collective-permute-start | bytes 491528 | tf_op jit(solution)/shard_map/ppermute | solution.py:376
  17.7 2.8 %collective-permute-start.4 = (f32[16,8,128]{2,1,0:T(8,128)S(1)}, f32[16,8,128]{2,1,0:T(8,128)S(1)}, u32[]{:S(2)}, u32[]{:S(2)}) collective-permute-start(f32[16,8,128]{2,1,0:T(8,128)S(1)} %bitcast.126), channel_id=1, source_target_pairs={{8,16},{16,8},{9,17},{17,9},{10,18},{18,10},{11,19},{19,11},{12,20... | collective-permute-start | bytes 196616 | tf_op jit(solution)/shard_map/ppermute | solution.py:376
  18.4 3.8 %collective-permute-start.5 = (f32[16,8,128]{2,1,0:T(8,128)S(1)}, f32[16,8,128]{2,1,0:T(8,128)S(1)}, u32[]{:S(2)}, u32[]{:S(2)}) collective-permute-start(f32[16,8,128]{2,1,0:T(8,128)S(1)} %bitcast.125), channel_id=1, source_target_pairs={{0,8},{8,0},{16,24},{24,16},{1,9},{9,1},{17,25},{25,17},{2,10},{10... | collective-permute-start | bytes 196616 | tf_op jit(solution)/shard_map/ppermute | solution.py:375
  29.9 6.9 %collective-permute-start.7 = (f32[16,8,128]{2,1,0:T(8,128)S(1)}, f32[16,8,128]{2,1,0:T(8,128)S(1)}, u32[]{:S(2)}, u32[]{:S(2)}) collective-permute-start(f32[16,8,128]{2,1,0:T(8,128)S(1)} %bitcast.83), channel_id=1, source_target_pairs={{0,1},{1,0},{2,3},{3,2},{4,5},{5,4},{6,7},{7,6},{8,9},{9,8},{10,11... | collective-permute-start | bytes 196616 | tf_op jit(solution)/shard_map/ppermute | solution.py:375
  35.2 1.7 %collective-permute-start.6 = (f32[16,8,128]{2,1,0:T(8,128)S(1)}, f32[16,8,128]{2,1,0:T(8,128)S(1)}, u32[]{:S(2)}, u32[]{:S(2)}) collective-permute-start(f32[16,8,128]{2,1,0:T(8,128)S(1)} %bitcast.84), channel_id=1, source_target_pairs={{1,2},{3,4},{5,6},{2,1},{4,3},{6,5},{9,10},{11,12},{13,14},{10,9},... | collective-permute-start | bytes 196616 | tf_op jit(solution)/shard_map/ppermute | solution.py:376
  36.9 5.5 %collective-permute-start.9 = (f32[42,8,128]{2,1,0:T(8,128)S(1)}, f32[42,8,128]{2,1,0:T(8,128)S(1)}, u32[]{:S(2)}, u32[]{:S(2)}) collective-permute-start(f32[42,8,128]{2,1,0:T(8,128)S(1)} %bitcast.120), channel_id=1, source_target_pairs={{0,32},{32,0},{64,96},{96,64},{128,160},{160,128},{192,224},{224,1... | collective-permute-start | bytes 516104 | tf_op jit(solution)/shard_map/ppermute | solution.py:375
  37.0 8.4 %collective-permute-start.8 = (f32[42,8,128]{2,1,0:T(8,128)S(1)}, f32[42,8,128]{2,1,0:T(8,128)S(1)}, u32[]{:S(2)}, u32[]{:S(2)}) collective-permute-start(f32[42,8,128]{2,1,0:T(8,128)S(1)} %bitcast.119), channel_id=1, source_target_pairs={{32,64},{96,128},{160,192},{64,32},{128,96},{192,160},{33,65},{97,... | collective-permute-start | bytes 516104 | tf_op jit(solution)/shard_map/ppermute | solution.py:376
  45.9 4.1 %collective-permute-start.10 = (f32[9,8,128]{2,1,0:T(8,128)S(1)}, f32[9,8,128]{2,1,0:T(8,128)S(1)}, u32[]{:S(2)}, u32[]{:S(2)}) collective-permute-start(f32[9,8,128]{2,1,0:T(8,128)S(1)} %bitcast.128), channel_id=1, source_target_pairs={{8,16},{16,8},{9,17},{17,9},{10,18},{18,10},{11,19},{19,11},{12,20... | collective-permute-start | bytes 110600 | tf_op jit(solution)/shard_map/ppermute | solution.py:376
  46.5 4.8 %collective-permute-start.11 = (f32[9,8,128]{2,1,0:T(8,128)S(1)}, f32[9,8,128]{2,1,0:T(8,128)S(1)}, u32[]{:S(2)}, u32[]{:S(2)}) collective-permute-start(f32[9,8,128]{2,1,0:T(8,128)S(1)} %bitcast.127), channel_id=1, source_target_pairs={{0,8},{8,0},{16,24},{24,16},{1,9},{9,1},{17,25},{25,17},{2,10},{10... | collective-permute-start | bytes 110600 | tf_op jit(solution)/shard_map/ppermute | solution.py:375
  55.0 23.7 %collective-permute-start.12 = (f32[24,8,128]{2,1,0:T(8,128)S(1)}, f32[24,8,128]{2,1,0:T(8,128)S(1)}, u32[]{:S(2)}, u32[]{:S(2)}) collective-permute-start(f32[24,8,128]{2,1,0:T(8,128)S(1)} %get-tuple-element.47), channel_id=1, source_target_pairs={{1,2},{3,4},{5,6},{2,1},{4,3},{6,5},{9,10},{11,12},{13,14},{10,9},... | collective-permute-start | bytes 294920 | tf_op jit(solution)/shard_map/ppermute | solution.py:376
  55.7 23.0 %collective-permute-start.13 = (f32[24,8,128]{2,1,0:T(8,128)S(1)}, f32[24,8,128]{2,1,0:T(8,128)S(1)}, u32[]{:S(2)}, u32[]{:S(2)}) collective-permute-start(f32[24,8,128]{2,1,0:T(8,128)S(1)} %get-tuple-element.48), channel_id=1, source_target_pairs={{0,1},{1,0},{2,3},{3,2},{4,5},{5,4},{6,7},{7,6},{8,9},{9,8},{10,11... | collective-permute-start | bytes 294920 | tf_op jit(solution)/shard_map/ppermute | solution.py:375
  65.2 45.7 %all-to-all-start = ((f32[256,8,128]{2,1,0:T(8,128)}), f32[256,8,128]{2,1,0:T(8,128)S(1)}, u32[]{:S(2)}, u32[]{:S(2)}) async-start(f32[256,8,128]{2,1,0:T(8,128)} %broadcast_in_dim.14), calls=%async_computation | async-start | bytes 2097152 | tf_op jit(solution)/shard_map/all_to_all | solution.py:433
  78.8 8.0 %collective-permute-start.14 = (f32[41,8,128]{2,1,0:T(8,128)S(1)}, f32[41,8,128]{2,1,0:T(8,128)S(1)}, u32[]{:S(2)}, u32[]{:S(2)}) collective-permute-start(f32[41,8,128]{2,1,0:T(8,128)S(1)} %get-tuple-element.33), channel_id=1, source_target_pairs={{32,64},{96,128},{160,192},{64,32},{128,96},{192,160},{33,65},{97,... | collective-permute-start | bytes 503816 | tf_op jit(solution)/shard_map/ppermute | solution.py:376
  82.4 4.4 %collective-permute-start.15 = (f32[41,8,128]{2,1,0:T(8,128)S(1)}, f32[41,8,128]{2,1,0:T(8,128)S(1)}, u32[]{:S(2)}, u32[]{:S(2)}) collective-permute-start(f32[41,8,128]{2,1,0:T(8,128)S(1)} %get-tuple-element.34), channel_id=1, source_target_pairs={{0,32},{32,0},{64,96},{96,64},{128,160},{160,128},{192,224},{224,1... | collective-permute-start | bytes 503816 | tf_op jit(solution)/shard_map/ppermute | solution.py:375
  87.4 3.9 %collective-permute-start.17 = (f32[14,8,128]{2,1,0:T(8,128)S(1)}, f32[14,8,128]{2,1,0:T(8,128)S(1)}, u32[]{:S(2)}, u32[]{:S(2)}) collective-permute-start(f32[14,8,128]{2,1,0:T(8,128)S(1)} %get-tuple-element.59), channel_id=1, source_target_pairs={{0,8},{8,0},{16,24},{24,16},{1,9},{9,1},{17,25},{25,17},{2,10},{10... | collective-permute-start | bytes 172040 | tf_op jit(solution)/shard_map/ppermute | solution.py:375
  89.0 2.4 %collective-permute-start.16 = (f32[14,8,128]{2,1,0:T(8,128)S(1)}, f32[14,8,128]{2,1,0:T(8,128)S(1)}, u32[]{:S(2)}, u32[]{:S(2)}) collective-permute-start(f32[14,8,128]{2,1,0:T(8,128)S(1)} %get-tuple-element.60), channel_id=1, source_target_pairs={{8,16},{16,8},{9,17},{17,9},{10,18},{18,10},{11,19},{19,11},{12,20... | collective-permute-start | bytes 172040 | tf_op jit(solution)/shard_map/ppermute | solution.py:376
  111.0 0.7 copy-start
where the time goes:
time: 159 us; the launch traced here: 158 us
  Pallas kernels  59.2 us (37%)
  starting transfers between devices  55.4 us (35%)
  waiting for transfers between devices  38.5 us (24%)
  other arithmetic  2.26 us (1%)
  local copies, waits for them, and re-layouts  1.82 us (1%)
    pallas_call x7, Pallas kernels, run(): pl.pallas_call(kernel, out_shape=out_shape, in_specs=specs, out_specs=jax...  59.2 us
    ppermute x9, starting transfers between devices, swap(): a = lax.ppermute(jnp.where(even, high, low), axis, first)  27.1 us
    all_to_all x1, waiting for transfers between devices, on_device(): lax.all_to_all(jnp.broadcast_to(tile[None], (256, 8, LANES)), ('gx', 'gy'...  19.6 us
    ppermute x9, starting transfers between devices, swap(): b = lax.ppermute(jnp.where(even, low, high), axis, second)  14.9 us
    all_to_all x1, starting transfers between devices, on_device(): lax.all_to_all(jnp.broadcast_to(tile[None], (256, 8, LANES)), ('gx', 'gy'...  13.4 us
    ppermute x9, waiting for transfers between devices, swap(): b = lax.ppermute(jnp.where(even, low, high), axis, second)  12.4 us
    ppermute x9, waiting for transfers between devices, swap(): a = lax.ppermute(jnp.where(even, high, low), axis, first)  6.5 us
  transfers between devices with their start and end apart: 19, of which 9 were waited for; matrix products, arithmetic and copies ran while one was open for 1% of the time, Pallas kernels for 0%

commit v1 on v0

v1 whole, which is shorter than its diff:
```python
import functools

import jax
import jax.numpy as jnp
from jax import lax
from jax.experimental import pallas as pl
from jax.experimental.pallas import tpu as pltpu
from jax.sharding import PartitionSpec as P

NU = 2
BOTTOM = 8
F32 = jnp.float32
LANES = 128
STRIP = 8
PER = LANES // STRIP

H0, X0, Z0 = 5, 26, 32
H1, X1, Z1 = 7, 22, 24


def roll(v, shift, axis):
    return pltpu.roll(v, shift % v.shape[axis], axis)


def iota(shape, axis):
    return lax.broadcasted_iota(jnp.int32, shape, axis)


def exact_dot(a, b):
    return jnp.dot(a, b, precision=lax.Precision.HIGHEST, preferred_element_type=F32)


def halving(width):
    k, l = iota((width, LANES), 0), iota((width, LANES), 1)
    return jnp.where(k // 2 == l, 0.125, 0.0).astype(F32)


def doubling(width):
    k, l = iota((LANES, width), 0), iota((LANES, width), 1)
    return jnp.where(l // 2 == k, 1.0, 0.0).astype(F32)


def reds(shape, parity):
    return (iota(shape, 0) + iota(shape, 1)) % 2 == parity % 2


def couplings(s_ref, f_ref, c_ref, g_ref, w_ref, first, last, scale, so=0, edges=False, step=1):
    shape = s_ref.shape[1:]
    if edges:
        z, y = iota(shape, 0), iota(shape, 1)
        walls = (None, None, z == shape[0] - 1, z == 0, y == shape[1] - 1, y == 0)

    def chunk(x, n):
        s = [s_ref[x + so + k] for k in range(-1, n + 1)]
        for k in range(n):
            centre = s[k + 1]
            near = [
                s[k + 2],
                s[k],
                roll(centre, -1, 0),
                roll(centre, 1, 0),
                roll(centre, -1, 1),
                roll(centre, 1, 1),
            ]
            if edges:
                near = [v if wall is None else jnp.where(wall, 0.0, v) for v, wall in zip(near, walls)]
            betas = [0.5 * (centre + v) for v in near]
            total = ((betas[0] + betas[1]) + (betas[2] + betas[3])) + (betas[4] + betas[5])
            inverse = jnp.where(centre > 0.0, 1.0 / total, 0.0)
            for d in range(6):
                c = betas[d] * inverse
                if edges and walls[d] is not None:
                    c = jnp.where(walls[d], 0.0, c)
                c_ref[d, x + k] = c
            g_ref[x + k] = f_ref[x + k] * (inverse * scale)
            w_ref[x + k] = total * (1.0 / scale)

    stepped(chunk, first, last, step)


def stepped(chunk, first, last, step):
    count, rest = divmod(last - first, step)
    if count == 1:
        chunk(first, step)
    elif count:

        def body(i, carry):
            chunk(first + i * step, step)
            return carry

        lax.fori_loop(0, count, body, 0)
    if rest:
        chunk(last - rest, rest)


def relaxed(u, c_ref, g_ref, x):
    low, centre, high = u
    a = c_ref[0, x] * high + c_ref[1, x] * low
    b = c_ref[2, x] * roll(centre, -1, 0) + c_ref[3, x] * roll(centre, 1, 0)
    d = c_ref[4, x] * roll(centre, -1, 1) + c_ref[5, x] * roll(centre, 1, 1)
    return g_ref[x] + ((a + b) + d)


def half_sweep(u_ref, c_ref, g_ref, first, last, parity, uo=0, step=4):
    shape = u_ref.shape[1:]
    masks = (reds(shape, parity + first), reds(shape, parity + first + 1))

    def chunk(x, n):
        u = [u_ref[x + uo + k] for k in range(-1, n + 1)]
        new = [jnp.where(masks[k % 2], relaxed(u[k : k + 3], c_ref, g_ref, x + k), u[k + 1]) for k in range(n)]
        for k in range(n):
            u_ref[x + uo + k] = new[k]

    stepped(chunk, first, last, step)


def first_half_sweep(u_ref, g_ref, first, last, parity, uo=0, step=4):
    shape = u_ref.shape[1:]
    masks = (reds(shape, parity + first), reds(shape, parity + first + 1))

    def chunk(x, n):
        for k in range(n):
            u_ref[x + uo + k] = jnp.where(masks[k % 2], g_ref[x + k], 0.0)

    stepped(chunk, first, last, step)


def residual_planes(u_ref, c_ref, g_ref, w_ref, x, n, uo=0):
    u = [u_ref[x + uo + k] for k in range(-1, n + 1)]
    return [w_ref[x + k] * (relaxed(u[k : k + 3], c_ref, g_ref, x + k) - u[k + 1]) for k in range(n)]


def packed(planes):
    rows = planes[0].shape[0]
    group = iota((rows, LANES), 1) // STRIP
    lo = hi = jnp.zeros((rows, LANES), F32)
    for k, v in enumerate(planes):
        lo = jnp.where(group == k, roll(v, STRIP * k, 1), lo)
        hi = jnp.where(group == k, roll(v, STRIP * (k + 1), 1), hi)
    return lo, hi


def unpacked(low, high, k):
    lane = iota(low.shape, 1)
    high = roll(high, -STRIP * k, 1)
    low = roll(low, LANES - STRIP - STRIP * k, 1)
    return jnp.where(lane < STRIP, high, jnp.where(lane >= LANES - STRIP, low, 0.0))


def fill_wide(out_ref, own, low, high, i):
    for part, at, count, k0 in ((low, 0, H0, 16 - H0), (own, H0, 16, 0), (high, H0 + 16, H0, 0)):
        planes_ref, below_ref, above_ref = part
        for k in range(count):
            out_ref[at + k, :, :LANES] = planes_ref[i, k]
            out_ref[at + k, :, LANES:] = unpacked(below_ref[i], above_ref[i], k0 + k)


def fill_narrow(out_ref, own, low, high, i):
    for part, at, count in ((low, 0, H1), (own, H1, 8), (high, H1 + 8, H1)):
        for k in range(count):
            out_ref[at + k] = part[i, k]


def call(kernel, out_shape, scratch, smem=0):
    def run(*args):
        specs = [pl.BlockSpec(memory_space=pltpu.SMEM)] * smem
        specs += [pl.BlockSpec(memory_space=pltpu.VMEM)] * (len(args) - smem)
        return pl.pallas_call(
            kernel,
            out_shape=out_shape,
            in_specs=specs,
            out_specs=jax.tree.map(lambda _: pl.BlockSpec(memory_space=pltpu.VMEM), out_shape),
            scratch_shapes=scratch,
            compiler_params=pltpu.CompilerParams(vmem_limit_bytes=40 * 2**20),
        )(*args)

    return run


def vmem(*shape):
    return pltpu.VMEM(shape, F32)


def packing(f_ref, s_ref, lo_ref, hi_ref):
    for i, ref in enumerate((f_ref, s_ref)):
        lo_ref[i], hi_ref[i] = packed([ref[k] for k in range(16)])


def descend0(e, el, eh, a, b, al, bl, ah, bh, u_out, ulo_out, uhi_out, next_out, s, f, c, g, w, u, q):
    fill_wide(f, (e, a, b), (el, al, bl), (eh, ah, bh), 0)
    fill_wide(s, (e, a, b), (el, al, bl), (eh, ah, bh), 1)
    couplings(s, f, c, g, w, 1, X0 - 1, 1.0, step=2)
    first_half_sweep(u, g, 1, X0 - 1, H0)
    half_sweep(u, c, g, 2, X0 - 2, H0 + 1)
    half_sweep(u, c, g, 3, X0 - 3, H0)
    half_sweep(u, c, g, 4, X0 - 4, H0 + 1)

    def body(i, carry):
        x = H0 + 4 * i
        r = residual_planes(u, c, g, w, x, 4)
        for k in range(2):
            q[0, 2 * i + k] = (r[2 * k] + r[2 * k + 1])[8:24, :LANES]
            q[1, 2 * i + k] = s[x + 2 * k, 8:24, :LANES] + s[x + 2 * k + 1, 8:24, :LANES]
        for k in range(4):
            u_out[4 * i + k] = u[x + k, 8:24, :LANES]
        return carry

    lax.fori_loop(0, 4, body, 0)
    ulo_out[...], uhi_out[...] = packed([u_out[k] for k in range(16)])
    pairs = q[:, :, pl.ds(0, 8, stride=2), :] + q[:, :, pl.ds(1, 8, stride=2), :]
    k, l = iota((LANES, LANES), 0), iota((LANES, LANES), 1)
    halve_twice = jnp.where(k // 2 == l % 64, 0.125, 0.0).astype(F32)
    next_out[...] = exact_dot(pairs.reshape(128, LANES), halve_twice).reshape(2, 8, 8, LANES)


def descend1(e, el, eh, u_out, tile_out, s, f, c, g, w, u, q, t):
    fill_narrow(f, e, el, eh, 0)
    fill_narrow(s, e, el, eh, 1)
    couplings(s, f, c, g, w, 3, X1 - 3, 4.0, step=4)
    first_half_sweep(u, g, 3, X1 - 3, H1, step=8)
    half_sweep(u, c, g, 4, X1 - 4, H1 + 1, step=8)
    half_sweep(u, c, g, 5, X1 - 5, H1, step=12)
    half_sweep(u, c, g, 6, X1 - 6, H1 + 1, step=10)
    k, l = iota((LANES, LANES), 0), iota((LANES, LANES), 1)
    total = jnp.zeros((8, LANES), F32)
    r = residual_planes(u, c, g, w, H1, 8)
    own = iota((8, LANES), 1) < 64
    for x in range(8):
        v = u[H1 + x, 8:16]
        u_out[x] = jnp.where(own, v, roll(v, 64, 1))
    for i in range(4):
        x = H1 + 2 * i
        q[i, 0] = (r[2 * i] + r[2 * i + 1])[8:16]
        q[i, 1] = s[x, 8:16] + s[x + 1, 8:16]
        for b in range(2):
            t[i, 4 * b : 4 * b + 4] = q[i, b, pl.ds(0, 4, stride=2), :] + q[i, b, pl.ds(1, 4, stride=2), :]
        place = jnp.where(jnp.logical_and(k < 64, l == 32 * i + k // 2), 0.125, 0.0).astype(F32)
        total = total + exact_dot(t[i], place)
    tile_out[...] = total


def coarse(where_ref, mine_ref, other_ref, out_ref, s2, f2, c2, g2, w2, u2, q2, d2, s3, f3, c3, g3, w3, u3, q3, d3, s4, f4, c4, g4, w4):
    lane = iota((8, LANES), 1)
    row = iota((8, LANES), 0)
    zero2 = jnp.zeros((32, LANES), F32)

    core = lax.rem(where_ref[0], 2)

    def assemble(xc, carry):
        for all_ref, ix in ((mine_ref, 2 * xc + core), (other_ref, 2 * xc + 1 - core)):
            for zt in range(4):
                sides = []
                for iz in (2 * zt, 2 * zt + 1):
                    tiles = [all_ref[(xc * 4 + iy) * 8 + iz] for iy in range(4)]
                    merged = []
                    for xl in range(4):
                        v = roll(tiles[0], -32 * xl, 1)
                        for iy in range(1, 4):
                            v = jnp.where(lane // 32 == iy, roll(tiles[iy], 32 * (iy - xl), 1), v)
                        merged.append(v)
                    sides.append(merged)
                for xl in range(4):
                    even, odd = sides[0][xl], sides[1][xl]
                    f2[ix * 4 + xl, 8 * zt : 8 * zt + 8] = jnp.where(row < 4, even, roll(odd, 4, 0))
                    s2[ix * 4 + xl + 1, 8 * zt : 8 * zt + 8] = jnp.where(row < 4, roll(even, 4, 0), odd)
        return carry

    lax.fori_loop(0, 4, assemble, 0)
    s2[0] = zero2
    s2[33] = zero2
    for x in (0, 1, 2, 3, 36, 37, 38, 39):
        u2[x] = zero2
    for x in (0, 17):
        s3[x] = zero2[:16]
        u3[x] = zero2[:16]
    for x in (0, 9):
        s4[x] = zero2[:8]

    def down(s, f, c, g, w, u, uo, n, scale, q, s_next, f_next, step):
        couplings(s, f, c, g, w, 0, n, scale, so=1, edges=True, step=step // 2)
        first_half_sweep(u, g, 0, n, 0, uo, step)
        half_sweep(u, c, g, 0, n, 1, uo, step)
        half_sweep(u, c, g, 0, n, 0, uo, step)
        half_sweep(u, c, g, 0, n, 1, uo, step)
        half = n // 2

        def chunk(x, m):
            r = residual_planes(u, c, g, w, 2 * x, 2 * m, uo)
            for k in range(m):
                q[0, x + k] = r[2 * k] + r[2 * k + 1]
                q[1, x + k] = s[2 * (x + k) + 1] + s[2 * (x + k) + 2]

        stepped(chunk, 0, half, step // 2)
        pairs = q[:, :, pl.ds(0, half, stride=2), :] + q[:, :, pl.ds(1, half, stride=2), :]
        fine = exact_dot(pairs.reshape(2 * half * half, LANES), halving(LANES)).reshape(2, half, half, LANES)
        f_next[...] = fine[0]
        s_next[1 : half + 1] = fine[1]

    def up(c, g, u, uo, n, coarser, d, step):
        half = n // 2
        twice = exact_dot(coarser.reshape(half * half, LANES), doubling(LANES)).reshape(half, half, LANES)
        d[:, pl.ds(0, half, stride=2), :] = twice
        d[:, pl.ds(1, half, stride=2), :] = twice

        def chunk(x, m):
            for k in range(m):
                v = d[x + k]
                for j in range(2):
                    at = 2 * (x + k) + j + uo
                    u[at] = u[at] + v

        stepped(chunk, 0, half, step // 2)
        for _ in range(NU):
            half_sweep(u, c, g, 0, n, 0, uo, step)
            half_sweep(u, c, g, 0, n, 1, uo, step)

    down(s2, f2, c2, g2, w2, u2, 4, 32, 16.0, q2, s3, f3, 8)
    down(s3, f3, c3, g3, w3, u3, 1, 16, 64.0, q3, s4, f4, 16)
    couplings(s4, f4, c4, g4, w4, 0, 8, 256.0, so=1, edges=True, step=8)
    masks = (reds((8, LANES), 0), reds((8, LANES), 1))
    nothing = jnp.zeros((8, LANES), F32)
    u4 = [jnp.where(masks[x % 2], g4[x], 0.0) for x in range(8)]
    for h in range(1, 2 * BOTTOM):
        around = [nothing] + u4 + [nothing]
        u4 = [jnp.where(masks[(x + h) % 2], relaxed(around[x : x + 3], c4, g4, x), u4[x]) for x in range(8)]
    up(c3, g3, u3, 1, 16, jnp.stack(u4), d3, 16)
    up(c2, g2, u2, 4, 32, u3[1:17], d2, 8)
    ix, iy, iz = where_ref[0], where_ref[1], where_ref[2]
    down_z = lax.rem(36 - 4 * iz, 32)
    down_y = lax.rem(LANES - 32 * iy, LANES)
    for x in range(12):
        v = pltpu.roll(u2[ix * 4 + x], down_z, 0)
        out_ref[x] = pltpu.roll(v[:16], down_y, 1)


def ascend(e, el, eh, a, b, al, bl, ah, bh, n, nl, nh, v, vl, vh, va, vb, val, vbl, vah, vbh, m, ml, mh, win, u_out, r_out, s, f, c, g, w, u, t0, d0, sl, fl, cl, gl, wl, ul, t1, d1):
    fill_narrow(fl, n, nl, nh, 0)
    fill_narrow(sl, n, nl, nh, 1)
    fill_narrow(ul, m, ml, mh, 0)
    couplings(sl, fl, cl, gl, wl, 1, X1 - 1, 4.0, step=4)
    k, l = iota((LANES, LANES), 0), iota((LANES, LANES), 1)
    widen = jnp.where(k == jnp.where(l < 96, l // 2, 64 + l // 2), 1.0, 0.0).astype(F32)
    t1[...] = exact_dot(win[...].reshape(192, LANES), widen).reshape(12, 16, LANES)
    d1[:, pl.ds(0, 12, stride=2), :] = t1[:, :12]
    d1[:, pl.ds(1, 12, stride=2), :] = t1[:, :12]
    for x in range(X1):
        ul[x] = jnp.where(sl[x] > 0.0, ul[x] + d1[(x + 1) // 2], 0.0)
    half_sweep(ul, cl, gl, 1, X1 - 1, H1, step=10)
    half_sweep(ul, cl, gl, 2, X1 - 2, H1 + 1, step=10)
    half_sweep(ul, cl, gl, 3, X1 - 3, H1, step=8)
    half_sweep(ul, cl, gl, 4, X1 - 4, H1 + 1, step=14)
    fill_wide(f, (e, a, b), (el, al, bl), (eh, ah, bh), 0)
    fill_wide(s, (e, a, b), (el, al, bl), (eh, ah, bh), 1)
    fill_wide(u, (v, va, vb), (vl, val, vbl), (vh, vah, vbh), 0)
    couplings(s, f, c, g, w, 1, X0 - 1, 1.0, step=2)
    t0[...] = exact_dot(ul[4:18].reshape(14 * Z1, LANES), doubling(2 * LANES)).reshape(14, Z1, 2 * LANES)
    for half in range(2):
        lanes = slice(half * LANES, half * LANES + LANES)
        d0[half, :, pl.ds(0, 16, stride=2), :] = t0[:, 4:20, lanes]
        d0[half, :, pl.ds(1, 16, stride=2), :] = t0[:, 4:20, lanes]
    for x in range(X0):
        for half in range(2):
            lanes = slice(half * LANES, half * LANES + LANES)
            u[x, :, lanes] = jnp.where(s[x, :, lanes] > 0.0, u[x, :, lanes] + d0[half, (x + 1) // 2], 0.0)
    half_sweep(u, c, g, 1, X0 - 1, H0)
    half_sweep(u, c, g, 2, X0 - 2, H0 + 1)
    half_sweep(u, c, g, 3, X0 - 3, H0)
    half_sweep(u, c, g, 4, X0 - 4, H0 + 1)

    def body(i, carry):
        r = residual_planes(u, c, g, w, H0 + 4 * i, 4)
        for j in range(4):
            u_out[4 * i + j] = u[H0 + 4 * i + j, 8:24, :LANES]
            r_out[4 * i + j] = r[j][8:24, :LANES]
        return carry

    lax.fori_loop(0, 4, body, 0)


def axis_of(name):
    return ("xc", "co") if name == "gx" else name


def swap(low, high, name):
    axis = axis_of(name)
    count = lax.axis_size(axis)
    even = lax.axis_index(axis) % 2 == 0
    first = [(i, i ^ 1) for i in range(count)]
    second = [(i, i + 1) for i in range(1, count - 1, 2)]
    second += [(j, i) for i, j in second]
    a = lax.ppermute(jnp.where(even, high, low), axis, first)
    b = lax.ppermute(jnp.where(even, low, high), axis, second)
    return jnp.where(even, b, a), jnp.where(even, a, b)


def join(pieces):
    return jnp.concatenate([p.reshape(-1, 8, LANES) for p in pieces], 0)


def split(joined, like):
    out, at = [], 0
    for p in like:
        n = p.size // (8 * LANES)
        out.append(joined[at : at + n].reshape(p.shape))
        at += n
    return out


def swap_many(lows, highs, axis):
    low, high = swap(join(lows), join(highs), axis)
    return split(low, lows), split(high, highs)


def extend_wide(field, lo, hi, rest=None):
    extra = [] if rest is None else [rest]
    (below, *r1), (above, *r2) = swap_many([lo] + extra, [hi] + extra, "gy")
    if extra:
        lane = lax.broadcasted_iota(jnp.int32, rest.shape, 3)
        extra = [jnp.where(lane < 64, rest, jnp.where(lane < 96, r2[0], r1[0]))]
    first = [field[:, :, :8], below[:, :8], above[:, :8]]
    last = [field[:, :, 8:], below[:, 8:], above[:, 8:]]
    lows, highs = swap_many(first + extra, last + extra, "gz")
    field = jnp.concatenate([lows[0], field, highs[0]], 2)
    below = jnp.concatenate([lows[1], below, highs[1]], 1)
    above = jnp.concatenate([lows[2], above, highs[2]], 1)
    extra = [jnp.concatenate([p, q, r], 2) for p, q, r in zip(lows[3:], extra, highs[3:])]
    first = [field[:, :H0], below, above] + [v[:, :H1] for v in extra]
    last = [field[:, -H0:], below, above] + [v[:, -H1:] for v in extra]
    lows, highs = swap_many(first, last, "gx")
    wide = [field, lows[0], highs[0], below, above, lows[1], lows[2], highs[1], highs[2]]
    return wide, (extra + lows[3:] + highs[3:])


def extend_narrow(field):
    below, above = swap(field, field, "gy")
    lane = lax.broadcasted_iota(jnp.int32, field.shape, 3)
    field = jnp.where(lane < 64, field, jnp.where(lane < 96, above, below))
    low, high = swap(field, field, "gz")
    field = jnp.concatenate([low, field, high], 2)
    low, high = swap(field[:, :H1], field[:, -H1:], "gx")
    return field, low, high


def gather(tile, sizes):
    def spread(x, axes):
        n = 1
        for a in axes:
            n *= sizes[a]
        every = lax.all_to_all(jnp.broadcast_to(x[None], (n,) + x.shape), axes, 0, 0)
        return every.reshape((-1,) + x.shape[1:])

    mine = spread(spread(tile[None], ("gz",)), ("xc", "gy"))
    return mine, lax.ppermute(mine, "co", [(0, 1), (1, 0)])


def level_scratch(planes, rows, lanes):
    p = (planes, rows, lanes)
    return [vmem(*p), vmem(*p), vmem(6, *p), vmem(*p), vmem(*p), vmem(*p)]


def full_scratch(n, uo):
    p = (n, LANES)
    return [vmem(n + 2, *p), vmem(n, *p), vmem(6, n, *p), vmem(n, *p), vmem(n, *p), vmem(n + 2 * uo, *p)]


def shape(*dims):
    return jax.ShapeDtypeStruct(dims, F32)


def on_device(sizes, right_side, sigma):
    lo, hi = call(packing, [shape(2, 16, LANES)] * 2, [])(right_side, sigma)
    wide, _ = extend_wide(jnp.stack([right_side, sigma]), lo, hi)
    u0, ulo, uhi, next1 = call(
        descend0,
        [shape(16, 16, LANES), shape(16, LANES), shape(16, LANES), shape(2, 8, 8, LANES)],
        level_scratch(X0, Z0, 2 * LANES) + [vmem(2, 8, 16, LANES)],
    )(*wide)
    uwide, narrow = extend_wide(u0[None], ulo[None], uhi[None], next1)
    u1, tile = call(
        descend1,
        [shape(8, 8, LANES), shape(8, LANES)],
        level_scratch(X1, Z1, LANES) + [vmem(4, 2, 8, LANES), vmem(4, 8, LANES)],
    )(*narrow)
    unarrow = extend_narrow(u1[None])
    mine, other = gather(tile, sizes)
    place = jnp.stack([lax.axis_index(axis_of("gx")), lax.axis_index("gy"), lax.axis_index("gz")]).astype(jnp.int32)
    window = call(
        coarse,
        shape(12, 16, LANES),
        full_scratch(32, 4)
        + [vmem(2, 16, 32, LANES), vmem(16, 32, LANES)]
        + full_scratch(16, 1)
        + [vmem(2, 8, 16, LANES), vmem(8, 16, LANES)]
        + full_scratch(8, 1)[:-1],
        smem=1,
    )(place, mine, other)
    return call(
        ascend,
        (shape(16, 16, LANES), shape(16, 16, LANES)),
        level_scratch(X0, Z0, 2 * LANES)
        + [vmem(14, Z1, 2 * LANES), vmem(2, 14, Z0, LANES)]
        + level_scratch(X1, Z1, LANES)
        + [vmem(12, 16, LANES), vmem(12, Z1, LANES)],
    )(*wide, *narrow, *uwide, *unarrow, window)


def solution(mesh):
    names, dims = list(mesh.axis_names), list(mesh.devices.shape)
    at = names.index("gx")
    fine = jax.sharding.Mesh(
        mesh.devices.reshape(dims[:at] + [dims[at] // 2, 2] + dims[at + 1 :]),
        names[:at] + ["xc", "co"] + names[at + 1 :],
    )
    placed = P(("xc", "co"), "gz", "gy")
    return jax.shard_map(
        functools.partial(on_device, dict(fine.shape)),
        mesh=fine,
        in_specs=(placed, placed),
        out_specs=(placed, placed),
        check_vma=False,
    )
```

time: 159 us -> 125 us (0.79)
  Pallas kernels: 59.2 us -> 26.6 us
  waiting for transfers between devices: 38.5 us -> 33.3 us
  starting transfers between devices: 55.4 us -> 58.4 us
  local copies, waits for them, and re-layouts: 1.82 us -> 4.47 us
  other arithmetic: 2.26 us -> 0.56 us
    pallas_call x7 -> x5, Pallas kernels: 59.2 us -> 26.6 us  [run(): pl.pallas_call(kernel, out_shape=out_shape, in_specs=specs, out_specs=jax...]
    all_to_all x1 -> x2, waiting for transfers between devices: 19.6 us -> 14 us  [spread(): lax.all_to_all(jnp.broadcast_to(x[None], (n,) + x.shape), axes, 0, 0)]
    ppermute x0 -> x1, starting transfers between devices: none -> 3.09 us  [gather(): return (mine, lax.ppermute(mine, 'co', [(0, 1), (1, 0)]))]
    unnamed x6 -> x8, local copies, waits for them, and re-layouts: 0.67 us -> 2.74 us
    all_to_all x1 -> x2, starting transfers between devices: 13.4 us -> 13 us  [spread(): lax.all_to_all(jnp.broadcast_to(x[None], (n,) + x.shape), axes, 0, 0)]
  transfers between devices with their start and end apart: 19 -> 21, of which waited for: 9 -> 9; matrix products, arithmetic and copies ran while one was open for 1% -> 1% of each run, Pallas kernels for 0% -> 0%
where the time goes in v1:
time: 125 us
  starting transfers between devices  58.4 us (47%)
  waiting for transfers between devices  33.3 us (27%)
  Pallas kernels  26.6 us (21%)
  local copies, waits for them, and re-layouts  4.47 us (4%)
  between operations  1.27 us (1%)
    ppermute x9, starting transfers between devices, swap(): a = lax.ppermute(jnp.where(even, high, low), axis, first)  27.2 us
    pallas_call x5, Pallas kernels, run(): pl.pallas_call(kernel, out_shape=out_shape, in_specs=specs, out_specs=jax...  26.6 us
    ppermute x9, starting transfers between devices, swap(): b = lax.ppermute(jnp.where(even, low, high), axis, second)  15.1 us
    all_to_all x2, waiting for transfers between devices, spread(): lax.all_to_all(jnp.broadcast_to(x[None], (n,) + x.shape), axes, 0, 0)  14 us
    all_to_all x2, starting transfers between devices, spread(): lax.all_to_all(jnp.broadcast_to(x[None], (n,) + x.shape), axes, 0, 0)  13 us
    ppermute x9, waiting for transfers between devices, swap(): b = lax.ppermute(jnp.where(even, low, high), axis, second)  12.1 us
    ppermute x9, waiting for transfers between devices, swap(): a = lax.ppermute(jnp.where(even, high, low), axis, first)  7.14 us
    ppermute x1, starting transfers between devices, gather(): return (mine, lax.ppermute(mine, 'co', [(0, 1), (1, 0)]))  3.09 us
  transfers between devices with their start and end apart: 21, of which 9 were waited for; matrix products, arithmetic and copies ran while one was open for 1% of the time, Pallas kernels for 0%

profile of v1, /device:TPU:1, one launch (start us, length us, event | category | flops | bytes accessed | tf_op | source)
XLA Modules:
  0.0 124.6 jit_solution(4406388198180180841)
XLA Ops:
  0.6 0.0 copy-start
  0.7 0.9 copy-done
  1.6 0.0 copy-start.2
  1.6 0.9 copy-done.2
  2.5 0.2 shard_map.41
  2.7 2.1 %collective-permute-start.1 = (f32[4,8,128]{2,1,0:T(8,128)S(1)}, f32[4,8,128]{2,1,0:T(8,128)S(1)}, u32[]{:S(2)}, u32[]{:S(2)}) collective-permute-start(f32[4,8,128]{2,1,0:T(8,128)S(1)} %bitcast.122), channel_id=1, source_target_pairs={{0,8},{8,0},{16,24},{24,16},{1,9},{9,1},{17,25},{25,17},{2,10},{10... | collective-permute-start | bytes 49160 | tf_op jit(solution)/shard_map/ppermute | solution.py:391
  4.8 0.7 collective-permute-start
  5.5 0.4 collective-permute-done.1
  5.9 0.0 collective-permute-done
  6.0 0.7 collective-permute-start.2
  6.7 4.8 %collective-permute-start.3 = (f32[36,8,128]{2,1,0:T(8,128)S(1)}, f32[36,8,128]{2,1,0:T(8,128)S(1)}, u32[]{:S(2)}, u32[]{:S(2)}) collective-permute-start(f32[36,8,128]{2,1,0:T(8,128)S(1)} %get-tuple-element.31), channel_id=1, source_target_pairs={{0,1},{1,0},{2,3},{3,2},{4,5},{5,4},{6,7},{7,6},{8,9},{9,8},{10,11... | collective-permute-start | bytes 442376 | tf_op jit(solution)/shard_map/ppermute | solution.py:391
  11.5 0.0 collective-permute-done.2
  11.5 2.5 %collective-permute-done.3 = f32[36,8,128]{2,1,0:T(8,128)S(1)} collective-permute-done((f32[36,8,128]{2,1,0:T(8,128)S(1)}, f32[36,8,128]{2,1,0:T(8,128)S(1)}, u32[]{:S(2)}, u32[]{:S(2)}) %collective-permute-start.3) | collective-permute-done | bytes 147488 | tf_op jit(solution)/shard_map/ppermute | solution.py:391
  14.1 0.0 copy-start.1
  14.1 0.0 copy-start.3
  14.1 0.9 copy-done.1
  15.0 0.1 copy-done.3
  15.2 3.1 %collective-permute-start.5 = (f32[56,8,128]{2,1,0:T(8,128)S(1)}, f32[56,8,128]{2,1,0:T(8,128)S(1)}, u32[]{:S(2)}, u32[]{:S(2)}) collective-permute-start(f32[56,8,128]{2,1,0:T(8,128)S(1)} %get-tuple-element.26), channel_id=1, source_target_pairs={{0,32},{32,0},{64,96},{96,64},{128,160},{160,128},{192,224},{224,1... | collective-permute-start | bytes 688136 | tf_op jit(solution)/shard_map/ppermute | solution.py:391
  18.3 3.1 %collective-permute-start.4 = (f32[56,8,128]{2,1,0:T(8,128)S(1)}, f32[56,8,128]{2,1,0:T(8,128)S(1)}, u32[]{:S(2)}, u32[]{:S(2)}) collective-permute-start(f32[56,8,128]{2,1,0:T(8,128)S(1)} %get-tuple-element.27), channel_id=1, source_target_pairs={{32,64},{96,128},{160,192},{64,32},{128,96},{192,160},{33,65},{97,... | collective-permute-start | bytes 688136 | tf_op jit(solution)/shard_map/ppermute | solution.py:392
  21.4 0.0 collective-permute-done.5
  21.4 4.2 %collective-permute-done.4 = f32[56,8,128]{2,1,0:T(8,128)S(1)} collective-permute-done((f32[56,8,128]{2,1,0:T(8,128)S(1)}, f32[56,8,128]{2,1,0:T(8,128)S(1)}, u32[]{:S(2)}, u32[]{:S(2)}) %collective-permute-start.4) | collective-permute-done | bytes 229408 | tf_op jit(solution)/shard_map/ppermute | solution.py:392
  25.7 5.2 %shard_map.42 = (f32[16,16,128]{2,1,0:T(8,128)S(1)}, f32[16,128]{1,0:T(8,128)S(1)}, f32[16,128]{1,0:T(8,128)S(1)}, f32[2,8,8,128]{3,2,1,0:T(8,128)S(1)}) custom-call(f32[2,16,32,128]{3,2,1,0:T(8,128)S(1)} %pad_maximum_fusion.e, f32[2,5,32,128]{3,2,1,0:T(8,128)S(1)} %bitcast.76, f32[2,5,32,128]{3,2,1,0:T(8,128)S(1)} %bitcast.74, ...), custom_call_target="tpu_custom_call" | custom-call | tf_op jit(solution)/shard_map/pallas_call | solution.py:168
  31.0 0.7 collective-permute-start.6
  31.7 6.8 %collective-permute-start.7 = (f32[18,8,128]{2,1,0:T(8,128)S(1)}, f32[18,8,128]{2,1,0:T(8,128)S(1)}, u32[]{:S(2)}, u32[]{:S(2)}) collective-permute-start(f32[18,8,128]{2,1,0:T(8,128)S(1)} %get-tuple-element.71), channel_id=1, source_target_pairs={{0,8},{8,0},{16,24},{24,16},{1,9},{9,1},{17,25},{25,17},{2,10},{10... | collective-permute-start | bytes 221192 | tf_op jit(solution)/shard_map/ppermute | solution.py:391
  38.5 0.0 collective-permute-done.6
  38.5 1.7 %collective-permute-done.7 = f32[18,8,128]{2,1,0:T(8,128)S(1)} collective-permute-done((f32[18,8,128]{2,1,0:T(8,128)S(1)}, f32[18,8,128]{2,1,0:T(8,128)S(1)}, u32[]{:S(2)}, u32[]{:S(2)}) %collective-permute-start.7) | collective-permute-done | bytes 73760 | tf_op jit(solution)/shard_map/ppermute | solution.py:391
  40.4 0.7 collective-permute-start.8
  41.0 5.8 %collective-permute-start.9 = (f32[34,8,128]{2,1,0:T(8,128)S(1)}, f32[34,8,128]{2,1,0:T(8,128)S(1)}, u32[]{:S(2)}, u32[]{:S(2)}) collective-permute-start(f32[34,8,128]{2,1,0:T(8,128)S(1)} %get-tuple-element.47), channel_id=1, source_target_pairs={{0,1},{1,0},{2,3},{3,2},{4,5},{5,4},{6,7},{7,6},{8,9},{9,8},{10,11... | collective-permute-start | bytes 417800 | tf_op jit(solution)/shard_map/ppermute | solution.py:391
  46.8 0.0 collective-permute-done.8
  46.9 2.4 %collective-permute-done.9 = f32[34,8,128]{2,1,0:T(8,128)S(1)} collective-permute-done((f32[34,8,128]{2,1,0:T(8,128)S(1)}, f32[34,8,128]{2,1,0:T(8,128)S(1)}, u32[]{:S(2)}, u32[]{:S(2)}) %collective-permute-start.9) | collective-permute-done | bytes 139296 | tf_op jit(solution)/shard_map/ppermute | solution.py:391
  49.6 0.1 collective-permute-start.11
  49.7 5.9 %collective-permute-start.10 = (f32[70,8,128]{2,1,0:T(8,128)S(1)}, f32[70,8,128]{2,1,0:T(8,128)S(1)}, u32[]{:S(2)}, u32[]{:S(2)}) collective-permute-start(f32[70,8,128]{2,1,0:T(8,128)S(1)} %get-tuple-element.21), channel_id=1, source_target_pairs={{32,64},{96,128},{160,192},{64,32},{128,96},{192,160},{33,65},{97,... | collective-permute-start | bytes 860168 | tf_op jit(solution)/shard_map/ppermute | solution.py:392
  55.6 0.0 collective-permute-done.11
  55.6 4.3 %collective-permute-done.10 = f32[70,8,128]{2,1,0:T(8,128)S(1)} collective-permute-done((f32[70,8,128]{2,1,0:T(8,128)S(1)}, f32[70,8,128]{2,1,0:T(8,128)S(1)}, u32[]{:S(2)}, u32[]{:S(2)}) %collective-permute-start.10) | collective-permute-done | bytes 286752 | tf_op jit(solution)/shard_map/ppermute | solution.py:392
  60.0 1.1 shard_map.43
  61.1 0.7 collective-permute-start.13
  61.8 2.8 %collective-permute-start.12 = (f32[1,8,8,128]{3,2,1,0:T(8,128)S(1)}, f32[1,8,8,128]{3,2,1,0:T(8,128)S(1)}, u32[]{:S(2)}, u32[]{:S(2)}) collective-permute-start(f32[1,8,8,128]{3,2,1,0:T(8,128)S(1)} %bitcast.98), channel_id=1, source_target_pairs={{0,8},{8,0},{16,24},{24,16},{1,9},{9,1},{17,25},{25,17},{2,10},{10... | collective-permute-start | bytes 98312 | tf_op jit(solution)/shard_map/ppermute | solution.py:391
  64.6 0.1 pad_add_fusion.where_ref
  64.7 0.6 broadcast_in_dim.20
  65.3 6.4 %all-to-all-start = ((f32[8,1,8,128]{3,2,1,0:T(8,128)}), f32[8,1,8,128]{3,2,1,0:T(8,128)S(1)}, u32[]{:S(2)}, u32[]{:S(2)}) async-start(f32[8,1,8,128]{3,2,1,0:T(8,128)} %broadcast_in_dim.20), calls=%async_computation | async-start | bytes 65536 | tf_op jit(solution)/shard_map/all_to_all | solution.py:449
  71.6 0.0 collective-permute-done.13
  71.6 0.0 collective-permute-done.12
  71.7 1.5 %collective-permute-start.15 = (f32[1,8,8,128]{3,2,1,0:T(8,128)S(1)}, f32[1,8,8,128]{3,2,1,0:T(8,128)S(1)}, u32[]{:S(2)}, u32[]{:S(2)}) collective-permute-start(f32[1,8,8,128]{3,2,1,0:T(8,128)S(1)} %select_select_fusion.1), channel_id=1, source_target_pairs={{0,1},{1,0},{2,3},{3,2},{4,5},{5,4},{6,7},{7,6},{8,9},{9,8},{10,11... | collective-permute-start | bytes 98312 | tf_op jit(solution)/shard_map/ppermute | solution.py:391
  73.2 0.7 collective-permute-start.14
  73.9 4.6 %all-to-all-done = f32[8,1,8,128]{3,2,1,0:T(8,128)S(1)} async-done(((f32[8,1,8,128]{3,2,1,0:T(8,128)}), f32[8,1,8,128]{3,2,1,0:T(8,128)S(1)}, u32[]{:S(2)}, u32[]{:S(2)}) %all-to-all-start) | async-done | bytes 32800 | tf_op jit(solution)/shard_map/all_to_all | solution.py:449
  78.5 0.9 broadcast_in_dim.22
  79.4 6.6 %all-to-all-start.1 = ((f32[16,8,8,128]{3,2,1,0:T(8,128)}), f32[16,8,8,128]{3,2,1,0:T(8,128)S(1)}, u32[]{:S(2)}, u32[]{:S(2)}) async-start(f32[16,8,8,128]{3,2,1,0:T(8,128)} %broadcast_in_dim.22), calls=%async_computation.1 | async-start | bytes 1048576 | tf_op jit(solution)/shard_map/all_to_all | solution.py:449
  86.0 0.0 collective-permute-done.15
  86.0 0.0 collective-permute-done.14
  86.0 9.4 %all-to-all-done.1 = f32[16,8,8,128]{3,2,1,0:T(8,128)S(1)} async-done(((f32[16,8,8,128]{3,2,1,0:T(8,128)}), f32[16,8,8,128]{3,2,1,0:T(8,128)S(1)}, u32[]{:S(2)}, u32[]{:S(2)}) %all-to-all-start.1) | async-done | bytes 524320 | tf_op jit(solution)/shard_map/all_to_all | solution.py:449
  95.4 3.1 %collective-permute-start.18 = (f32[128,8,128]{2,1,0:T(8,128)S(1)}, f32[128,8,128]{2,1,0:T(8,128)S(1)}, u32[]{:S(2)}, u32[]{:S(2)}) collective-permute-start(f32[128,8,128]{2,1,0:T(8,128)S(1)} %bitcast.68), channel_id=1, source_target_pairs={{0,32},{32,0},{1,33},{33,1},{2,34},{34,2},{3,35},{35,3},{4,36},{36... | collective-permute-start | bytes 1572872 | tf_op jit(solution)/shard_map/ppermute | solution.py:453
  98.5 0.1 collective-permute-start.17
  98.6 2.1 %collective-permute-start.16 = (f32[1,7,24,128]{3,2,1,0:T(8,128)S(1)}, f32[1,7,24,128]{3,2,1,0:T(8,128)S(1)}, u32[]{:S(2)}, u32[]{:S(2)}) collective-permute-start(f32[1,7,24,128]{3,2,1,0:T(8,128)S(1)} %get-tuple-element.69), channel_id=1, source_target_pairs={{32,64},{96,128},{160,192},{64,32},{128,96},{192,160},{33,65},{97,... | collective-permute-start | bytes 258056 | tf_op jit(solution)/shard_map/ppermute | solution.py:392
  100.8 0.0 collective-permute-done.17
  100.8 3.6 %collective-permute-done.16 = f32[1,7,24,128]{3,2,1,0:T(8,128)S(1)} collective-permute-done((f32[1,7,24,128]{3,2,1,0:T(8,128)S(1)}, f32[1,7,24,128]{3,2,1,0:T(8,128)S(1)}, u32[]{:S(2)}, u32[]{:S(2)}) %collective-permute-start.16) | collective-permute-done | bytes 86048 | tf_op jit(solution)/shard_map/ppermute | solution.py:392
  104.5 0.0 collective-permute-done.18.other_ref
  104.5 10.9 %shard_map.44.win = f32[12,16,128]{2,1,0:T(8,128)S(1)} custom-call(s32[3]{0:T(128)S(1)} %pad_add_fusion.where_ref, f32[128,8,128]{2,1,0:T(8,128)S(1)} %bitcast.69, f32[128,8,128]{2,1,0:T(8,128)S(1)} %collective-permute-done.18.other_ref), custom_call_target="tpu_custom_call" | custom-call | tf_op jit(solution)/shard_map/pallas_call | solution.py:168
  115.4 9.2 %shard_map.45 = (f32[16,16,128]{2,1,0:T(8,128)}, f32[16,16,128]{2,1,0:T(8,128)}) custom-call(f32[2,16,32,128]{3,2,1,0:T(8,128)S(1)} %pad_maximum_fusion.e, f32[2,5,32,128]{3,2,1,0:T(8,128)S(1)} %bitcast.77, f32[2,5,32,128]{3,2,1,0:T(8,128)S(1)} %bitcast.75, f32[2,32,128]{2,1,0:T(8,128)S(1)} %pad_maximum_fusion.19.a, f32[2,32,128]{2,1,0:T(8,128)S(1)} %pad_maximum_fusion.20.b, ...), custom_call_target="tpu_custom_call" | custom-call | tf_op jit(solution)/shard_map/pallas_call | solution.py:168
  (56 shorter events, 0.7 us)
Async XLA Ops:
  0.6 0.9 copy-start
  1.6 0.9 copy-start.2
  2.7 3.3 %collective-permute-start.1 = (f32[4,8,128]{2,1,0:T(8,128)S(1)}, f32[4,8,128]{2,1,0:T(8,128)S(1)}, u32[]{:S(2)}, u32[]{:S(2)}) collective-permute-start(f32[4,8,128]{2,1,0:T(8,128)S(1)} %bitcast.122), channel_id=1, source_target_pairs={{0,8},{8,0},{16,24},{24,16},{1,9},{9,1},{17,25},{25,17},{2,10},{10... | collective-permute-start | bytes 49160 | tf_op jit(solution)/shard_map/ppermute | solution.py:391
  4.8 1.1 collective-permute-start
  6.0 5.5 %collective-permute-start.2 = (f32[36,8,128]{2,1,0:T(8,128)S(1)}, f32[36,8,128]{2,1,0:T(8,128)S(1)}, u32[]{:S(2)}, u32[]{:S(2)}) collective-permute-start(f32[36,8,128]{2,1,0:T(8,128)S(1)} %get-tuple-element.30), channel_id=1, source_target_pairs={{1,2},{3,4},{5,6},{2,1},{4,3},{6,5},{9,10},{11,12},{13,14},{10,9},... | collective-permute-start | bytes 442376 | tf_op jit(solution)/shard_map/ppermute | solution.py:392
  6.7 7.4 %collective-permute-start.3 = (f32[36,8,128]{2,1,0:T(8,128)S(1)}, f32[36,8,128]{2,1,0:T(8,128)S(1)}, u32[]{:S(2)}, u32[]{:S(2)}) collective-permute-start(f32[36,8,128]{2,1,0:T(8,128)S(1)} %get-tuple-element.31), channel_id=1, source_target_pairs={{0,1},{1,0},{2,3},{3,2},{4,5},{5,4},{6,7},{7,6},{8,9},{9,8},{10,11... | collective-permute-start | bytes 442376 | tf_op jit(solution)/shard_map/ppermute | solution.py:391
  14.1 0.9 copy-start.1
  14.1 1.0 copy-start.3
  15.2 6.2 %collective-permute-start.5 = (f32[56,8,128]{2,1,0:T(8,128)S(1)}, f32[56,8,128]{2,1,0:T(8,128)S(1)}, u32[]{:S(2)}, u32[]{:S(2)}) collective-permute-start(f32[56,8,128]{2,1,0:T(8,128)S(1)} %get-tuple-element.26), channel_id=1, source_target_pairs={{0,32},{32,0},{64,96},{96,64},{128,160},{160,128},{192,224},{224,1... | collective-permute-start | bytes 688136 | tf_op jit(solution)/shard_map/ppermute | solution.py:391
  18.3 7.3 %collective-permute-start.4 = (f32[56,8,128]{2,1,0:T(8,128)S(1)}, f32[56,8,128]{2,1,0:T(8,128)S(1)}, u32[]{:S(2)}, u32[]{:S(2)}) collective-permute-start(f32[56,8,128]{2,1,0:T(8,128)S(1)} %get-tuple-element.27), channel_id=1, source_target_pairs={{32,64},{96,128},{160,192},{64,32},{128,96},{192,160},{33,65},{97,... | collective-permute-start | bytes 688136 | tf_op jit(solution)/shard_map/ppermute | solution.py:392
  31.0 7.5 %collective-permute-start.6 = (f32[18,8,128]{2,1,0:T(8,128)S(1)}, f32[18,8,128]{2,1,0:T(8,128)S(1)}, u32[]{:S(2)}, u32[]{:S(2)}) collective-permute-start(f32[18,8,128]{2,1,0:T(8,128)S(1)} %get-tuple-element.70), channel_id=1, source_target_pairs={{8,16},{16,8},{9,17},{17,9},{10,18},{18,10},{11,19},{19,11},{12,20... | collective-permute-start | bytes 221192 | tf_op jit(solution)/shard_map/ppermute | solution.py:392
  31.7 8.6 %collective-permute-start.7 = (f32[18,8,128]{2,1,0:T(8,128)S(1)}, f32[18,8,128]{2,1,0:T(8,128)S(1)}, u32[]{:S(2)}, u32[]{:S(2)}) collective-permute-start(f32[18,8,128]{2,1,0:T(8,128)S(1)} %get-tuple-element.71), channel_id=1, source_target_pairs={{0,8},{8,0},{16,24},{24,16},{1,9},{9,1},{17,25},{25,17},{2,10},{10... | collective-permute-start | bytes 221192 | tf_op jit(solution)/shard_map/ppermute | solution.py:391
  40.4 6.5 %collective-permute-start.8 = (f32[34,8,128]{2,1,0:T(8,128)S(1)}, f32[34,8,128]{2,1,0:T(8,128)S(1)}, u32[]{:S(2)}, u32[]{:S(2)}) collective-permute-start(f32[34,8,128]{2,1,0:T(8,128)S(1)} %get-tuple-element.46), channel_id=1, source_target_pairs={{1,2},{3,4},{5,6},{2,1},{4,3},{6,5},{9,10},{11,12},{13,14},{10,9},... | collective-permute-start | bytes 417800 | tf_op jit(solution)/shard_map/ppermute | solution.py:392
  41.0 8.3 %collective-permute-start.9 = (f32[34,8,128]{2,1,0:T(8,128)S(1)}, f32[34,8,128]{2,1,0:T(8,128)S(1)}, u32[]{:S(2)}, u32[]{:S(2)}) collective-permute-start(f32[34,8,128]{2,1,0:T(8,128)S(1)} %get-tuple-element.47), channel_id=1, source_target_pairs={{0,1},{1,0},{2,3},{3,2},{4,5},{5,4},{6,7},{7,6},{8,9},{9,8},{10,11... | collective-permute-start | bytes 417800 | tf_op jit(solution)/shard_map/ppermute | solution.py:391
  49.6 6.1 %collective-permute-start.11 = (f32[70,8,128]{2,1,0:T(8,128)S(1)}, f32[70,8,128]{2,1,0:T(8,128)S(1)}, u32[]{:S(2)}, u32[]{:S(2)}) collective-permute-start(f32[70,8,128]{2,1,0:T(8,128)S(1)} %get-tuple-element.20), channel_id=1, source_target_pairs={{0,32},{32,0},{64,96},{96,64},{128,160},{160,128},{192,224},{224,1... | collective-permute-start | bytes 860168 | tf_op jit(solution)/shard_map/ppermute | solution.py:391
  49.7 10.3 %collective-permute-start.10 = (f32[70,8,128]{2,1,0:T(8,128)S(1)}, f32[70,8,128]{2,1,0:T(8,128)S(1)}, u32[]{:S(2)}, u32[]{:S(2)}) collective-permute-start(f32[70,8,128]{2,1,0:T(8,128)S(1)} %get-tuple-element.21), channel_id=1, source_target_pairs={{32,64},{96,128},{160,192},{64,32},{128,96},{192,160},{33,65},{97,... | collective-permute-start | bytes 860168 | tf_op jit(solution)/shard_map/ppermute | solution.py:392
  61.1 10.5 %collective-permute-start.13 = (f32[1,8,8,128]{3,2,1,0:T(8,128)S(1)}, f32[1,8,8,128]{3,2,1,0:T(8,128)S(1)}, u32[]{:S(2)}, u32[]{:S(2)}) collective-permute-start(f32[1,8,8,128]{3,2,1,0:T(8,128)S(1)} %bitcast.97), channel_id=1, source_target_pairs={{8,16},{16,8},{9,17},{17,9},{10,18},{18,10},{11,19},{19,11},{12,20... | collective-permute-start | bytes 98312 | tf_op jit(solution)/shard_map/ppermute | solution.py:392
  61.8 9.9 %collective-permute-start.12 = (f32[1,8,8,128]{3,2,1,0:T(8,128)S(1)}, f32[1,8,8,128]{3,2,1,0:T(8,128)S(1)}, u32[]{:S(2)}, u32[]{:S(2)}) collective-permute-start(f32[1,8,8,128]{3,2,1,0:T(8,128)S(1)} %bitcast.98), channel_id=1, source_target_pairs={{0,8},{8,0},{16,24},{24,16},{1,9},{9,1},{17,25},{25,17},{2,10},{10... | collective-permute-start | bytes 98312 | tf_op jit(solution)/shard_map/ppermute | solution.py:391
  65.3 13.2 %all-to-all-start = ((f32[8,1,8,128]{3,2,1,0:T(8,128)}), f32[8,1,8,128]{3,2,1,0:T(8,128)S(1)}, u32[]{:S(2)}, u32[]{:S(2)}) async-start(f32[8,1,8,128]{3,2,1,0:T(8,128)} %broadcast_in_dim.20), calls=%async_computation | async-start | bytes 65536 | tf_op jit(solution)/shard_map/all_to_all | solution.py:449
  71.7 14.3 %collective-permute-start.15 = (f32[1,8,8,128]{3,2,1,0:T(8,128)S(1)}, f32[1,8,8,128]{3,2,1,0:T(8,128)S(1)}, u32[]{:S(2)}, u32[]{:S(2)}) collective-permute-start(f32[1,8,8,128]{3,2,1,0:T(8,128)S(1)} %select_select_fusion.1), channel_id=1, source_target_pairs={{0,1},{1,0},{2,3},{3,2},{4,5},{5,4},{6,7},{7,6},{8,9},{9,8},{10,11... | collective-permute-start | bytes 98312 | tf_op jit(solution)/shard_map/ppermute | solution.py:391
  73.2 12.8 %collective-permute-start.14 = (f32[1,8,8,128]{3,2,1,0:T(8,128)S(1)}, f32[1,8,8,128]{3,2,1,0:T(8,128)S(1)}, u32[]{:S(2)}, u32[]{:S(2)}) collective-permute-start(f32[1,8,8,128]{3,2,1,0:T(8,128)S(1)} %select_select_fusion.1), channel_id=1, source_target_pairs={{1,2},{3,4},{5,6},{2,1},{4,3},{6,5},{9,10},{11,12},{13,14},{10,9},... | collective-permute-start | bytes 98312 | tf_op jit(solution)/shard_map/ppermute | solution.py:392
  79.4 16.1 %all-to-all-start.1 = ((f32[16,8,8,128]{3,2,1,0:T(8,128)}), f32[16,8,8,128]{3,2,1,0:T(8,128)S(1)}, u32[]{:S(2)}, u32[]{:S(2)}) async-start(f32[16,8,8,128]{3,2,1,0:T(8,128)} %broadcast_in_dim.22), calls=%async_computation.1 | async-start | bytes 1048576 | tf_op jit(solution)/shard_map/all_to_all | solution.py:449
  95.4 9.0 %collective-permute-start.18 = (f32[128,8,128]{2,1,0:T(8,128)S(1)}, f32[128,8,128]{2,1,0:T(8,128)S(1)}, u32[]{:S(2)}, u32[]{:S(2)}) collective-permute-start(f32[128,8,128]{2,1,0:T(8,128)S(1)} %bitcast.68), channel_id=1, source_target_pairs={{0,32},{32,0},{1,33},{33,1},{2,34},{34,2},{3,35},{35,3},{4,36},{36... | collective-permute-start | bytes 1572872 | tf_op jit(solution)/shard_map/ppermute | solution.py:453
  98.5 2.3 %collective-permute-start.17 = (f32[1,7,24,128]{3,2,1,0:T(8,128)S(1)}, f32[1,7,24,128]{3,2,1,0:T(8,128)S(1)}, u32[]{:S(2)}, u32[]{:S(2)}) collective-permute-start(f32[1,7,24,128]{3,2,1,0:T(8,128)S(1)} %get-tuple-element.68), channel_id=1, source_target_pairs={{0,32},{32,0},{64,96},{96,64},{128,160},{160,128},{192,224},{224,1... | collective-permute-start | bytes 258056 | tf_op jit(solution)/shard_map/ppermute | solution.py:391
  98.6 5.8 %collective-permute-start.16 = (f32[1,7,24,128]{3,2,1,0:T(8,128)S(1)}, f32[1,7,24,128]{3,2,1,0:T(8,128)S(1)}, u32[]{:S(2)}, u32[]{:S(2)}) collective-permute-start(f32[1,7,24,128]{3,2,1,0:T(8,128)S(1)} %get-tuple-element.69), channel_id=1, source_target_pairs={{32,64},{96,128},{160,192},{64,32},{128,96},{192,160},{33,65},{97,... | collective-permute-start | bytes 258056 | tf_op jit(solution)/shard_map/ppermute | solution.py:392

commit v2 on v1

--- a/solution.py
+++ b/solution.py
@@ -12,9 +12,11 @@
 F32 = jnp.float32
 LANES = 128
 STRIP = 8
-PER = LANES // STRIP
-
+
+HD, XD, ZD = 14, 44, 48
+NEAR = 5
 H0, X0, Z0 = 5, 26, 32
+HALF = LANES // 2
 H1, X1, Z1 = 7, 22, 24
 
 
@@ -130,29 +132,120 @@
     return [w_ref[x + k] * (relaxed(u[k : k + 3], c_ref, g_ref, x + k) - u[k + 1]) for k in range(n)]
 
 
-def packed(planes):
+def phases(shape, parity):
+    return (iota(shape, 0) + parity) % 2 == 0
+
+
+def beside(v, below):
+    return jnp.where(below, roll(v, 1, 1), roll(v, -1, 1))
+
+
+def couplings_rb(s, f, c, g, w, first, last, scale, parity, step):
+    shape = s.shape[2:]
+    masks = (phases(shape, parity), phases(shape, parity + 1))
+
+    def chunk(x, n):
+        for col in range(2):
+            for k in range(n):
+                centre, v = s[col, x + k], s[1 - col, x + k]
+                near = [
+                    s[1 - col, x + k + 1],
+                    s[1 - col, x + k - 1],
+                    roll(v, -1, 0),
+                    roll(v, 1, 0),
+                    v,
+                    beside(v, masks[(first + k + col) % 2]),
+                ]
+                betas = [0.5 * (centre + v) for v in near]
+                total = ((betas[0] + betas[1]) + (betas[2] + betas[3])) + (betas[4] + betas[5])
+                inverse = jnp.where(centre > 0.0, 1.0 / total, 0.0)
+                for d in range(6):
+                    c[col, d, x + k] = betas[d] * inverse
+                g[col, x + k] = f[col, x + k] * (inverse * scale)
+                w[col, x + k] = total * (1.0 / scale)
+
+    stepped(chunk, first, last, step)
+
+
+def relaxed_rb(v, c, g, col, x, mask):
+    low, centre, high = v
+    a = c[col, 0, x] * high + c[col, 1, x] * low
+    b = c[col, 2, x] * roll(centre, -1, 0) + c[col, 3, x] * roll(centre, 1, 0)
+    d = c[col, 4, x] * centre + c[col, 5, x] * beside(centre, mask)
+    return g[col, x] + ((a + b) + d)
+
+
+def half_sweep_rb(u_ref, v_ref, c, g, col, first, last, parity, step):
+    shape = v_ref.shape[1:]
+    masks = (phases(shape, parity), phases(shape, parity + 1))
+
+    def chunk(x, n):
+        v = [v_ref[x + k] for k in range(-1, n + 1)]
+        for k in range(n):
+            u_ref[x + k] = relaxed_rb(v[k : k + 3], c, g, col, x + k, masks[(first + k + col) % 2])
+
+    stepped(chunk, first, last, step)
+
+
+def residuals_rb(u, c, g, w, first, x, n, parity):
+    shape = u.shape[2:]
+    masks = (phases(shape, parity), phases(shape, parity + 1))
+    out = []
+    for col in range(2):
+        v = [u[1 - col, x + k] for k in range(-1, n + 1)]
+        out.append(
+            [
+                w[col, x + k] * (relaxed_rb(v[k : k + 3], c, g, col, x + k, masks[(first + k + col) % 2]) - u[col, x + k])
+                for k in range(n)
+            ]
+        )
+    return out
+
+
+def permuted(v, back):
+    k, l = iota((LANES, LANES), 0), iota((LANES, LANES), 1)
+    if back:
+        k, l = l, k
+    move = jnp.where(k == jnp.where(l < HALF, 2 * l, 2 * (l - HALF) + 1), 1.0, 0.0).astype(jnp.bfloat16)
+    first = v.astype(jnp.bfloat16)
+    rest = v - first.astype(F32)
+    second = rest.astype(jnp.bfloat16)
+    third = (rest - second.astype(F32)).astype(jnp.bfloat16)
+    parts = [jnp.dot(x, move, preferred_element_type=F32) for x in (first, second, third)]
+    return (parts[0] + parts[1]) + parts[2]
+
+
+def swapped_rows(v, parity):
+    return jnp.where(phases(v.shape, parity), v, roll(v, HALF, 1))
+
+
+def packed(planes, at):
     rows = planes[0].shape[0]
     group = iota((rows, LANES), 1) // STRIP
-    lo = hi = jnp.zeros((rows, LANES), F32)
+    out = jnp.zeros((rows, LANES), F32)
     for k, v in enumerate(planes):
-        lo = jnp.where(group == k, roll(v, STRIP * k, 1), lo)
-        hi = jnp.where(group == k, roll(v, STRIP * (k + 1), 1), hi)
-    return lo, hi
-
-
-def unpacked(low, high, k):
-    lane = iota(low.shape, 1)
-    high = roll(high, -STRIP * k, 1)
+        out = jnp.where(group == k, roll(v, STRIP * k - at, 1), out)
+    return out
+
+
+def with_halo(v, low, high, k):
+    lane = iota(v.shape, 1)
+    high = roll(high, HALF - STRIP * k, 1)
     low = roll(low, LANES - STRIP - STRIP * k, 1)
-    return jnp.where(lane < STRIP, high, jnp.where(lane >= LANES - STRIP, low, 0.0))
-
-
-def fill_wide(out_ref, own, low, high, i):
-    for part, at, count, k0 in ((low, 0, H0, 16 - H0), (own, H0, 16, 0), (high, H0 + 16, H0, 0)):
-        planes_ref, below_ref, above_ref = part
-        for k in range(count):
-            out_ref[at + k, :, :LANES] = planes_ref[i, k]
-            out_ref[at + k, :, LANES:] = unpacked(below_ref[i], above_ref[i], k0 + k)
+    halo = jnp.where(lane < HALF + STRIP, high, jnp.where(lane >= LANES - STRIP, low, 0.0))
+    return jnp.where(lane < HALF, v, halo)
+
+
+def fill_rb(out, i, at, planes_ref, below, above, k0, count, rows=None):
+    r = slice(0, ZD) if rows is None else rows
+    for n in range(count):
+        v = planes_ref[i, n]
+        for col in range(2):
+            own = v if col == 0 else roll(v, HALF, 1)
+            out[col, at + n, r] = with_halo(own, below[2 * i + col, r], above[2 * i + col, r], k0 + n)
+            if rows is not None:
+                out[col, at + n, : r.start] = jnp.zeros((r.start, LANES), F32)
+                out[col, at + n, r.stop :] = jnp.zeros((ZD - r.stop, LANES), F32)
 
 
 def fill_narrow(out_ref, own, low, high, i):
@@ -181,60 +274,79 @@
     return pltpu.VMEM(shape, F32)
 
 
-def packing(f_ref, s_ref, lo_ref, hi_ref):
+def packing(f_ref, s_ref, out_ref, lo_ref, hi_ref):
     for i, ref in enumerate((f_ref, s_ref)):
-        lo_ref[i], hi_ref[i] = packed([ref[k] for k in range(16)])
-
-
-def descend0(e, el, eh, a, b, al, bl, ah, bh, u_out, ulo_out, uhi_out, next_out, s, f, c, g, w, u, q):
-    fill_wide(f, (e, a, b), (el, al, bl), (eh, ah, bh), 0)
-    fill_wide(s, (e, a, b), (el, al, bl), (eh, ah, bh), 1)
-    couplings(s, f, c, g, w, 1, X0 - 1, 1.0, step=2)
-    first_half_sweep(u, g, 1, X0 - 1, H0)
-    half_sweep(u, c, g, 2, X0 - 2, H0 + 1)
-    half_sweep(u, c, g, 3, X0 - 3, H0)
-    half_sweep(u, c, g, 4, X0 - 4, H0 + 1)
-
-    def body(i, carry):
-        x = H0 + 4 * i
-        r = residual_planes(u, c, g, w, x, 4)
+        out_ref[i] = permuted(ref[...].reshape(256, LANES), False).reshape(16, 16, LANES)
+        planes = [swapped_rows(out_ref[i, x], x) for x in range(16)]
+        for x in range(16):
+            out_ref[i, x] = planes[x]
+        for col in range(2):
+            lo_ref[2 * i + col] = packed(planes, HALF * col)
+            hi_ref[2 * i + col] = packed(planes, HALF * col + HALF - STRIP)
+
+
+def descend(e, b, a, ln, lf, lb, la, hn, hf, hb, ha, top_out, s1_out, next_out, tile_out, s, f, c, g, w, u, q, fl, cl, gl, wl, ul, ql, t):
+    far = slice(8, ZD - 8)
+    for i, out in enumerate((f, s)):
+        fill_rb(out, i, 0, lf, lb, la, 16 - HD, HD - NEAR, far)
+        fill_rb(out, i, HD - NEAR, ln, lb, la, 16 - NEAR, NEAR)
+        fill_rb(out, i, HD, e, b, a, 0, 16)
+        fill_rb(out, i, HD + 16, hn, hb, ha, 0, NEAR)
+        fill_rb(out, i, HD + 16 + NEAR, hf, hb, ha, NEAR, HD - NEAR, far)
+    couplings_rb(s, f, c, g, w, 2, XD - 2, 1.0, 0, 2)
+    red, black = u.at[0], u.at[1]
+    half_sweep_rb(black, g.at[0], c, g, 1, 3, XD - 3, 0, 4)
+    half_sweep_rb(red, black, c, g, 0, 4, XD - 4, 0, 4)
+    half_sweep_rb(black, red, c, g, 1, 5, XD - 5, 0, 4)
+
+    def residual_body(i, carry):
+        r = residuals_rb(u, c, g, w, 6, 6 + 4 * i, 4, 0)
         for k in range(2):
-            q[0, 2 * i + k] = (r[2 * k] + r[2 * k + 1])[8:24, :LANES]
-            q[1, 2 * i + k] = s[x + 2 * k, 8:24, :LANES] + s[x + 2 * k + 1, 8:24, :LANES]
-        for k in range(4):
-            u_out[4 * i + k] = u[x + k, 8:24, :LANES]
+            q[0, 2 * i + k + 3] = (r[0][2 * k] + r[0][2 * k + 1]) + (r[1][2 * k] + r[1][2 * k + 1])
         return carry
 
-    lax.fori_loop(0, 4, body, 0)
-    ulo_out[...], uhi_out[...] = packed([u_out[k] for k in range(16)])
-    pairs = q[:, :, pl.ds(0, 8, stride=2), :] + q[:, :, pl.ds(1, 8, stride=2), :]
-    k, l = iota((LANES, LANES), 0), iota((LANES, LANES), 1)
-    halve_twice = jnp.where(k // 2 == l % 64, 0.125, 0.0).astype(F32)
-    next_out[...] = exact_dot(pairs.reshape(128, LANES), halve_twice).reshape(2, 8, 8, LANES)
-
-
-def descend1(e, el, eh, u_out, tile_out, s, f, c, g, w, u, q, t):
-    fill_narrow(f, e, el, eh, 0)
-    fill_narrow(s, e, el, eh, 1)
-    couplings(s, f, c, g, w, 3, X1 - 3, 4.0, step=4)
-    first_half_sweep(u, g, 3, X1 - 3, H1, step=8)
-    half_sweep(u, c, g, 4, X1 - 4, H1 + 1, step=8)
-    half_sweep(u, c, g, 5, X1 - 5, H1, step=12)
-    half_sweep(u, c, g, 6, X1 - 6, H1 + 1, step=10)
+    lax.fori_loop(0, 8, residual_body, 0)
+    nothing = jnp.zeros((ZD, LANES), F32)
+    for i in (0, 1, 2, 19, 20, 21):
+        q[0, i] = nothing
+
+    def coefficient_body(i, carry):
+        q[1, i] = (s[0, 2 * i] + s[0, 2 * i + 1]) + (s[1, 2 * i] + s[1, 2 * i + 1])
+        return carry
+
+    lax.fori_loop(0, X1, coefficient_body, 0)
+    sl = s1_out
+    for i, ref in enumerate((fl, sl)):
+        ref[...] = 0.125 * (q[i, :, pl.ds(0, Z1, stride=2), :] + q[i, :, pl.ds(1, Z1, stride=2), :])
+
+    def top_body(i, carry):
+        for col in range(2):
+            top_out[col, i] = s[col, HD - H0 + i, 8 : ZD - 8]
+            top_out[2 + col, i] = f[col, HD - H0 + i, 8 : ZD - 8]
+        top_out[4, i] = black[HD - H0 + i, 8 : ZD - 8]
+        return carry
+
+    lax.fori_loop(0, X0, top_body, 0)
+    couplings(sl, fl, cl, gl, wl, 3, X1 - 3, 4.0, step=4)
+    first_half_sweep(ul, gl, 3, X1 - 3, H1, step=8)
+    half_sweep(ul, cl, gl, 4, X1 - 4, H1 + 1, step=14)
+    half_sweep(ul, cl, gl, 5, X1 - 5, H1, step=12)
+    half_sweep(ul, cl, gl, 6, X1 - 6, H1 + 1, step=10)
     k, l = iota((LANES, LANES), 0), iota((LANES, LANES), 1)
     total = jnp.zeros((8, LANES), F32)
-    r = residual_planes(u, c, g, w, H1, 8)
-    own = iota((8, LANES), 1) < 64
+    r = residual_planes(ul, cl, gl, wl, H1, 8)
+    own = iota((8, LANES), 1) < HALF
     for x in range(8):
-        v = u[H1 + x, 8:16]
-        u_out[x] = jnp.where(own, v, roll(v, 64, 1))
+        for i, ref in enumerate((ul, fl)):
+            v = ref[H1 + x, 8:16]
+            next_out[i, x] = jnp.where(own, v, roll(v, HALF, 1))
     for i in range(4):
         x = H1 + 2 * i
-        q[i, 0] = (r[2 * i] + r[2 * i + 1])[8:16]
-        q[i, 1] = s[x, 8:16] + s[x + 1, 8:16]
+        ql[i, 0] = (r[2 * i] + r[2 * i + 1])[8:16]
+        ql[i, 1] = sl[x, 8:16] + sl[x + 1, 8:16]
         for b in range(2):
-            t[i, 4 * b : 4 * b + 4] = q[i, b, pl.ds(0, 4, stride=2), :] + q[i, b, pl.ds(1, 4, stride=2), :]
-        place = jnp.where(jnp.logical_and(k < 64, l == 32 * i + k // 2), 0.125, 0.0).astype(F32)
+            t[i, 4 * b : 4 * b + 4] = ql[i, b, pl.ds(0, 4, stride=2), :] + ql[i, b, pl.ds(1, 4, stride=2), :]
+        place = jnp.where(jnp.logical_and(k < HALF, l == 32 * i + k // 2), 0.125, 0.0).astype(F32)
         total = total + exact_dot(t[i], place)
     tile_out[...] = total
 
@@ -333,48 +445,47 @@
         out_ref[x] = pltpu.roll(v[:16], down_y, 1)
 
 
-def ascend(e, el, eh, a, b, al, bl, ah, bh, n, nl, nh, v, vl, vh, va, vb, val, vbl, vah, vbh, m, ml, mh, win, u_out, r_out, s, f, c, g, w, u, t0, d0, sl, fl, cl, gl, wl, ul, t1, d1):
-    fill_narrow(fl, n, nl, nh, 0)
-    fill_narrow(sl, n, nl, nh, 1)
+def ascend(top, sl, m, ml, mh, win, u_out, r_out, c, g, w, u, d0, fl, cl, gl, wl, ul, t1, d1):
     fill_narrow(ul, m, ml, mh, 0)
+    fill_narrow(fl, m, ml, mh, 1)
     couplings(sl, fl, cl, gl, wl, 1, X1 - 1, 4.0, step=4)
     k, l = iota((LANES, LANES), 0), iota((LANES, LANES), 1)
-    widen = jnp.where(k == jnp.where(l < 96, l // 2, 64 + l // 2), 1.0, 0.0).astype(F32)
+    widen = jnp.where(k == jnp.where(l < 96, l // 2, HALF + l // 2), 1.0, 0.0).astype(F32)
     t1[...] = exact_dot(win[...].reshape(192, LANES), widen).reshape(12, 16, LANES)
     d1[:, pl.ds(0, 12, stride=2), :] = t1[:, :12]
     d1[:, pl.ds(1, 12, stride=2), :] = t1[:, :12]
     for x in range(X1):
         ul[x] = jnp.where(sl[x] > 0.0, ul[x] + d1[(x + 1) // 2], 0.0)
     half_sweep(ul, cl, gl, 1, X1 - 1, H1, step=10)
-    half_sweep(ul, cl, gl, 2, X1 - 2, H1 + 1, step=10)
-    half_sweep(ul, cl, gl, 3, X1 - 3, H1, step=8)
+    half_sweep(ul, cl, gl, 2, X1 - 2, H1 + 1, step=18)
+    half_sweep(ul, cl, gl, 3, X1 - 3, H1, step=16)
     half_sweep(ul, cl, gl, 4, X1 - 4, H1 + 1, step=14)
-    fill_wide(f, (e, a, b), (el, al, bl), (eh, ah, bh), 0)
-    fill_wide(s, (e, a, b), (el, al, bl), (eh, ah, bh), 1)
-    fill_wide(u, (v, va, vb), (vl, val, vbl), (vh, vah, vbh), 0)
-    couplings(s, f, c, g, w, 1, X0 - 1, 1.0, step=2)
-    t0[...] = exact_dot(ul[4:18].reshape(14 * Z1, LANES), doubling(2 * LANES)).reshape(14, Z1, 2 * LANES)
-    for half in range(2):
-        lanes = slice(half * LANES, half * LANES + LANES)
-        d0[half, :, pl.ds(0, 16, stride=2), :] = t0[:, 4:20, lanes]
-        d0[half, :, pl.ds(1, 16, stride=2), :] = t0[:, 4:20, lanes]
+    s, f, black, red = top.at[0:2], top.at[2:4], u.at[1], u.at[0]
+    couplings_rb(s, f, c, g, w, 1, X0 - 1, 1.0, 1, 2)
+    fine = ul[4:18, 4:20]
+    d0[:, pl.ds(0, 16, stride=2), :] = fine
+    d0[:, pl.ds(1, 16, stride=2), :] = fine
     for x in range(X0):
-        for half in range(2):
-            lanes = slice(half * LANES, half * LANES + LANES)
-            u[x, :, lanes] = jnp.where(s[x, :, lanes] > 0.0, u[x, :, lanes] + d0[half, (x + 1) // 2], 0.0)
-    half_sweep(u, c, g, 1, X0 - 1, H0)
-    half_sweep(u, c, g, 2, X0 - 2, H0 + 1)
-    half_sweep(u, c, g, 3, X0 - 3, H0)
-    half_sweep(u, c, g, 4, X0 - 4, H0 + 1)
+        black[x] = jnp.where(top[1, x] > 0.0, top[4, x] + d0[(x + 1) // 2], 0.0)
+    half_sweep_rb(red, black, c, g, 0, 1, X0 - 1, 1, 6)
+    half_sweep_rb(black, red, c, g, 1, 2, X0 - 2, 1, 6)
+    half_sweep_rb(red, black, c, g, 0, 3, X0 - 3, 1, 6)
+    half_sweep_rb(black, red, c, g, 1, 4, X0 - 4, 1, 6)
+
+    lane = iota((16, LANES), 1)
 
     def body(i, carry):
-        r = residual_planes(u, c, g, w, H0 + 4 * i, 4)
+        x = H0 + 4 * i
+        r = residuals_rb(u, c, g, w, H0, x, 4, 1)
         for j in range(4):
-            u_out[4 * i + j] = u[H0 + 4 * i + j, 8:24, :LANES]
-            r_out[4 * i + j] = r[j][8:24, :LANES]
+            for out, a, b in ((u_out, u[0, x + j], u[1, x + j]), (r_out, r[0][j], r[1][j])):
+                both = jnp.where(lane < HALF, a[8:24], roll(b[8:24], HALF, 1))
+                out[4 * i + j] = swapped_rows(both, j)
         return carry
 
     lax.fori_loop(0, 4, body, 0)
+    for out in (u_out, r_out):
+        out[...] = permuted(out[...].reshape(256, LANES), True).reshape(16, 16, LANES)
 
 
 def axis_of(name):
@@ -411,24 +522,16 @@
     return split(low, lows), split(high, highs)
 
 
-def extend_wide(field, lo, hi, rest=None):
-    extra = [] if rest is None else [rest]
-    (below, *r1), (above, *r2) = swap_many([lo] + extra, [hi] + extra, "gy")
-    if extra:
-        lane = lax.broadcasted_iota(jnp.int32, rest.shape, 3)
-        extra = [jnp.where(lane < 64, rest, jnp.where(lane < 96, r2[0], r1[0]))]
-    first = [field[:, :, :8], below[:, :8], above[:, :8]]
-    last = [field[:, :, 8:], below[:, 8:], above[:, 8:]]
-    lows, highs = swap_many(first + extra, last + extra, "gz")
-    field = jnp.concatenate([lows[0], field, highs[0]], 2)
-    below = jnp.concatenate([lows[1], below, highs[1]], 1)
-    above = jnp.concatenate([lows[2], above, highs[2]], 1)
-    extra = [jnp.concatenate([p, q, r], 2) for p, q, r in zip(lows[3:], extra, highs[3:])]
-    first = [field[:, :H0], below, above] + [v[:, :H1] for v in extra]
-    last = [field[:, -H0:], below, above] + [v[:, -H1:] for v in extra]
+def extend_wide(field, lo, hi):
+    below, above = swap(lo, hi, "gy")
+    pieces = [field, below, above]
+    lows, highs = swap_many(pieces, pieces, "gz")
+    field, below, above = [jnp.concatenate(v, v[0].ndim - 2) for v in zip(lows, pieces, highs)]
+    rows = slice(8, ZD - 8)
+    first = [field[:, :NEAR], field[:, NEAR:HD, rows], below, above]
+    last = [field[:, -NEAR:], field[:, -HD:-NEAR, rows], below, above]
     lows, highs = swap_many(first, last, "gx")
-    wide = [field, lows[0], highs[0], below, above, lows[1], lows[2], highs[1], highs[2]]
-    return wide, (extra + lows[3:] + highs[3:])
+    return [field, below, above] + lows + highs
 
 
 def extend_narrow(field):
@@ -453,9 +556,14 @@
     return mine, lax.ppermute(mine, "co", [(0, 1), (1, 0)])
 
 
-def level_scratch(planes, rows, lanes):
-    p = (planes, rows, lanes)
+def level_scratch(planes, rows):
+    p = (planes, rows, LANES)
     return [vmem(*p), vmem(*p), vmem(6, *p), vmem(*p), vmem(*p), vmem(*p)]
+
+
+def rb_scratch(planes, rows, count):
+    p = (planes, rows, LANES)
+    return ([vmem(2, *p)] * 6)[: count - 4] + [vmem(2, 6, *p)] + [vmem(2, *p)] * 3
 
 
 def full_scratch(n, uo):
@@ -468,20 +576,16 @@
 
 
 def on_device(sizes, right_side, sigma):
-    lo, hi = call(packing, [shape(2, 16, LANES)] * 2, [])(right_side, sigma)
-    wide, _ = extend_wide(jnp.stack([right_side, sigma]), lo, hi)
-    u0, ulo, uhi, next1 = call(
-        descend0,
-        [shape(16, 16, LANES), shape(16, LANES), shape(16, LANES), shape(2, 8, 8, LANES)],
-        level_scratch(X0, Z0, 2 * LANES) + [vmem(2, 8, 16, LANES)],
-    )(*wide)
-    uwide, narrow = extend_wide(u0[None], ulo[None], uhi[None], next1)
-    u1, tile = call(
-        descend1,
-        [shape(8, 8, LANES), shape(8, LANES)],
-        level_scratch(X1, Z1, LANES) + [vmem(4, 2, 8, LANES), vmem(4, 8, LANES)],
-    )(*narrow)
-    unarrow = extend_narrow(u1[None])
+    field, lo, hi = call(packing, [shape(2, 16, 16, LANES), shape(4, 16, LANES), shape(4, 16, LANES)], [])(right_side, sigma)
+    top, s1, next1, tile = call(
+        descend,
+        [shape(5, X0, Z0, LANES), shape(X1, Z1, LANES), shape(2, 8, 8, LANES), shape(8, LANES)],
+        rb_scratch(XD, ZD, 6)
+        + [vmem(2, X1, ZD, LANES)]
+        + level_scratch(X1, Z1)[1:]
+        + [vmem(4, 2, 8, LANES), vmem(4, 8, LANES)],
+    )(*extend_wide(field, lo, hi))
+    narrow = extend_narrow(next1)
     mine, other = gather(tile, sizes)
     place = jnp.stack([lax.axis_index(axis_of("gx")), lax.axis_index("gy"), lax.axis_index("gz")]).astype(jnp.int32)
     window = call(
@@ -497,11 +601,11 @@
     return call(
         ascend,
         (shape(16, 16, LANES), shape(16, 16, LANES)),
-        level_scratch(X0, Z0, 2 * LANES)
-        + [vmem(14, Z1, 2 * LANES), vmem(2, 14, Z0, LANES)]
-        + level_scratch(X1, Z1, LANES)
+        rb_scratch(X0, Z0, 4)
+        + [vmem(14, Z0, LANES)]
+        + level_scratch(X1, Z1)[1:]
         + [vmem(12, 16, LANES), vmem(12, Z1, LANES)],
-    )(*wide, *narrow, *uwide, *unarrow, window)
+    )(top, s1, *narrow, window)
 
 
 def solution(mesh):

time: 125 us -> 113 us (0.904)
  starting transfers between devices: 58.4 us -> 41.2 us
  Pallas kernels: 26.6 us -> 30.7 us
  waiting for transfers between devices: 33.3 us -> 36.1 us
    ppermute x9 -> x6, starting transfers between devices: 27.2 us -> 12.5 us  [swap(): a = lax.ppermute(jnp.where(even, high, low), axis, first)]
    ppermute x9 -> x6, starting transfers between devices: 15.1 us -> 7.85 us  [swap(): b = lax.ppermute(jnp.where(even, low, high), axis, second)]
    all_to_all x2, starting transfers between devices: 13 us -> 17.8 us  [spread(): lax.all_to_all(jnp.broadcast_to(x[None], (n,) + x.shape), axes, 0, 0)]
    pallas_call x5 -> x4, Pallas kernels: 26.6 us -> 30.7 us  [run(): pl.pallas_call(kernel, out_shape=out_shape, in_specs=specs, out_specs=jax...]
    ppermute x9 -> x6, waiting for transfers between devices: 12.1 us -> 14.2 us  [swap(): b = lax.ppermute(jnp.where(even, low, high), axis, second)]
    ppermute x9 -> x6, waiting for transfers between devices: 7.14 us -> 8.87 us  [swap(): a = lax.ppermute(jnp.where(even, high, low), axis, first)]
    unnamed x8 -> x4, local copies, waits for them, and re-layouts: 2.74 us -> 1.8 us
  transfers between devices with their start and end apart: 21 -> 15, of which waited for: 9 -> 7; matrix products, arithmetic and copies ran while one was open for 1% -> 1% of each run, Pallas kernels for 0% -> 0%
where the time goes in v2:
time: 113 us
  starting transfers between devices  41.2 us (36%)
  waiting for transfers between devices  36.1 us (32%)
  Pallas kernels  30.7 us (27%)
  local copies, waits for them, and re-layouts  3.52 us (3%)
    pallas_call x4, Pallas kernels, run(): pl.pallas_call(kernel, out_shape=out_shape, in_specs=specs, out_specs=jax...  30.7 us
    all_to_all x2, starting transfers between devices, spread(): lax.all_to_all(jnp.broadcast_to(x[None], (n,) + x.shape), axes, 0, 0)  17.8 us
    ppermute x6, waiting for transfers between devices, swap(): b = lax.ppermute(jnp.where(even, low, high), axis, second)  14.2 us
    all_to_all x2, waiting for transfers between devices, spread(): lax.all_to_all(jnp.broadcast_to(x[None], (n,) + x.shape), axes, 0, 0)  13 us
    ppermute x6, starting transfers between devices, swap(): a = lax.ppermute(jnp.where(even, high, low), axis, first)  12.5 us
    ppermute x6, waiting for transfers between devices, swap(): a = lax.ppermute(jnp.where(even, high, low), axis, first)  8.87 us
    ppermute x6, starting transfers between devices, swap(): b = lax.ppermute(jnp.where(even, low, high), axis, second)  7.85 us
    ppermute x1, starting transfers between devices, gather(): return (mine, lax.ppermute(mine, 'co', [(0, 1), (1, 0)]))  3.11 us
  transfers between devices with their start and end apart: 15, of which 7 were waited for; matrix products, arithmetic and copies ran while one was open for 1% of the time, Pallas kernels for 0%

profile of v2, /device:TPU:1, one launch (start us, length us, event | category | flops | bytes accessed | tf_op | source)
XLA Modules:
  0.0 113.0 jit_solution(677205165874225010)
XLA Ops:
  0.6 0.0 copy-start
  0.7 0.9 copy-done
  1.5 0.0 copy-start.1
  1.6 0.9 copy-done.1
  2.5 0.6 shard_map.41
  3.1 0.7 collective-permute-start
  3.8 4.6 %collective-permute-start.1 = (f32[4,16,128]{2,1,0:T(8,128)S(1)}, f32[4,16,128]{2,1,0:T(8,128)S(1)}, u32[]{:S(2)}, u32[]{:S(2)}) collective-permute-start(f32[4,16,128]{2,1,0:T(8,128)S(1)} %get-tuple-element.43), channel_id=1, source_target_pairs={{0,8},{8,0},{16,24},{24,16},{1,9},{9,1},{17,25},{25,17},{2,10},{10... | collective-permute-start | bytes 98312 | tf_op jit(solution)/shard_map/ppermute | solution.py:502
  8.3 0.0 collective-permute-done
  8.3 1.3 %collective-permute-done.1 = f32[4,16,128]{2,1,0:T(8,128)S(1)} collective-permute-done((f32[4,16,128]{2,1,0:T(8,128)S(1)}, f32[4,16,128]{2,1,0:T(8,128)S(1)}, u32[]{:S(2)}, u32[]{:S(2)}) %collective-permute-start.1) | collective-permute-done | bytes 32800 | tf_op jit(solution)/shard_map/ppermute | solution.py:502
  9.7 1.7 %collective-permute-start.3 = (f32[80,8,128]{2,1,0:T(8,128)S(1)}, f32[80,8,128]{2,1,0:T(8,128)S(1)}, u32[]{:S(2)}, u32[]{:S(2)}) collective-permute-start(f32[80,8,128]{2,1,0:T(8,128)S(1)} %pad_maximum_fusion.5), channel_id=1, source_target_pairs={{0,1},{1,0},{2,3},{3,2},{4,5},{5,4},{6,7},{7,6},{8,9},{9,8},{10,11... | collective-permute-start | bytes 983048 | tf_op jit(solution)/shard_map/ppermute | solution.py:502
  11.4 0.7 collective-permute-start.2
  12.1 5.4 %collective-permute-done.3 = f32[80,8,128]{2,1,0:T(8,128)S(1)} collective-permute-done((f32[80,8,128]{2,1,0:T(8,128)S(1)}, f32[80,8,128]{2,1,0:T(8,128)S(1)}, u32[]{:S(2)}, u32[]{:S(2)}) %collective-permute-start.3) | collective-permute-done | bytes 327712 | tf_op jit(solution)/shard_map/ppermute | solution.py:502
  17.5 0.0 collective-permute-done.2
  17.6 0.1 pad_maximum_fusion.4.e
  17.7 0.1 fusion.3
  17.8 0.1 fusion
  17.9 2.7 %collective-permute-start.5 = (f32[180,8,128]{2,1,0:T(8,128)S(1)}, f32[180,8,128]{2,1,0:T(8,128)S(1)}, u32[]{:S(2)}, u32[]{:S(2)}) collective-permute-start(f32[180,8,128]{2,1,0:T(8,128)S(1)} %get-tuple-element.18), channel_id=1, source_target_pairs={{0,32},{32,0},{64,96},{96,64},{128,160},{160,128},{192,224},{224,1... | collective-permute-start | bytes 2211848 | tf_op jit(solution)/shard_map/ppermute | solution.py:502
  20.6 3.1 %collective-permute-start.4 = (f32[180,8,128]{2,1,0:T(8,128)S(1)}, f32[180,8,128]{2,1,0:T(8,128)S(1)}, u32[]{:S(2)}, u32[]{:S(2)}) collective-permute-start(f32[180,8,128]{2,1,0:T(8,128)S(1)} %get-tuple-element.19), channel_id=1, source_target_pairs={{32,64},{96,128},{160,192},{64,32},{128,96},{192,160},{33,65},{97,... | collective-permute-start | bytes 2211848 | tf_op jit(solution)/shard_map/ppermute | solution.py:503
  23.7 0.0 collective-permute-done.5
  23.7 9.6 %collective-permute-done.4 = f32[180,8,128]{2,1,0:T(8,128)S(1)} collective-permute-done((f32[180,8,128]{2,1,0:T(8,128)S(1)}, f32[180,8,128]{2,1,0:T(8,128)S(1)}, u32[]{:S(2)}, u32[]{:S(2)}) %collective-permute-start.4) | collective-permute-done | bytes 737312 | tf_op jit(solution)/shard_map/ppermute | solution.py:503
  33.4 0.1 broadcast_select_fusion
  33.6 12.1 %shard_map.42 = (f32[5,26,32,128]{3,2,1,0:T(8,128)S(1)}, f32[22,24,128]{2,1,0:T(8,128)S(1)}, f32[2,8,8,128]{3,2,1,0:T(8,128)S(1)}, f32[8,128]{1,0:T(8,128)S(1)}) custom-call(f32[2,16,48,128]{3,2,1,0:T(8,128)S(1)} %pad_maximum_fusion.4.e, f32[4,48,128]{2,1,0:T(8,128)S(1)} %get-tuple-element.44.b, f32[4,48,128]{2,1,0:T(8,128)S(1)} %get-tuple-element.45.a, ...), custom_call_target="tpu_custom_call" | custom-call | tf_op jit(solution)/shard_map/pallas_call | solution.py:261
  45.8 0.7 collective-permute-start.7
  46.4 3.0 %collective-permute-start.6 = (f32[2,8,8,128]{3,2,1,0:T(8,128)S(1)}, f32[2,8,8,128]{3,2,1,0:T(8,128)S(1)}, u32[]{:S(2)}, u32[]{:S(2)}) collective-permute-start(f32[2,8,8,128]{3,2,1,0:T(8,128)S(1)} %get-tuple-element.14), channel_id=1, source_target_pairs={{0,8},{8,0},{16,24},{24,16},{1,9},{9,1},{17,25},{25,17},{2,10},{10... | collective-permute-start | bytes 196616 | tf_op jit(solution)/shard_map/ppermute | solution.py:502
  49.5 0.6 broadcast_in_dim.12
  50.1 11.8 %all-to-all-start = ((f32[8,1,8,128]{3,2,1,0:T(8,128)}), f32[8,1,8,128]{3,2,1,0:T(8,128)S(1)}, u32[]{:S(2)}, u32[]{:S(2)}) async-start(f32[8,1,8,128]{3,2,1,0:T(8,128)} %broadcast_in_dim.12), calls=%async_computation | async-start | bytes 65536 | tf_op jit(solution)/shard_map/all_to_all | solution.py:552
  62.0 6.9 %all-to-all-done = f32[8,1,8,128]{3,2,1,0:T(8,128)S(1)} async-done(((f32[8,1,8,128]{3,2,1,0:T(8,128)}), f32[8,1,8,128]{3,2,1,0:T(8,128)S(1)}, u32[]{:S(2)}, u32[]{:S(2)}) %all-to-all-start) | async-done | bytes 32800 | tf_op jit(solution)/shard_map/all_to_all | solution.py:552
  68.8 0.8 broadcast_in_dim.14
  69.7 5.9 %all-to-all-start.1 = ((f32[16,8,8,128]{3,2,1,0:T(8,128)}), f32[16,8,8,128]{3,2,1,0:T(8,128)S(1)}, u32[]{:S(2)}, u32[]{:S(2)}) async-start(f32[16,8,8,128]{3,2,1,0:T(8,128)} %broadcast_in_dim.14), calls=%async_computation.1 | async-start | bytes 1048576 | tf_op jit(solution)/shard_map/all_to_all | solution.py:552
  75.6 0.0 collective-permute-done.7
  75.6 0.0 collective-permute-done.6
  75.7 0.4 collective-permute-start.9
  76.0 0.7 collective-permute-start.8
  76.7 2.2 %collective-permute-done.9 = f32[2,8,8,128]{3,2,1,0:T(8,128)S(1)} collective-permute-done((f32[2,8,8,128]{3,2,1,0:T(8,128)S(1)}, f32[2,8,8,128]{3,2,1,0:T(8,128)S(1)}, u32[]{:S(2)}, u32[]{:S(2)}) %collective-permute-start.9) | collective-permute-done | bytes 65568 | tf_op jit(solution)/shard_map/ppermute | solution.py:502
  78.9 0.0 collective-permute-done.8
  78.9 6.1 %all-to-all-done.1 = f32[16,8,8,128]{3,2,1,0:T(8,128)S(1)} async-done(((f32[16,8,8,128]{3,2,1,0:T(8,128)}), f32[16,8,8,128]{3,2,1,0:T(8,128)S(1)}, u32[]{:S(2)}, u32[]{:S(2)}) %all-to-all-start.1) | async-done | bytes 524320 | tf_op jit(solution)/shard_map/all_to_all | solution.py:552
  85.0 3.1 %collective-permute-start.12 = (f32[128,8,128]{2,1,0:T(8,128)S(1)}, f32[128,8,128]{2,1,0:T(8,128)S(1)}, u32[]{:S(2)}, u32[]{:S(2)}) collective-permute-start(f32[128,8,128]{2,1,0:T(8,128)S(1)} %bitcast.28), channel_id=1, source_target_pairs={{0,32},{32,0},{1,33},{33,1},{2,34},{34,2},{3,35},{35,3},{4,36},{36... | collective-permute-start | bytes 1572872 | tf_op jit(solution)/shard_map/ppermute | solution.py:556
  88.2 0.1 collective-permute-start.11
  88.3 2.1 %collective-permute-start.10 = (f32[2,7,24,128]{3,2,1,0:T(8,128)S(1)}, f32[2,7,24,128]{3,2,1,0:T(8,128)S(1)}, u32[]{:S(2)}, u32[]{:S(2)}) collective-permute-start(f32[2,7,24,128]{3,2,1,0:T(8,128)S(1)} %get-tuple-element.37), channel_id=1, source_target_pairs={{32,64},{96,128},{160,192},{64,32},{128,96},{192,160},{33,65},{97,... | collective-permute-start | bytes 516104 | tf_op jit(solution)/shard_map/ppermute | solution.py:503
  90.4 0.1 pad_add_fusion.where_ref
  90.5 0.0 collective-permute-done.11
  90.5 4.5 %collective-permute-done.10 = f32[2,7,24,128]{3,2,1,0:T(8,128)S(1)} collective-permute-done((f32[2,7,24,128]{3,2,1,0:T(8,128)S(1)}, f32[2,7,24,128]{3,2,1,0:T(8,128)S(1)}, u32[]{:S(2)}, u32[]{:S(2)}) %collective-permute-start.10) | collective-permute-done | bytes 172064 | tf_op jit(solution)/shard_map/ppermute | solution.py:503
  95.0 0.0 collective-permute-done.12.other_ref
  95.0 10.9 %shard_map.43.win = f32[12,16,128]{2,1,0:T(8,128)S(1)} custom-call(s32[3]{0:T(128)S(1)} %pad_add_fusion.where_ref, f32[128,8,128]{2,1,0:T(8,128)S(1)} %bitcast.29, f32[128,8,128]{2,1,0:T(8,128)S(1)} %collective-permute-done.12.other_ref), custom_call_target="tpu_custom_call" | custom-call | tf_op jit(solution)/shard_map/pallas_call | solution.py:261
  106.0 7.0 %shard_map.44 = (f32[16,16,128]{2,1,0:T(8,128)}, f32[16,16,128]{2,1,0:T(8,128)}) custom-call(f32[5,26,32,128]{3,2,1,0:T(8,128)S(1)} %get-tuple-element.12.top, f32[22,24,128]{2,1,0:T(8,128)S(1)} %get-tuple-element.13.sl, f32[2,8,24,128]{3,2,1,0:T(8,128)S(1)} %pad_maximum_fusion.6.m, f32[2,7,24,128]{3,2,1,0:T(8,128)S(1)} %get-tuple-element.31.ml, ...), custom_call_target="tpu_custom_call" | custom-call | tf_op jit(solution)/shard_map/pallas_call | solution.py:261
  (22 shorter events, 0.4 us)
Async XLA Ops:
  0.6 0.9 copy-start
  1.5 0.9 copy-start.1
  3.1 5.3 %collective-permute-start = (f32[4,16,128]{2,1,0:T(8,128)S(1)}, f32[4,16,128]{2,1,0:T(8,128)S(1)}, u32[]{:S(2)}, u32[]{:S(2)}) collective-permute-start(f32[4,16,128]{2,1,0:T(8,128)S(1)} %get-tuple-element.42), channel_id=1, source_target_pairs={{8,16},{16,8},{9,17},{17,9},{10,18},{18,10},{11,19},{19,11},{12,20... | collective-permute-start | bytes 98312 | tf_op jit(solution)/shard_map/ppermute | solution.py:503
  3.8 5.9 %collective-permute-start.1 = (f32[4,16,128]{2,1,0:T(8,128)S(1)}, f32[4,16,128]{2,1,0:T(8,128)S(1)}, u32[]{:S(2)}, u32[]{:S(2)}) collective-permute-start(f32[4,16,128]{2,1,0:T(8,128)S(1)} %get-tuple-element.43), channel_id=1, source_target_pairs={{0,8},{8,0},{16,24},{24,16},{1,9},{9,1},{17,25},{25,17},{2,10},{10... | collective-permute-start | bytes 98312 | tf_op jit(solution)/shard_map/ppermute | solution.py:502
  9.7 7.8 %collective-permute-start.3 = (f32[80,8,128]{2,1,0:T(8,128)S(1)}, f32[80,8,128]{2,1,0:T(8,128)S(1)}, u32[]{:S(2)}, u32[]{:S(2)}) collective-permute-start(f32[80,8,128]{2,1,0:T(8,128)S(1)} %pad_maximum_fusion.5), channel_id=1, source_target_pairs={{0,1},{1,0},{2,3},{3,2},{4,5},{5,4},{6,7},{7,6},{8,9},{9,8},{10,11... | collective-permute-start | bytes 983048 | tf_op jit(solution)/shard_map/ppermute | solution.py:502
  11.4 6.1 %collective-permute-start.2 = (f32[80,8,128]{2,1,0:T(8,128)S(1)}, f32[80,8,128]{2,1,0:T(8,128)S(1)}, u32[]{:S(2)}, u32[]{:S(2)}) collective-permute-start(f32[80,8,128]{2,1,0:T(8,128)S(1)} %pad_maximum_fusion.5), channel_id=1, source_target_pairs={{1,2},{3,4},{5,6},{2,1},{4,3},{6,5},{9,10},{11,12},{13,14},{10,9},... | collective-permute-start | bytes 983048 | tf_op jit(solution)/shard_map/ppermute | solution.py:503
  17.9 5.8 %collective-permute-start.5 = (f32[180,8,128]{2,1,0:T(8,128)S(1)}, f32[180,8,128]{2,1,0:T(8,128)S(1)}, u32[]{:S(2)}, u32[]{:S(2)}) collective-permute-start(f32[180,8,128]{2,1,0:T(8,128)S(1)} %get-tuple-element.18), channel_id=1, source_target_pairs={{0,32},{32,0},{64,96},{96,64},{128,160},{160,128},{192,224},{224,1... | collective-permute-start | bytes 2211848 | tf_op jit(solution)/shard_map/ppermute | solution.py:502
  20.6 12.8 %collective-permute-start.4 = (f32[180,8,128]{2,1,0:T(8,128)S(1)}, f32[180,8,128]{2,1,0:T(8,128)S(1)}, u32[]{:S(2)}, u32[]{:S(2)}) collective-permute-start(f32[180,8,128]{2,1,0:T(8,128)S(1)} %get-tuple-element.19), channel_id=1, source_target_pairs={{32,64},{96,128},{160,192},{64,32},{128,96},{192,160},{33,65},{97,... | collective-permute-start | bytes 2211848 | tf_op jit(solution)/shard_map/ppermute | solution.py:503
  45.8 29.8 %collective-permute-start.7 = (f32[2,8,8,128]{3,2,1,0:T(8,128)S(1)}, f32[2,8,8,128]{3,2,1,0:T(8,128)S(1)}, u32[]{:S(2)}, u32[]{:S(2)}) collective-permute-start(f32[2,8,8,128]{3,2,1,0:T(8,128)S(1)} %get-tuple-element.14), channel_id=1, source_target_pairs={{8,16},{16,8},{9,17},{17,9},{10,18},{18,10},{11,19},{19,11},{12,20... | collective-permute-start | bytes 196616 | tf_op jit(solution)/shard_map/ppermute | solution.py:503
  46.4 29.2 %collective-permute-start.6 = (f32[2,8,8,128]{3,2,1,0:T(8,128)S(1)}, f32[2,8,8,128]{3,2,1,0:T(8,128)S(1)}, u32[]{:S(2)}, u32[]{:S(2)}) collective-permute-start(f32[2,8,8,128]{3,2,1,0:T(8,128)S(1)} %get-tuple-element.14), channel_id=1, source_target_pairs={{0,8},{8,0},{16,24},{24,16},{1,9},{9,1},{17,25},{25,17},{2,10},{10... | collective-permute-start | bytes 196616 | tf_op jit(solution)/shard_map/ppermute | solution.py:502
  50.1 18.7 %all-to-all-start = ((f32[8,1,8,128]{3,2,1,0:T(8,128)}), f32[8,1,8,128]{3,2,1,0:T(8,128)S(1)}, u32[]{:S(2)}, u32[]{:S(2)}) async-start(f32[8,1,8,128]{3,2,1,0:T(8,128)} %broadcast_in_dim.12), calls=%async_computation | async-start | bytes 65536 | tf_op jit(solution)/shard_map/all_to_all | solution.py:552
  69.7 15.4 %all-to-all-start.1 = ((f32[16,8,8,128]{3,2,1,0:T(8,128)}), f32[16,8,8,128]{3,2,1,0:T(8,128)S(1)}, u32[]{:S(2)}, u32[]{:S(2)}) async-start(f32[16,8,8,128]{3,2,1,0:T(8,128)} %broadcast_in_dim.14), calls=%async_computation.1 | async-start | bytes 1048576 | tf_op jit(solution)/shard_map/all_to_all | solution.py:552
  75.7 3.2 %collective-permute-start.9 = (f32[2,8,8,128]{3,2,1,0:T(8,128)S(1)}, f32[2,8,8,128]{3,2,1,0:T(8,128)S(1)}, u32[]{:S(2)}, u32[]{:S(2)}) collective-permute-start(f32[2,8,8,128]{3,2,1,0:T(8,128)S(1)} %select_select_fusion), channel_id=1, source_target_pairs={{0,1},{1,0},{2,3},{3,2},{4,5},{5,4},{6,7},{7,6},{8,9},{9,8},{10,11... | collective-permute-start | bytes 196616 | tf_op jit(solution)/shard_map/ppermute | solution.py:502
  76.0 2.8 %collective-permute-start.8 = (f32[2,8,8,128]{3,2,1,0:T(8,128)S(1)}, f32[2,8,8,128]{3,2,1,0:T(8,128)S(1)}, u32[]{:S(2)}, u32[]{:S(2)}) collective-permute-start(f32[2,8,8,128]{3,2,1,0:T(8,128)S(1)} %select_select_fusion), channel_id=1, source_target_pairs={{1,2},{3,4},{5,6},{2,1},{4,3},{6,5},{9,10},{11,12},{13,14},{10,9},... | collective-permute-start | bytes 196616 | tf_op jit(solution)/shard_map/ppermute | solution.py:503
  85.0 10.0 %collective-permute-start.12 = (f32[128,8,128]{2,1,0:T(8,128)S(1)}, f32[128,8,128]{2,1,0:T(8,128)S(1)}, u32[]{:S(2)}, u32[]{:S(2)}) collective-permute-start(f32[128,8,128]{2,1,0:T(8,128)S(1)} %bitcast.28), channel_id=1, source_target_pairs={{0,32},{32,0},{1,33},{33,1},{2,34},{34,2},{3,35},{35,3},{4,36},{36... | collective-permute-start | bytes 1572872 | tf_op jit(solution)/shard_map/ppermute | solution.py:556
  88.2 2.3 %collective-permute-start.11 = (f32[2,7,24,128]{3,2,1,0:T(8,128)S(1)}, f32[2,7,24,128]{3,2,1,0:T(8,128)S(1)}, u32[]{:S(2)}, u32[]{:S(2)}) collective-permute-start(f32[2,7,24,128]{3,2,1,0:T(8,128)S(1)} %get-tuple-element.36), channel_id=1, source_target_pairs={{0,32},{32,0},{64,96},{96,64},{128,160},{160,128},{192,224},{224,1... | collective-permute-start | bytes 516104 | tf_op jit(solution)/shard_map/ppermute | solution.py:502
  88.3 6.7 %collective-permute-start.10 = (f32[2,7,24,128]{3,2,1,0:T(8,128)S(1)}, f32[2,7,24,128]{3,2,1,0:T(8,128)S(1)}, u32[]{:S(2)}, u32[]{:S(2)}) collective-permute-start(f32[2,7,24,128]{3,2,1,0:T(8,128)S(1)} %get-tuple-element.37), channel_id=1, source_target_pairs={{32,64},{96,128},{160,192},{64,32},{128,96},{192,160},{33,65},{97,... | collective-permute-start | bytes 516104 | tf_op jit(solution)/shard_map/ppermute | solution.py:503

commit v3 on v2

v3 whole, which is shorter than its diff:
```python
import functools

import jax
import jax.numpy as jnp
from jax import lax
from jax.experimental import pallas as pl
from jax.experimental.pallas import tpu as pltpu
from jax.sharding import PartitionSpec as P

NU = 2
BOTTOM = 8
F32 = jnp.float32
LANES = 128
STRIP = 8

HD, XD, ZD = 14, 44, 48
NEAR = 5
H0, X0, Z0 = 5, 26, 32
HALF = LANES // 2
H1, X1, Z1 = 7, 22, 24


def roll(v, shift, axis):
    return pltpu.roll(v, shift % v.shape[axis], axis)


def iota(shape, axis):
    return lax.broadcasted_iota(jnp.int32, shape, axis)


def exact_dot(a, b):
    return jnp.dot(a, b, precision=lax.Precision.HIGHEST, preferred_element_type=F32)


def reds(shape, parity):
    return ((iota(shape, 0) + iota(shape, 1)) & 1) == parity % 2


def couplings(s_ref, f_ref, c_ref, g_ref, w_ref, first, last, scale, so=0, edges=False, step=1, lanes=1):
    shape = s_ref.shape[1:]
    if edges:
        z = iota(shape, 0)
        walls = (None, None, z == shape[0] - 1, z == 0, None, None)

    def chunk(x, n):
        s = [s_ref[x + so + k] for k in range(-1, n + 1)]
        for k in range(n):
            centre = s[k + 1]
            near = [
                s[k + 2],
                s[k],
                roll(centre, -1, 0),
                roll(centre, 1, 0),
                roll(centre, -lanes, 1),
                roll(centre, lanes, 1),
            ]
            if edges:
                near = [v if wall is None else jnp.where(wall, 0.0, v) for v, wall in zip(near, walls)]
            betas = [centre + v for v in near]
            total = ((betas[0] + betas[1]) + (betas[2] + betas[3])) + (betas[4] + betas[5])
            inverse = jnp.where(centre > 0.0, 1.0 / total, 0.0)
            for d in range(6):
                c = betas[d] * inverse
                if edges and walls[d] is not None:
                    c = jnp.where(walls[d], 0.0, c)
                c_ref[d, x + k] = c
            g_ref[x + k] = f_ref[x + k] * (inverse * (2.0 * scale))
            w_ref[x + k] = total * (0.5 / scale)

    stepped(chunk, first, last, step)


def stepped(chunk, first, last, step):
    count, rest = divmod(last - first, step)
    if count == 1:
        chunk(first, step)
    elif count:

        def body(i, carry):
            chunk(first + i * step, step)
            return carry

        lax.fori_loop(0, count, body, 0)
    if rest:
        chunk(last - rest, rest)


def relaxed(u, c_ref, g_ref, x, lanes=1):
    low, centre, high = u
    a = c_ref[0, x] * high + c_ref[1, x] * low
    b = c_ref[2, x] * roll(centre, -1, 0) + c_ref[3, x] * roll(centre, 1, 0)
    d = c_ref[4, x] * roll(centre, -lanes, 1) + c_ref[5, x] * roll(centre, lanes, 1)
    return g_ref[x] + ((a + b) + d)


def half_sweep(u_ref, c_ref, g_ref, first, last, parity, uo=0, step=4):
    shape = u_ref.shape[1:]
    masks = (reds(shape, parity + first), reds(shape, parity + first + 1))

    def chunk(x, n):
        u = [u_ref[x + uo + k] for k in range(-1, n + 1)]
        new = [jnp.where(masks[k % 2], relaxed(u[k : k + 3], c_ref, g_ref, x + k), u[k + 1]) for k in range(n)]
        for k in range(n):
            u_ref[x + uo + k] = new[k]

    stepped(chunk, first, last, step)


def first_half_sweep(u_ref, g_ref, first, last, parity, uo=0, step=4):
    shape = u_ref.shape[1:]
    masks = (reds(shape, parity + first), reds(shape, parity + first + 1))

    def chunk(x, n):
        for k in range(n):
            u_ref[x + uo + k] = jnp.where(masks[k % 2], g_ref[x + k], 0.0)

    stepped(chunk, first, last, step)


def residual_planes(u_ref, c_ref, g_ref, w_ref, x, n, uo=0):
    u = [u_ref[x + uo + k] for k in range(-1, n + 1)]
    return [w_ref[x + k] * (relaxed(u[k : k + 3], c_ref, g_ref, x + k) - u[k + 1]) for k in range(n)]


def phases(shape, parity):
    return (iota(shape, 0) & 1) == parity % 2


def beside(planes, below):
    out = []
    for a, b in zip(planes[0::2], planes[1::2]):
        lower = roll(jnp.where(below, a, b), 1, 1)
        upper = roll(jnp.where(below, b, a), -1, 1)
        out += [jnp.where(below, lower, upper), jnp.where(below, upper, lower)]
    return out


def couplings_rb(s, f, c, g, w, first, last, scale, parity, step, so=0, edges=False):
    shape = s.shape[2:]
    masks = (phases(shape, parity), phases(shape, parity + 1))
    z, j = iota(shape, 0), iota(shape, 1) & (HALF - 1)
    walls = [None] * 5
    if edges:
        walls = [None, None, z == shape[0] - 1, z == 0, None]
        ends = [j == jnp.where(m, 0, HALF - 1) for m in masks]

    def chunk(x, n):
        for col in range(2):
            others = [s[1 - col, x + k + so] for k in range(n)]
            others = list(zip(others, beside(others, masks[(first + col) % 2])))
            for k in range(n):
                m = (first + k + col) % 2
                centre = s[col, x + k + so]
                v, second = others[k]
                near = [
                    s[1 - col, x + k + so + 1],
                    s[1 - col, x + k + so - 1],
                    roll(v, -1, 0),
                    roll(v, 1, 0),
                    v,
                    second,
                ]
                wall = walls + [ends[m] if edges else None]
                near = [v if e is None else jnp.where(e, 0.0, v) for v, e in zip(near, wall)]
                betas = [centre + v for v in near]
                total = ((betas[0] + betas[1]) + (betas[2] + betas[3])) + (betas[4] + betas[5])
                inverse = jnp.where(centre > 0.0, 1.0 / total, 0.0)
                for d in range(6):
                    v = betas[d] * inverse
                    c[col, d, x + k] = v if wall[d] is None else jnp.where(wall[d], 0.0, v)
                g[col, x + k] = f[col, x + k] * (inverse * (2.0 * scale))
                w[col, x + k] = total * (0.5 / scale)

    stepped(chunk, first, last, step)


def relaxed_rb(v, second, c, g, col, x):
    low, centre, high = v
    a = c[col, 0, x] * high + c[col, 1, x] * low
    b = c[col, 2, x] * roll(centre, -1, 0) + c[col, 3, x] * roll(centre, 1, 0)
    d = c[col, 4, x] * centre + c[col, 5, x] * second
    return g[col, x] + ((a + b) + d)


def half_sweep_rb(u_ref, v_ref, c, g, col, first, last, parity, step, uo=0):
    mask = phases(v_ref.shape[1:], parity + first + col)

    def chunk(x, n):
        v = [v_ref[x + k + uo] for k in range(-1, n + 1)]
        seconds = beside(v[1:-1], mask)
        for k in range(n):
            u_ref[x + k + uo] = relaxed_rb(v[k : k + 3], seconds[k], c, g, col, x + k)

    stepped(chunk, first, last, step)


def residuals_rb(u, c, g, w, first, x, n, parity, uo=0):
    out = []
    for col in range(2):
        v = [u[1 - col, x + k + uo] for k in range(-1, n + 1)]
        seconds = beside(v[1:-1], phases(u.shape[2:], parity + first + col))
        new = [relaxed_rb(v[k : k + 3], seconds[k], c, g, col, x + k) for k in range(n)]
        out.append([w[col, x + k] * (new[k] - u[col, x + k + uo]) for k in range(n)])
    return out


def permuted(v, back):
    k, l = iota((LANES, LANES), 0), iota((LANES, LANES), 1)
    if back:
        k, l = l, k
    move = jnp.where(k == jnp.where(l < HALF, 2 * l, 2 * (l - HALF) + 1), 1.0, 0.0).astype(jnp.bfloat16)
    first = v.astype(jnp.bfloat16)
    rest = v - first.astype(F32)
    second = rest.astype(jnp.bfloat16)
    third = (rest - second.astype(F32)).astype(jnp.bfloat16)
    parts = [jnp.dot(x, move, preferred_element_type=F32) for x in (first, second, third)]
    return (parts[0] + parts[1]) + parts[2]


def swapped_rows(v, parity):
    return jnp.where(phases(v.shape, parity), v, roll(v, HALF, 1))


def packed(planes, at, group):
    rows = planes[0].shape[0]
    groups = iota((rows, LANES), 1) >> 3
    out = jnp.zeros((rows, LANES), F32)
    for k, v in enumerate(planes):
        out = jnp.where(groups == group(k), roll(v, STRIP * group(k) - at, 1), out)
    return out


def high_group(k):
    return 2 * k


def low_group(k):
    return (2 * k + 7) % 16


def fill_rb(out, i, at, planes_ref, strips, k0, count, rows, step=4):
    number = rows.stop - rows.start
    lane = iota((number, LANES), 1)
    own = lane < HALF
    halo = jnp.logical_or(lane < HALF + STRIP, lane >= LANES - STRIP)

    def chunk(n, many):
        for m in range(many):
            v = planes_ref[n + m]
            shift = lax.rem(HALF + LANES - 2 * STRIP * lax.rem(n + m + k0, 8), LANES)
            for col in range(2):
                h = jnp.where(halo, pltpu.roll(strips(2 * i + col), shift, 1), 0.0)
                out[col, at + n + m, rows.start : rows.stop] = jnp.where(own, roll(v, HALF, 1) if col else v, h)
                if number < ZD:
                    out[col, at + n + m, : rows.start] = jnp.zeros((rows.start, LANES), F32)
                    out[col, at + n + m, rows.stop :] = jnp.zeros((ZD - rows.stop, LANES), F32)

    def body(n, carry):
        chunk(n * step, step)
        return carry

    lax.fori_loop(0, count // step, body, 0)
    if count % step:
        chunk(jnp.int32(count - count % step), count % step)


def fill_narrow(u, f, own, low, high):
    lane = iota((Z1, LANES), 1)
    for part, at, count in ((low, 0, H1), (own, H1, 8), (high, H1 + 8, H1)):
        for k in range(count):
            v, h = part[0, k], part[1, k]
            u[at + k] = jnp.where(lane < HALF, v, roll(h, HALF, 1))
            f[at + k] = jnp.where(lane < HALF, roll(v, HALF, 1), h)


def call(kernel, out_shape, scratch, smem=0, cost=4):
    def run(*args):
        specs = [pl.BlockSpec(memory_space=pltpu.SMEM)] * smem
        specs += [pl.BlockSpec(memory_space=pltpu.VMEM)] * (len(args) - smem)
        return pl.pallas_call(
            kernel,
            out_shape=out_shape,
            in_specs=specs,
            out_specs=jax.tree.map(lambda _: pl.BlockSpec(memory_space=pltpu.VMEM), out_shape),
            scratch_shapes=scratch,
            compiler_params=pltpu.CompilerParams(vmem_limit_bytes=40 * 2**20),
            cost_estimate=pl.CostEstimate(flops=cost * 10**6, bytes_accessed=cost * 3 * 10**6, transcendentals=0),
        )(*args)

    return run


def vmem(*shape):
    return pltpu.VMEM(shape, F32)


def packing(f_ref, s_ref, out_ref, lo_ref, hi_ref):
    for i, ref in enumerate((f_ref, s_ref)):
        out_ref[i] = permuted(ref[...].reshape(256, LANES), False).reshape(16, 16, LANES)
        planes = [swapped_rows(out_ref[i, x], x) for x in range(16)]
        for x in range(16):
            out_ref[i, x] = planes[x]
        for col in range(2):
            for q in range(2):
                some = planes[8 * q : 8 * q + 8]
                lo_ref[2 * i + col, q] = packed(some, HALF * col, high_group)
                hi_ref[2 * i + col, q] = packed(some, HALF * col + HALF - STRIP, low_group)


def descend(e, b, lsn, lsf, lfn, lff, lb0, lb1, hsn, hsf, hfn, hff, hb0, hb1, top_out, s1_out, next_out, tile_out, s, f, c, g, w, u, q, fl, cl, gl, wl, ul, ql, t):
    every, some = slice(0, ZD), slice(8, ZD - 8)
    for i, out, ln, lf, hn, hf, near, deep in ((0, f, lfn, lff, hfn, hff, 3, 12), (1, s, lsn, lsf, hsn, hsf, NEAR, HD)):
        first = 16 - deep
        fill_rb(out, i, HD - deep, lf, lambda n: lb0[n], first, 8 - first, some)
        fill_rb(out, i, HD - 8, lf.at[8 - first :], lambda n: lb1[n, 8 : ZD - 8], 8, 8 - near, some)
        fill_rb(out, i, HD - near, ln, lambda n: lb1[n], 16 - near, near, every)
        for h in range(2):
            fill_rb(out, i, HD + 8 * h, e.at[i, 8 * h : 8 * h + 8], lambda n, h=h: b[n, h], 8 * h, 8, every)
        fill_rb(out, i, HD + 16, hn, lambda n: hb0[n], 0, near, every)
        fill_rb(out, i, HD + 16 + near, hf, lambda n: hb0[n, 8 : ZD - 8], near, 8 - near, some)
        fill_rb(out, i, HD + 24, hf.at[8 - near :], lambda n: hb1[n], 8, deep - 8, some)
    couplings_rb(s, f, c, g, w, 2, XD - 2, 1.0, 0, 4)
    red, black = u.at[0], u.at[1]
    half_sweep_rb(black, g.at[0], c, g, 1, 3, XD - 3, 0, 10)
    half_sweep_rb(red, black, c, g, 0, 4, XD - 4, 0, 12)
    half_sweep_rb(black, red, c, g, 1, 5, XD - 5, 0, 12)

    def residual_body(i, carry):
        r = residuals_rb(u, c, g, w, 6, 6 + 8 * i, 8, 0)
        for k in range(4):
            q[0, 4 * i + k + 3] = (r[0][2 * k] + r[0][2 * k + 1]) + (r[1][2 * k] + r[1][2 * k + 1])
        return carry

    lax.fori_loop(0, 4, residual_body, 0)
    nothing = jnp.zeros((ZD, LANES), F32)
    for i in (0, 1, 2, 19, 20, 21):
        q[0, i] = nothing

    def coefficient_body(i, carry):
        q[1, i] = (s[0, 2 * i] + s[0, 2 * i + 1]) + (s[1, 2 * i] + s[1, 2 * i + 1])
        return carry

    lax.fori_loop(0, X1, coefficient_body, 0)
    sl = s1_out
    for i, ref in enumerate((fl, sl)):
        ref[...] = 0.125 * (q[i, :, pl.ds(0, Z1, stride=2), :] + q[i, :, pl.ds(1, Z1, stride=2), :])

    def top_body(i, carry):
        for col in range(2):
            top_out[col, i] = s[col, HD - H0 + i, 8 : ZD - 8]
            top_out[2 + col, i] = f[col, HD - H0 + i, 8 : ZD - 8]
        top_out[4, i] = black[HD - H0 + i, 8 : ZD - 8]
        return carry

    lax.fori_loop(0, X0, top_body, 0)
    couplings(sl, fl, cl, gl, wl, 3, X1 - 3, 4.0, step=4)
    first_half_sweep(ul, gl, 3, X1 - 3, H1, step=8)
    half_sweep(ul, cl, gl, 4, X1 - 4, H1 + 1, step=14)
    half_sweep(ul, cl, gl, 5, X1 - 5, H1, step=12)
    half_sweep(ul, cl, gl, 6, X1 - 6, H1 + 1, step=10)
    k, l = iota((LANES, LANES), 0), iota((LANES, LANES), 1)
    total = jnp.zeros((8, LANES), F32)
    r = residual_planes(ul, cl, gl, wl, H1, 8)
    own = iota((8, LANES), 1) < HALF
    for x in range(8):
        next_out[x] = jnp.where(own, ul[H1 + x, 8:16], roll(fl[H1 + x, 8:16], HALF, 1))
    for i in range(4):
        x = H1 + 2 * i
        ql[i, 0] = (r[2 * i] + r[2 * i + 1])[8:16]
        ql[i, 1] = sl[x, 8:16] + sl[x + 1, 8:16]
        for b in range(2):
            t[i, 4 * b : 4 * b + 4] = ql[i, b, pl.ds(0, 4, stride=2), :] + ql[i, b, pl.ds(1, 4, stride=2), :]
        to = 32 * i + 16 * ((k // 2) % 2) + k // 4
        place = jnp.where(jnp.logical_and(k < HALF, l == to), 0.125, 0.0).astype(F32)
        total = total + exact_dot(t[i], place)
    group = iota((8, LANES), 1) // 16
    other = jnp.where(group % 2 == 0, roll(total, -16, 1), roll(total, 16, 1))
    tile_out[...] = jnp.where((group // 2 + iota((8, LANES), 0)) % 2 == 0, total, other)


def coarse(where_ref, mine_ref, other_ref, out_ref, s2, f2, c2, g2, w2, u2, q2, d2, s3, f3, c3, g3, w3, u3, q3, d3, s4, f4, c4, g4, w4):
    lane = iota((8, LANES), 1)
    wide = iota((32, LANES), 1)
    zero2 = jnp.zeros((32, LANES), F32)
    core = lax.rem(where_ref[0], 2)

    def transposed(groups):
        for s in (1, 2, 4):
            upper = (lane & (16 * s)) != 0
            for tiles in groups:
                for m in range(8):
                    if not m & s:
                        a, b = tiles[m], tiles[m + s]
                        tiles[m] = jnp.where(upper, roll(b, 16 * s, 1), a)
                        tiles[m + s] = jnp.where(upper, b, roll(a, -16 * s, 1))
        return groups

    def assemble(xcl, carry):
        for all_ref, c in ((mine_ref, core), (other_ref, 1 - core)):
            plane = 4 * (2 * xcl + c)
            groups = []
            for zi in range(8):
                at = [((2 * xh + xcl) * 4 + iy) * 8 + zi for xh in range(2) for iy in range(4)]
                groups.append([all_ref[i] for i in at])
            for zi, tiles in enumerate(transposed(groups)):
                rows = slice(8 * (zi // 2), 8 * (zi // 2) + 8)
                for g, v in enumerate(tiles):
                    if zi % 2 == 0:
                        f2[g % 2, plane + g // 2, rows] = v
                    else:
                        s2[g % 2, plane + g // 2 + 1, rows] = v
        return carry

    lax.fori_loop(0, 2, assemble, 0)

    def wrap(ref):
        ref[0] = jnp.where(wide < HALF, 0.0, roll(ref[16], HALF, 1))
        ref[17] = jnp.where(wide < HALF, roll(ref[1], HALF, 1), 0.0)

    for col in range(2):
        wrap(s2.at[col])
    for x in (0, 17):
        s3[x] = zero2[:16]
        u3[x] = zero2[:16]
    for x in (0, 9):
        s4[x] = zero2[:8]

    red, black = u2.at[0], u2.at[1]

    def sweep2(col):
        half_sweep_rb(u2.at[col], u2.at[1 - col], c2, g2, col, 0, 16, 0, 16, 1)
        wrap(u2.at[col])

    couplings_rb(s2, f2, c2, g2, w2, 0, 16, 16.0, 0, 4, 1, True)
    for x in range(16):
        red[x + 1] = g2[0, x]
    wrap(red)
    sweep2(1)
    sweep2(0)
    sweep2(1)

    def restrict2(i, carry):
        r = residuals_rb(u2, c2, g2, w2, 0, 8 * i, 8, 0, 1)
        for k in range(4):
            x = 8 * i + 2 * k + 1
            q2[0, 4 * i + k] = (r[0][2 * k] + r[0][2 * k + 1]) + (r[1][2 * k] + r[1][2 * k + 1])
            q2[1, 4 * i + k] = (s2[0, x] + s2[0, x + 1]) + (s2[1, x] + s2[1, x + 1])
        return carry

    lax.fori_loop(0, 2, restrict2, 0)
    narrow = iota((16, LANES), 1) < HALF
    for i, ref, at in ((0, f3, 0), (1, s3, 1)):
        for x in range(8):
            v = 0.125 * (q2[i, x, pl.ds(0, 16, stride=2), :] + q2[i, x, pl.ds(1, 16, stride=2), :])
            ref[x + at] = jnp.where(narrow, v, 0.0)
            ref[x + at + 8] = jnp.where(narrow, roll(v, HALF, 1), 0.0)
    couplings(s3, f3, c3, g3, w3, 0, 16, 64.0, so=1, edges=True, step=8)
    first_half_sweep(u3, g3, 0, 16, 0, 1, 16)
    for col in (1, 0, 1):
        half_sweep(u3, c3, g3, 0, 16, col, 1, 16)
    r = residual_planes(u3, c3, g3, w3, 0, 16, 1)
    for i in range(8):
        q3[0, i] = r[2 * i] + r[2 * i + 1]
        q3[1, i] = s3[2 * i + 1] + s3[2 * i + 2]
    lane4 = iota((8, LANES), 1)
    for i, ref, at in ((0, f4, 0), (1, s4, 1)):
        for x in range(8):
            v = 0.125 * (q3[i, x, pl.ds(0, 8, stride=2), :] + q3[i, x, pl.ds(1, 8, stride=2), :])
            ref[x + at] = jnp.where((lane4 & 1) == 0, v + roll(v, -1, 1), 0.0)
    couplings(s4, f4, c4, g4, w4, 0, 8, 256.0, so=1, edges=True, step=8, lanes=2)
    odd = (iota((8, LANES), 0) + (lane4 >> 1)) & 1
    masks = (odd == 0, odd == 1)
    nothing = jnp.zeros((8, LANES), F32)
    u4 = [jnp.where(masks[x % 2], g4[x], 0.0) for x in range(8)]
    for h in range(1, 2 * BOTTOM):
        around = [nothing] + u4 + [nothing]
        u4 = [jnp.where(masks[(x + h) % 2], relaxed(around[x : x + 3], c4, g4, x, 2), u4[x]) for x in range(8)]
    for x in range(8):
        v = u4[x] + roll(u4[x], 1, 1)
        d3[x, pl.ds(0, 8, stride=2), :] = v
        d3[x, pl.ds(1, 8, stride=2), :] = v
    for x in range(16):
        u3[x + 1] = u3[x + 1] + d3[x // 2]
    for col in (0, 1) * NU:
        half_sweep(u3, c3, g3, 0, 16, col, 1, 16)
    for x in range(8):
        v = jnp.where(narrow, u3[x + 1], roll(u3[x + 9], HALF, 1))
        d2[x, pl.ds(0, 16, stride=2), :] = v
        d2[x, pl.ds(1, 16, stride=2), :] = v
    for x in range(16):
        black[x + 1] = black[x + 1] + d2[x // 2]
    wrap(black)
    for _ in range(NU):
        sweep2(0)
        sweep2(1)
    ix, iy, iz = where_ref[0], where_ref[1], where_ref[2]
    down_z = lax.rem(36 - 4 * iz, 32)
    for n in range(12):
        x = 4 * ix + 12 + n
        at = lax.rem(x, 16) + 1
        shift = lax.rem(4 * LANES - HALF * (x // 16) - 16 * iy + HALF, LANES)
        for col in range(2):
            v = pltpu.roll(u2[col, at], down_z, 0)
            out_ref[col, n] = pltpu.roll(v[:16], shift, 1)


def ascend(top, sl, m, ml, mh, win, u_out, r_out, c, g, w, u, d0, fl, cl, gl, wl, ul, t1, d1):
    fill_narrow(ul, fl, m, ml, mh)
    couplings(sl, fl, cl, gl, wl, 1, X1 - 1, 4.0, step=4)
    k, l = iota((LANES, LANES), 0), iota((LANES, LANES), 1)
    from_lane = jnp.where(l < 96, l // 4, 96 + l // 4)
    parity = iota((1, 16, LANES), 1) + iota((12, 16, LANES), 0)
    v = [win[0], win[1]]
    both = [jnp.where(parity % 2 == 0, v[i], v[1 - i]).reshape(192, LANES) for i in range(2)]
    widen = [jnp.where(jnp.logical_and(k == from_lane, (l // 2) % 2 == i), 1.0, 0.0).astype(F32) for i in range(2)]
    t1[...] = (exact_dot(both[0], widen[0]) + exact_dot(both[1], widen[1])).reshape(12, 16, LANES)
    d1[:, pl.ds(0, 12, stride=2), :] = t1[:, :12]
    d1[:, pl.ds(1, 12, stride=2), :] = t1[:, :12]
    for x in range(X1):
        ul[x] = jnp.where(sl[x] > 0.0, ul[x] + d1[(x + 1) // 2], 0.0)
    half_sweep(ul, cl, gl, 1, X1 - 1, H1, step=10)
    half_sweep(ul, cl, gl, 2, X1 - 2, H1 + 1, step=18)
    half_sweep(ul, cl, gl, 3, X1 - 3, H1, step=16)
    half_sweep(ul, cl, gl, 4, X1 - 4, H1 + 1, step=14)
    s, f, black, red = top.at[0:2], top.at[2:4], u.at[1], u.at[0]
    couplings_rb(s, f, c, g, w, 1, X0 - 1, 1.0, 1, 6)
    fine = ul[4:18, 4:20]
    d0[:, pl.ds(0, 16, stride=2), :] = fine
    d0[:, pl.ds(1, 16, stride=2), :] = fine
    for x in range(X0):
        black[x] = jnp.where(top[1, x] > 0.0, top[4, x] + d0[(x + 1) // 2], 0.0)
    half_sweep_rb(red, black, c, g, 0, 1, X0 - 1, 1, 12)
    half_sweep_rb(black, red, c, g, 1, 2, X0 - 2, 1, 12)
    half_sweep_rb(red, black, c, g, 0, 3, X0 - 3, 1, 10)
    half_sweep_rb(black, red, c, g, 1, 4, X0 - 4, 1, 18)

    lane = iota((16, LANES), 1)

    def body(i, carry):
        x = H0 + 8 * i
        r = residuals_rb(u, c, g, w, H0, x, 8, 1)
        for j in range(8):
            for out, a, b in ((u_out, u[0, x + j], u[1, x + j]), (r_out, r[0][j], r[1][j])):
                both = jnp.where(lane < HALF, a[8:24], roll(b[8:24], HALF, 1))
                out[8 * i + j] = swapped_rows(both, j)
        return carry

    lax.fori_loop(0, 2, body, 0)
    for out in (u_out, r_out):
        out[...] = permuted(out[...].reshape(256, LANES), True).reshape(16, 16, LANES)


def axis_of(name):
    return ("xc", "co") if name == "gx" else name


def swap(low, high, name):
    axis = axis_of(name)
    count = lax.axis_size(axis)
    even = lax.axis_index(axis) % 2 == 0
    first = [(i, i ^ 1) for i in range(count)]
    second = [(i, i + 1) for i in range(1, count - 1, 2)]
    second += [(j, i) for i, j in second]
    a = lax.ppermute(jnp.where(even, high, low), axis, first)
    b = lax.ppermute(jnp.where(even, low, high), axis, second)
    return jnp.where(even, b, a), jnp.where(even, a, b)


def join(pieces):
    return jnp.concatenate([p.reshape(-1, 8, LANES) for p in pieces], 0)


def split(joined, like):
    out, at = [], 0
    for p in like:
        n = p.size // (8 * LANES)
        out.append(joined[at : at + n].reshape(p.shape))
        at += n
    return out


def swap_many(lows, highs, axis):
    low, high = swap(join(lows), join(highs), axis)
    return split(low, lows), split(high, highs)


def extend_wide(field, lo, hi):
    below, above = swap(lo, hi, "gy")
    group = lax.broadcasted_iota(jnp.int32, lo.shape, 3) // STRIP
    strips = jnp.where(group % 2 == 0, above, below)
    pieces = [field, strips]
    lows, highs = swap_many(pieces, pieces, "gz")
    field, strips = [jnp.concatenate(v, v[0].ndim - 2) for v in zip(lows, pieces, highs)]
    some = slice(8, ZD - 8)
    f, s = field[0], field[1]
    first = [s[:NEAR], s[NEAR:HD, some], f[:3], f[3:12, some], strips[:, 0], strips[:, 1, some]]
    last = [s[-NEAR:], s[-HD:-NEAR, some], f[-3:], f[-12:-3, some], strips[:, 0, some], strips[:, 1]]
    low, high = swap(join(first), join(last), "gx")
    return [field, strips] + split(low, last) + split(high, first)


def extend_narrow(own):
    below, above = swap(own, own, "gy")
    lane = lax.broadcasted_iota(jnp.int32, own.shape, 2)
    own = jnp.stack([own, jnp.where(lane % HALF < HALF // 2, above, below)])
    low, high = swap(own, own, "gz")
    own = jnp.concatenate([low, own, high], 2)
    low, high = swap(own[:, :H1], own[:, -H1:], "gx")
    return own, low, high


def spread(x, axes, sizes):
    n = 1
    for a in axes:
        n *= sizes[a]
    return lax.all_to_all(jnp.broadcast_to(x[None], (n,) + x.shape), axes, 0, 0)


def level_scratch(planes, rows):
    p = (planes, rows, LANES)
    return [vmem(*p), vmem(*p), vmem(6, *p), vmem(*p), vmem(*p), vmem(*p)]


def rb_scratch(planes, rows, count):
    p = (planes, rows, LANES)
    return ([vmem(2, *p)] * 6)[: count - 4] + [vmem(2, 6, *p)] + [vmem(2, *p)] * 3


def full_scratch(n, uo):
    p = (n, LANES)
    return [vmem(n + 2, *p), vmem(n, *p), vmem(6, n, *p), vmem(n, *p), vmem(n, *p), vmem(n + 2 * uo, *p)]


def shape(*dims):
    return jax.ShapeDtypeStruct(dims, F32)


def on_device(sizes, right_side, sigma):
    field, lo, hi = call(packing, [shape(2, 16, 16, LANES), shape(4, 2, 16, LANES), shape(4, 2, 16, LANES)], [])(right_side, sigma)
    top, s1, next1, tile = call(
        descend,
        [shape(5, X0, Z0, LANES), shape(X1, Z1, LANES), shape(8, 8, LANES), shape(8, LANES)],
        rb_scratch(XD, ZD, 6)
        + [vmem(2, X1, ZD, LANES)]
        + level_scratch(X1, Z1)[1:]
        + [vmem(4, 2, 8, LANES), vmem(4, 8, LANES)],
    )(*extend_wide(field, lo, hi))
    narrow = extend_narrow(next1)
    line = spread(tile, ("gz",), sizes)
    tiles = line.reshape(4, 2, 2, 4, LANES).transpose(0, 2, 1, 3, 4).reshape(8, 8, LANES)
    mine = spread(tiles, ("xc", "gy"), sizes).reshape(-1, 8, LANES)
    other = lax.ppermute(mine, "co", [(0, 1), (1, 0)])
    place = jnp.stack([lax.axis_index(axis_of("gx")), lax.axis_index("gy"), lax.axis_index("gz")]).astype(jnp.int32)
    window = call(
        coarse,
        shape(2, 12, 16, LANES),
        [vmem(2, 18, 32, LANES)]
        + rb_scratch(16, 32, 5)[:-1]
        + [vmem(2, 18, 32, LANES), vmem(2, 8, 32, LANES), vmem(8, 32, LANES)]
        + full_scratch(16, 1)
        + [vmem(2, 8, 16, LANES), vmem(8, 16, LANES)]
        + full_scratch(8, 1)[:-1],
        smem=1,
        cost=10,
    )(place, mine, other)
    return call(
        ascend,
        (shape(16, 16, LANES), shape(16, 16, LANES)),
        rb_scratch(X0, Z0, 4)
        + [vmem(14, Z0, LANES)]
        + level_scratch(X1, Z1)[1:]
        + [vmem(12, 16, LANES), vmem(12, Z1, LANES)],
    )(top, s1, *narrow, window)


def solution(mesh):
    names, dims = list(mesh.axis_names), list(mesh.devices.shape)
    at = names.index("gx")
    fine = jax.sharding.Mesh(
        mesh.devices.reshape(dims[:at] + [dims[at] // 2, 2] + dims[at + 1 :]),
        names[:at] + ["xc", "co"] + names[at + 1 :],
    )
    placed = P(("xc", "co"), "gz", "gy")
    return jax.shard_map(
        functools.partial(on_device, dict(fine.shape)),
        mesh=fine,
        in_specs=(placed, placed),
        out_specs=(placed, placed),
        check_vma=False,
    )
```

time: 113 us -> 102 us (0.903)
  Pallas kernels: 30.7 us -> 21.5 us
  waiting for transfers between devices: 36.1 us -> 33.1 us
    pallas_call x4, Pallas kernels: 30.7 us -> 21.5 us  [run(): pl.pallas_call(kernel, out_shape=out_shape, in_specs=specs, out_specs=jax...]
    all_to_all x2, starting transfers between devices: 17.8 us -> 14.5 us  [spread(): return lax.all_to_all(jnp.broadcast_to(x[None], (n,) + x.shape), axes, 0, 0)]
    ppermute x6, starting transfers between devices: 7.85 us -> 10.4 us  [swap(): b = lax.ppermute(jnp.where(even, low, high), axis, second)]
    ppermute x6, waiting for transfers between devices: 14.2 us -> 12.6 us  [swap(): b = lax.ppermute(jnp.where(even, low, high), axis, second)]
where the time goes in v3:
time: 102 us; the launch traced here: 101 us
  starting transfers between devices  41.1 us (40%)
  waiting for transfers between devices  33.1 us (32%)
  Pallas kernels  21.5 us (21%)
  local copies, waits for them, and re-layouts  3.71 us (4%)
  between operations  1.13 us (1%)
    pallas_call x4, Pallas kernels, run(): pl.pallas_call(kernel, out_shape=out_shape, in_specs=specs, out_specs=jax...  21.5 us
    all_to_all x2, starting transfers between devices, spread(): return lax.all_to_all(jnp.broadcast_to(x[None], (n,) + x.shape), axes, 0, 0)  14.5 us
    ppermute x6, starting transfers between devices, swap(): a = lax.ppermute(jnp.where(even, high, low), axis, first)  12.9 us
    ppermute x6, waiting for transfers between devices, swap(): b = lax.ppermute(jnp.where(even, low, high), axis, second)  12.6 us
    all_to_all x2, waiting for transfers between devices, spread(): return lax.all_to_all(jnp.broadcast_to(x[None], (n,) + x.shape), axes, 0, 0)  12 us
    ppermute x6, starting transfers between devices, swap(): b = lax.ppermute(jnp.where(even, low, high), axis, second)  10.4 us
    ppermute x6, waiting for transfers between devices, swap(): a = lax.ppermute(jnp.where(even, high, low), axis, first)  8.54 us
    ppermute x1, starting transfers between devices, on_device(): other = lax.ppermute(mine, 'co', [(0, 1), (1, 0)])  3.33 us
  transfers between devices with their start and end apart: 15, of which 7 were waited for; matrix products, arithmetic and copies ran while one was open for 1% of the time, Pallas kernels for 0%

profile of v3, /device:TPU:1, one launch (start us, length us, event | category | flops | bytes accessed | tf_op | source)
XLA Modules:
  0.0 101.2 jit_solution(14235251564007988338)
XLA Ops:
  0.6 0.0 copy-start
  0.7 0.9 copy-done
  1.5 0.0 copy-start.1
  1.6 0.9 copy-done.1
  2.5 0.5 shard_map.41
  3.0 2.1 %collective-permute-start = (f32[4,2,16,128]{3,2,1,0:T(8,128)S(1)}, f32[4,2,16,128]{3,2,1,0:T(8,128)S(1)}, u32[]{:S(2)}, u32[]{:S(2)}) collective-permute-start(f32[4,2,16,128]{3,2,1,0:T(8,128)S(1)} %get-tuple-element.46), channel_id=1, source_target_pairs={{0,8},{8,0},{16,24},{24,16},{1,9},{9,1},{17,25},{25,17},{2,10},{10... | collective-permute-start | bytes 196616 | tf_op jit(solution)/shard_map/ppermute | solution.py:564
  5.1 0.7 collective-permute-start.1
  5.8 1.0 collective-permute-done
  6.7 0.0 collective-permute-done.1
  6.8 0.7 collective-permute-start.2
  7.5 4.8 %collective-permute-start.3 = (f32[80,8,128]{2,1,0:T(8,128)S(1)}, f32[80,8,128]{2,1,0:T(8,128)S(1)}, u32[]{:S(2)}, u32[]{:S(2)}) collective-permute-start(f32[80,8,128]{2,1,0:T(8,128)S(1)} %pad_maximum_fusion.1), channel_id=1, source_target_pairs={{0,1},{1,0},{2,3},{3,2},{4,5},{5,4},{6,7},{7,6},{8,9},{9,8},{10,11... | collective-permute-start | bytes 983048 | tf_op jit(solution)/shard_map/ppermute | solution.py:564
  12.3 0.0 collective-permute-done.2
  12.3 5.9 %collective-permute-done.3 = f32[80,8,128]{2,1,0:T(8,128)S(1)} collective-permute-done((f32[80,8,128]{2,1,0:T(8,128)S(1)}, f32[80,8,128]{2,1,0:T(8,128)S(1)}, u32[]{:S(2)}, u32[]{:S(2)}) %collective-permute-start.3) | collective-permute-done | bytes 327712 | tf_op jit(solution)/shard_map/ppermute | solution.py:564
  18.3 0.1 pad_maximum_fusion.e
  18.4 0.1 slice_bitcast_fusion
  18.9 0.1 broadcast_select_fusion.2
  19.0 5.8 %collective-permute-start.4 = (f32[160,8,128]{2,1,0:T(8,128)S(1)}, f32[160,8,128]{2,1,0:T(8,128)S(1)}, u32[]{:S(2)}, u32[]{:S(2)}) collective-permute-start(f32[160,8,128]{2,1,0:T(8,128)S(1)} %get-tuple-element.19), channel_id=1, source_target_pairs={{32,64},{96,128},{160,192},{64,32},{128,96},{192,160},{33,65},{97,... | collective-permute-start | bytes 1966088 | tf_op jit(solution)/shard_map/ppermute | solution.py:565
  24.8 0.1 collective-permute-start.5
  24.9 8.1 %collective-permute-done.4 = f32[160,8,128]{2,1,0:T(8,128)S(1)} collective-permute-done((f32[160,8,128]{2,1,0:T(8,128)S(1)}, f32[160,8,128]{2,1,0:T(8,128)S(1)}, u32[]{:S(2)}, u32[]{:S(2)}) %collective-permute-start.4) | collective-permute-done | bytes 655392 | tf_op jit(solution)/shard_map/ppermute | solution.py:565
  33.1 0.0 collective-permute-done.5
  33.1 0.1 broadcast_select_fusion
  33.4 8.9 %shard_map.42 = (f32[5,26,32,128]{3,2,1,0:T(8,128)S(1)}, f32[22,24,128]{2,1,0:T(8,128)S(1)}, f32[8,8,128]{2,1,0:T(8,128)S(1)}, f32[8,128]{1,0:T(8,128)S(1)}) custom-call(f32[2,16,48,128]{3,2,1,0:T(8,128)S(1)} %pad_maximum_fusion.e, f32[4,2,48,128]{3,2,1,0:T(8,128)S(1)} %pad_maximum_fusion.2.b, f32[5,48,128]{2,1,0:T(8,128)S(1)} %bitcast.52, ...), custom_call_target="tpu_custom_call" | custom-call | flops 4000000 | bytes 12000000 | tf_op jit(solution)/shard_map/pallas_call | solution.py:280
  42.3 3.8 %collective-permute-start.6 = (f32[8,8,128]{2,1,0:T(8,128)S(1)}, f32[8,8,128]{2,1,0:T(8,128)S(1)}, u32[]{:S(2)}, u32[]{:S(2)}) collective-permute-start(f32[8,8,128]{2,1,0:T(8,128)S(1)} %get-tuple-element.14), channel_id=1, source_target_pairs={{0,8},{8,0},{16,24},{24,16},{1,9},{9,1},{17,25},{25,17},{2,10},{10... | collective-permute-start | bytes 98312 | tf_op jit(solution)/shard_map/ppermute | solution.py:564
  46.1 0.7 collective-permute-start.7
  46.7 0.6 broadcast_in_dim.6
  47.4 7.5 %all-to-all-start = ((f32[8,8,128]{2,1,0:T(8,128)}), f32[8,8,128]{2,1,0:T(8,128)S(1)}, u32[]{:S(2)}, u32[]{:S(2)}) async-start(f32[8,8,128]{2,1,0:T(8,128)} %broadcast_in_dim.6), calls=%async_computation | async-start | bytes 65536 | tf_op jit(solution)/shard_map/all_to_all | solution.py:616
  54.8 0.0 collective-permute-done.6
  54.8 0.0 collective-permute-done.7
  54.9 6.8 %all-to-all-done = f32[8,8,128]{2,1,0:T(8,128)S(1)} async-done(((f32[8,8,128]{2,1,0:T(8,128)}), f32[8,8,128]{2,1,0:T(8,128)S(1)}, u32[]{:S(2)}, u32[]{:S(2)}) %all-to-all-start) | async-done | bytes 32800 | tf_op jit(solution)/shard_map/all_to_all | solution.py:616
  61.7 0.8 broadcast_in_dim.15
  62.6 7.0 %all-to-all-start.1 = ((f32[16,8,8,128]{3,2,1,0:T(8,128)}), f32[16,8,8,128]{3,2,1,0:T(8,128)S(1)}, u32[]{:S(2)}, u32[]{:S(2)}) async-start(f32[16,8,8,128]{3,2,1,0:T(8,128)} %broadcast_in_dim.15), calls=%async_computation.1 | async-start | bytes 1048576 | tf_op jit(solution)/shard_map/all_to_all | solution.py:616
  69.6 0.7 collective-permute-start.8
  70.3 1.8 %collective-permute-start.9 = (f32[2,8,8,128]{3,2,1,0:T(8,128)S(1)}, f32[2,8,8,128]{3,2,1,0:T(8,128)S(1)}, u32[]{:S(2)}, u32[]{:S(2)}) collective-permute-start(f32[2,8,8,128]{3,2,1,0:T(8,128)S(1)} %pad_maximum_fusion.4), channel_id=1, source_target_pairs={{0,1},{1,0},{2,3},{3,2},{4,5},{5,4},{6,7},{7,6},{8,9},{9,8},{10,11... | collective-permute-start | bytes 196616 | tf_op jit(solution)/shard_map/ppermute | solution.py:564
  72.1 0.0 collective-permute-done.8
  72.1 1.7 %collective-permute-done.9 = f32[2,8,8,128]{3,2,1,0:T(8,128)S(1)} collective-permute-done((f32[2,8,8,128]{3,2,1,0:T(8,128)S(1)}, f32[2,8,8,128]{3,2,1,0:T(8,128)S(1)}, u32[]{:S(2)}, u32[]{:S(2)}) %collective-permute-start.9) | collective-permute-done | bytes 65568 | tf_op jit(solution)/shard_map/ppermute | solution.py:564
  73.8 5.2 %all-to-all-done.1 = f32[16,8,8,128]{3,2,1,0:T(8,128)S(1)} async-done(((f32[16,8,8,128]{3,2,1,0:T(8,128)}), f32[16,8,8,128]{3,2,1,0:T(8,128)S(1)}, u32[]{:S(2)}, u32[]{:S(2)}) %all-to-all-start.1) | async-done | bytes 524320 | tf_op jit(solution)/shard_map/all_to_all | solution.py:616
  78.9 3.3 %collective-permute-start.12 = (f32[128,8,128]{2,1,0:T(8,128)S(1)}, f32[128,8,128]{2,1,0:T(8,128)S(1)}, u32[]{:S(2)}, u32[]{:S(2)}) collective-permute-start(f32[128,8,128]{2,1,0:T(8,128)S(1)} %bitcast.45), channel_id=1, source_target_pairs={{0,32},{32,0},{1,33},{33,1},{2,34},{34,2},{3,35},{35,3},{4,36},{36... | collective-permute-start | bytes 1572872 | tf_op jit(solution)/shard_map/ppermute | solution.py:652
  82.3 1.9 %collective-permute-start.10 = (f32[2,7,24,128]{3,2,1,0:T(8,128)S(1)}, f32[2,7,24,128]{3,2,1,0:T(8,128)S(1)}, u32[]{:S(2)}, u32[]{:S(2)}) collective-permute-start(f32[2,7,24,128]{3,2,1,0:T(8,128)S(1)} %get-tuple-element.39), channel_id=1, source_target_pairs={{32,64},{96,128},{160,192},{64,32},{128,96},{192,160},{33,65},{97,... | collective-permute-start | bytes 516104 | tf_op jit(solution)/shard_map/ppermute | solution.py:565
  84.2 0.3 collective-permute-start.11
  84.5 0.1 pad_add_fusion.where_ref
  84.6 4.4 %collective-permute-done.10 = f32[2,7,24,128]{3,2,1,0:T(8,128)S(1)} collective-permute-done((f32[2,7,24,128]{3,2,1,0:T(8,128)S(1)}, f32[2,7,24,128]{3,2,1,0:T(8,128)S(1)}, u32[]{:S(2)}, u32[]{:S(2)}) %collective-permute-start.10) | collective-permute-done | bytes 172064 | tf_op jit(solution)/shard_map/ppermute | solution.py:565
  89.0 0.0 collective-permute-done.11
  89.1 0.0 collective-permute-done.12.other_ref
  89.1 6.7 %shard_map.43.win = f32[2,12,16,128]{3,2,1,0:T(8,128)S(1)} custom-call(s32[3]{0:T(128)S(1)} %pad_add_fusion.where_ref, f32[128,8,128]{2,1,0:T(8,128)S(1)} %bitcast.46, f32[128,8,128]{2,1,0:T(8,128)S(1)} %collective-permute-done.12.other_ref), custom_call_target="tpu_custom_call" | custom-call | flops 10000000 | bytes 30000000 | tf_op jit(solution)/shard_map/pallas_call | solution.py:280
  95.7 5.5 %shard_map.44 = (f32[16,16,128]{2,1,0:T(8,128)}, f32[16,16,128]{2,1,0:T(8,128)}) custom-call(f32[5,26,32,128]{3,2,1,0:T(8,128)S(1)} %get-tuple-element.12.top, f32[22,24,128]{2,1,0:T(8,128)S(1)} %get-tuple-element.13.sl, f32[2,8,24,128]{3,2,1,0:T(8,128)S(1)} %pad_maximum_fusion.3.m, f32[2,7,24,128]{3,2,1,0:T(8,128)S(1)} %get-tuple-element.37.ml, ...), custom_call_target="tpu_custom_call" | custom-call | flops 4000000 | bytes 12000000 | tf_op jit(solution)/shard_map/pallas_call | solution.py:280
  (48 shorter events, 0.6 us)
Async XLA Ops:
  0.6 0.9 copy-start
  1.5 0.9 copy-start.1
  3.0 3.8 %collective-permute-start = (f32[4,2,16,128]{3,2,1,0:T(8,128)S(1)}, f32[4,2,16,128]{3,2,1,0:T(8,128)S(1)}, u32[]{:S(2)}, u32[]{:S(2)}) collective-permute-start(f32[4,2,16,128]{3,2,1,0:T(8,128)S(1)} %get-tuple-element.46), channel_id=1, source_target_pairs={{0,8},{8,0},{16,24},{24,16},{1,9},{9,1},{17,25},{25,17},{2,10},{10... | collective-permute-start | bytes 196616 | tf_op jit(solution)/shard_map/ppermute | solution.py:564
  5.1 1.7 %collective-permute-start.1 = (f32[4,2,16,128]{3,2,1,0:T(8,128)S(1)}, f32[4,2,16,128]{3,2,1,0:T(8,128)S(1)}, u32[]{:S(2)}, u32[]{:S(2)}) collective-permute-start(f32[4,2,16,128]{3,2,1,0:T(8,128)S(1)} %get-tuple-element.47), channel_id=1, source_target_pairs={{8,16},{16,8},{9,17},{17,9},{10,18},{18,10},{11,19},{19,11},{12,20... | collective-permute-start | bytes 196616 | tf_op jit(solution)/shard_map/ppermute | solution.py:565
  6.8 5.5 %collective-permute-start.2 = (f32[80,8,128]{2,1,0:T(8,128)S(1)}, f32[80,8,128]{2,1,0:T(8,128)S(1)}, u32[]{:S(2)}, u32[]{:S(2)}) collective-permute-start(f32[80,8,128]{2,1,0:T(8,128)S(1)} %pad_maximum_fusion.1), channel_id=1, source_target_pairs={{1,2},{3,4},{5,6},{2,1},{4,3},{6,5},{9,10},{11,12},{13,14},{10,9},... | collective-permute-start | bytes 983048 | tf_op jit(solution)/shard_map/ppermute | solution.py:565
  7.5 10.8 %collective-permute-start.3 = (f32[80,8,128]{2,1,0:T(8,128)S(1)}, f32[80,8,128]{2,1,0:T(8,128)S(1)}, u32[]{:S(2)}, u32[]{:S(2)}) collective-permute-start(f32[80,8,128]{2,1,0:T(8,128)S(1)} %pad_maximum_fusion.1), channel_id=1, source_target_pairs={{0,1},{1,0},{2,3},{3,2},{4,5},{5,4},{6,7},{7,6},{8,9},{9,8},{10,11... | collective-permute-start | bytes 983048 | tf_op jit(solution)/shard_map/ppermute | solution.py:564
  19.0 14.1 %collective-permute-start.4 = (f32[160,8,128]{2,1,0:T(8,128)S(1)}, f32[160,8,128]{2,1,0:T(8,128)S(1)}, u32[]{:S(2)}, u32[]{:S(2)}) collective-permute-start(f32[160,8,128]{2,1,0:T(8,128)S(1)} %get-tuple-element.19), channel_id=1, source_target_pairs={{32,64},{96,128},{160,192},{64,32},{128,96},{192,160},{33,65},{97,... | collective-permute-start | bytes 1966088 | tf_op jit(solution)/shard_map/ppermute | solution.py:565
  24.8 8.3 %collective-permute-start.5 = (f32[160,8,128]{2,1,0:T(8,128)S(1)}, f32[160,8,128]{2,1,0:T(8,128)S(1)}, u32[]{:S(2)}, u32[]{:S(2)}) collective-permute-start(f32[160,8,128]{2,1,0:T(8,128)S(1)} %get-tuple-element.18), channel_id=1, source_target_pairs={{0,32},{32,0},{64,96},{96,64},{128,160},{160,128},{192,224},{224,1... | collective-permute-start | bytes 1966088 | tf_op jit(solution)/shard_map/ppermute | solution.py:564
  42.3 12.5 %collective-permute-start.6 = (f32[8,8,128]{2,1,0:T(8,128)S(1)}, f32[8,8,128]{2,1,0:T(8,128)S(1)}, u32[]{:S(2)}, u32[]{:S(2)}) collective-permute-start(f32[8,8,128]{2,1,0:T(8,128)S(1)} %get-tuple-element.14), channel_id=1, source_target_pairs={{0,8},{8,0},{16,24},{24,16},{1,9},{9,1},{17,25},{25,17},{2,10},{10... | collective-permute-start | bytes 98312 | tf_op jit(solution)/shard_map/ppermute | solution.py:564
  46.1 8.8 %collective-permute-start.7 = (f32[8,8,128]{2,1,0:T(8,128)S(1)}, f32[8,8,128]{2,1,0:T(8,128)S(1)}, u32[]{:S(2)}, u32[]{:S(2)}) collective-permute-start(f32[8,8,128]{2,1,0:T(8,128)S(1)} %get-tuple-element.14), channel_id=1, source_target_pairs={{8,16},{16,8},{9,17},{17,9},{10,18},{18,10},{11,19},{19,11},{12,20... | collective-permute-start | bytes 98312 | tf_op jit(solution)/shard_map/ppermute | solution.py:565
  47.4 14.4 %all-to-all-start = ((f32[8,8,128]{2,1,0:T(8,128)}), f32[8,8,128]{2,1,0:T(8,128)S(1)}, u32[]{:S(2)}, u32[]{:S(2)}) async-start(f32[8,8,128]{2,1,0:T(8,128)} %broadcast_in_dim.6), calls=%async_computation | async-start | bytes 65536 | tf_op jit(solution)/shard_map/all_to_all | solution.py:616
  62.6 16.4 %all-to-all-start.1 = ((f32[16,8,8,128]{3,2,1,0:T(8,128)}), f32[16,8,8,128]{3,2,1,0:T(8,128)S(1)}, u32[]{:S(2)}, u32[]{:S(2)}) async-start(f32[16,8,8,128]{3,2,1,0:T(8,128)} %broadcast_in_dim.15), calls=%async_computation.1 | async-start | bytes 1048576 | tf_op jit(solution)/shard_map/all_to_all | solution.py:616
  69.6 2.4 %collective-permute-start.8 = (f32[2,8,8,128]{3,2,1,0:T(8,128)S(1)}, f32[2,8,8,128]{3,2,1,0:T(8,128)S(1)}, u32[]{:S(2)}, u32[]{:S(2)}) collective-permute-start(f32[2,8,8,128]{3,2,1,0:T(8,128)S(1)} %pad_maximum_fusion.4), channel_id=1, source_target_pairs={{1,2},{3,4},{5,6},{2,1},{4,3},{6,5},{9,10},{11,12},{13,14},{10,9},... | collective-permute-start | bytes 196616 | tf_op jit(solution)/shard_map/ppermute | solution.py:565
  70.3 3.4 %collective-permute-start.9 = (f32[2,8,8,128]{3,2,1,0:T(8,128)S(1)}, f32[2,8,8,128]{3,2,1,0:T(8,128)S(1)}, u32[]{:S(2)}, u32[]{:S(2)}) collective-permute-start(f32[2,8,8,128]{3,2,1,0:T(8,128)S(1)} %pad_maximum_fusion.4), channel_id=1, source_target_pairs={{0,1},{1,0},{2,3},{3,2},{4,5},{5,4},{6,7},{7,6},{8,9},{9,8},{10,11... | collective-permute-start | bytes 196616 | tf_op jit(solution)/shard_map/ppermute | solution.py:564
  78.9 10.1 %collective-permute-start.12 = (f32[128,8,128]{2,1,0:T(8,128)S(1)}, f32[128,8,128]{2,1,0:T(8,128)S(1)}, u32[]{:S(2)}, u32[]{:S(2)}) collective-permute-start(f32[128,8,128]{2,1,0:T(8,128)S(1)} %bitcast.45), channel_id=1, source_target_pairs={{0,32},{32,0},{1,33},{33,1},{2,34},{34,2},{3,35},{35,3},{4,36},{36... | collective-permute-start | bytes 1572872 | tf_op jit(solution)/shard_map/ppermute | solution.py:652
  82.3 6.7 %collective-permute-start.10 = (f32[2,7,24,128]{3,2,1,0:T(8,128)S(1)}, f32[2,7,24,128]{3,2,1,0:T(8,128)S(1)}, u32[]{:S(2)}, u32[]{:S(2)}) collective-permute-start(f32[2,7,24,128]{3,2,1,0:T(8,128)S(1)} %get-tuple-element.39), channel_id=1, source_target_pairs={{32,64},{96,128},{160,192},{64,32},{128,96},{192,160},{33,65},{97,... | collective-permute-start | bytes 516104 | tf_op jit(solution)/shard_map/ppermute | solution.py:565
  84.2 4.8 %collective-permute-start.11 = (f32[2,7,24,128]{3,2,1,0:T(8,128)S(1)}, f32[2,7,24,128]{3,2,1,0:T(8,128)S(1)}, u32[]{:S(2)}, u32[]{:S(2)}) collective-permute-start(f32[2,7,24,128]{3,2,1,0:T(8,128)S(1)} %get-tuple-element.38), channel_id=1, source_target_pairs={{0,32},{32,0},{64,96},{96,64},{128,160},{160,128},{192,224},{224,1... | collective-permute-start | bytes 516104 | tf_op jit(solution)/shard_map/ppermute | solution.py:564

commit v4 on v3

--- a/solution.py
+++ b/solution.py
@@ -26,10 +26,6 @@
 
 def iota(shape, axis):
     return lax.broadcasted_iota(jnp.int32, shape, axis)
-
-
-def exact_dot(a, b):
-    return jnp.dot(a, b, precision=lax.Precision.HIGHEST, preferred_element_type=F32)
 
 
 def reds(shape, parity):
@@ -204,17 +200,21 @@
     return out
 
 
+def picked(v, matrix):
+    matrix = matrix.astype(jnp.bfloat16)
+    first = v.astype(jnp.bfloat16)
+    rest = v - first.astype(F32)
+    second = rest.astype(jnp.bfloat16)
+    third = (rest - second.astype(F32)).astype(jnp.bfloat16)
+    parts = [jnp.dot(x, matrix, preferred_element_type=F32) for x in (first, second, third)]
+    return (parts[0] + parts[1]) + parts[2]
+
+
 def permuted(v, back):
     k, l = iota((LANES, LANES), 0), iota((LANES, LANES), 1)
     if back:
         k, l = l, k
-    move = jnp.where(k == jnp.where(l < HALF, 2 * l, 2 * (l - HALF) + 1), 1.0, 0.0).astype(jnp.bfloat16)
-    first = v.astype(jnp.bfloat16)
-    rest = v - first.astype(F32)
-    second = rest.astype(jnp.bfloat16)
-    third = (rest - second.astype(F32)).astype(jnp.bfloat16)
-    parts = [jnp.dot(x, move, preferred_element_type=F32) for x in (first, second, third)]
-    return (parts[0] + parts[1]) + parts[2]
+    return picked(v, jnp.where(k == jnp.where(l < HALF, 2 * l, 2 * (l - HALF) + 1), 1.0, 0.0))
 
 
 def swapped_rows(v, parity):
@@ -264,11 +264,11 @@
         chunk(jnp.int32(count - count % step), count % step)
 
 
-def fill_narrow(u, f, own, low, high):
+def fill_narrow(u, f, even, own, first, second):
     lane = iota((Z1, LANES), 1)
-    for part, at, count in ((low, 0, H1), (own, H1, 8), (high, H1 + 8, H1)):
+    for parts, at, count in (((second, first), 0, H1), ((own, own), H1, 8), ((first, second), H1 + 8, H1)):
         for k in range(count):
-            v, h = part[0, k], part[1, k]
+            v, h = [parts[0][i, k] if count == 8 else jnp.where(even, parts[0][i, k], parts[1][i, k]) for i in range(2)]
             u[at + k] = jnp.where(lane < HALF, v, roll(h, HALF, 1))
             f[at + k] = jnp.where(lane < HALF, roll(v, HALF, 1), h)
 
@@ -294,9 +294,9 @@
     return pltpu.VMEM(shape, F32)
 
 
-def packing(f_ref, s_ref, out_ref, lo_ref, hi_ref):
-    for i, ref in enumerate((f_ref, s_ref)):
-        out_ref[i] = permuted(ref[...].reshape(256, LANES), False).reshape(16, 16, LANES)
+def packing(in_ref, out_ref, lo_ref, hi_ref):
+    for i in range(2):
+        out_ref[i] = permuted(in_ref[i].reshape(256, LANES), False).reshape(16, 16, LANES)
         planes = [swapped_rows(out_ref[i, x], x) for x in range(16)]
         for x in range(16):
             out_ref[i, x] = planes[x]
@@ -358,8 +358,6 @@
     half_sweep(ul, cl, gl, 4, X1 - 4, H1 + 1, step=14)
     half_sweep(ul, cl, gl, 5, X1 - 5, H1, step=12)
     half_sweep(ul, cl, gl, 6, X1 - 6, H1 + 1, step=10)
-    k, l = iota((LANES, LANES), 0), iota((LANES, LANES), 1)
-    total = jnp.zeros((8, LANES), F32)
     r = residual_planes(ul, cl, gl, wl, H1, 8)
     own = iota((8, LANES), 1) < HALF
     for x in range(8):
@@ -370,9 +368,11 @@
         ql[i, 1] = sl[x, 8:16] + sl[x + 1, 8:16]
         for b in range(2):
             t[i, 4 * b : 4 * b + 4] = ql[i, b, pl.ds(0, 4, stride=2), :] + ql[i, b, pl.ds(1, 4, stride=2), :]
-        to = 32 * i + 16 * ((k // 2) % 2) + k // 4
-        place = jnp.where(jnp.logical_and(k < HALF, l == to), 0.125, 0.0).astype(F32)
-        total = total + exact_dot(t[i], place)
+    k, l = iota((4 * LANES, LANES), 0), iota((4 * LANES, LANES), 1)
+    cell = (k & (LANES - 1)) >> 1
+    to = 32 * (k >> 7) + 16 * (cell & 1) + (cell >> 1)
+    place = jnp.where(jnp.logical_and((k & HALF) == 0, l == to), 0.125, 0.0)
+    total = picked(jnp.concatenate([t[i] for i in range(4)], 1), place)
     group = iota((8, LANES), 1) // 16
     other = jnp.where(group % 2 == 0, roll(total, -16, 1), roll(total, 16, 1))
     tile_out[...] = jnp.where((group // 2 + iota((8, LANES), 0)) % 2 == 0, total, other)
@@ -504,16 +504,16 @@
             out_ref[col, n] = pltpu.roll(v[:16], shift, 1)
 
 
-def ascend(top, sl, m, ml, mh, win, u_out, r_out, c, g, w, u, d0, fl, cl, gl, wl, ul, t1, d1):
-    fill_narrow(ul, fl, m, ml, mh)
+def ascend(where_ref, top, sl, m, ma, mb, win, u_out, r_out, c, g, w, u, d0, fl, cl, gl, wl, ul, t1, d1):
+    fill_narrow(ul, fl, lax.rem(where_ref[0], 2) == 0, m, ma, mb)
     couplings(sl, fl, cl, gl, wl, 1, X1 - 1, 4.0, step=4)
-    k, l = iota((LANES, LANES), 0), iota((LANES, LANES), 1)
-    from_lane = jnp.where(l < 96, l // 4, 96 + l // 4)
+    k, l = iota((2 * LANES, LANES), 0), iota((2 * LANES, LANES), 1)
+    from_lane = jnp.where(l < 96, l >> 2, 96 + (l >> 2))
+    widen = jnp.where(k == from_lane + LANES * ((l >> 1) & 1), 1.0, 0.0)
     parity = iota((1, 16, LANES), 1) + iota((12, 16, LANES), 0)
     v = [win[0], win[1]]
-    both = [jnp.where(parity % 2 == 0, v[i], v[1 - i]).reshape(192, LANES) for i in range(2)]
-    widen = [jnp.where(jnp.logical_and(k == from_lane, (l // 2) % 2 == i), 1.0, 0.0).astype(F32) for i in range(2)]
-    t1[...] = (exact_dot(both[0], widen[0]) + exact_dot(both[1], widen[1])).reshape(12, 16, LANES)
+    both = [jnp.where((parity & 1) == 0, v[i], v[1 - i]).reshape(192, LANES) for i in range(2)]
+    t1[...] = picked(jnp.concatenate(both, 1), widen).reshape(12, 16, LANES)
     d1[:, pl.ds(0, 12, stride=2), :] = t1[:, :12]
     d1[:, pl.ds(1, 12, stride=2), :] = t1[:, :12]
     for x in range(X1):
@@ -554,7 +554,7 @@
     return ("xc", "co") if name == "gx" else name
 
 
-def swap(low, high, name):
+def exchange(low, high, name):
     axis = axis_of(name)
     count = lax.axis_size(axis)
     even = lax.axis_index(axis) % 2 == 0
@@ -563,6 +563,12 @@
     second += [(j, i) for i, j in second]
     a = lax.ppermute(jnp.where(even, high, low), axis, first)
     b = lax.ppermute(jnp.where(even, low, high), axis, second)
+    return a, b
+
+
+def swap(low, high, name):
+    even = lax.axis_index(axis_of(name)) % 2 == 0
+    a, b = exchange(low, high, name)
     return jnp.where(even, b, a), jnp.where(even, a, b)
 
 
@@ -605,8 +611,7 @@
     own = jnp.stack([own, jnp.where(lane % HALF < HALF // 2, above, below)])
     low, high = swap(own, own, "gz")
     own = jnp.concatenate([low, own, high], 2)
-    low, high = swap(own[:, :H1], own[:, -H1:], "gx")
-    return own, low, high
+    return (own,) + exchange(own[:, :H1], own[:, -H1:], "gx")
 
 
 def spread(x, axes, sizes):
@@ -636,7 +641,7 @@
 
 
 def on_device(sizes, right_side, sigma):
-    field, lo, hi = call(packing, [shape(2, 16, 16, LANES), shape(4, 2, 16, LANES), shape(4, 2, 16, LANES)], [])(right_side, sigma)
+    field, lo, hi = call(packing, [shape(2, 16, 16, LANES), shape(4, 2, 16, LANES), shape(4, 2, 16, LANES)], [])(jnp.stack([right_side, sigma]))
     top, s1, next1, tile = call(
         descend,
         [shape(5, X0, Z0, LANES), shape(X1, Z1, LANES), shape(8, 8, LANES), shape(8, LANES)],
@@ -646,9 +651,8 @@
         + [vmem(4, 2, 8, LANES), vmem(4, 8, LANES)],
     )(*extend_wide(field, lo, hi))
     narrow = extend_narrow(next1)
-    line = spread(tile, ("gz",), sizes)
-    tiles = line.reshape(4, 2, 2, 4, LANES).transpose(0, 2, 1, 3, 4).reshape(8, 8, LANES)
-    mine = spread(tiles, ("xc", "gy"), sizes).reshape(-1, 8, LANES)
+    tiles = spread(tile, ("xc", "gy", "gz"), sizes)
+    mine = tiles.reshape(-1, 4, 2, 2, 4, LANES).transpose(0, 1, 3, 2, 4, 5).reshape(-1, 8, LANES)
     other = lax.ppermute(mine, "co", [(0, 1), (1, 0)])
     place = jnp.stack([lax.axis_index(axis_of("gx")), lax.axis_index("gy"), lax.axis_index("gz")]).astype(jnp.int32)
     window = call(
@@ -670,7 +674,8 @@
         + [vmem(14, Z0, LANES)]
         + level_scratch(X1, Z1)[1:]
         + [vmem(12, 16, LANES), vmem(12, Z1, LANES)],
-    )(top, s1, *narrow, window)
+        smem=1,
+    )(place, top, s1, *narrow, window)
 
 
 def solution(mesh):

time: 102 us -> 97.3 us (0.954)
  waiting for transfers between devices: 33.1 us -> 28.1 us
  local copies, waits for them, and re-layouts: 3.71 us -> 1.39 us
  starting transfers between devices: 41.1 us -> 43 us
    all_to_all x2 -> x1, waiting for transfers between devices: 12 us -> 6.68 us  [spread(): return lax.all_to_all(jnp.broadcast_to(x[None], (n,) + x.shape), axes, 0, 0)]
    ppermute x12, starting transfers between devices: 23.3 us -> 26.6 us  [the longest x6 18.7 us: exchange(): a = lax.ppermute(jnp.where(even, high, low), axis, first)]
    unnamed x14 -> x10, local copies, waits for them, and re-layouts: 1.9 us -> 0.1 us
    all_to_all x2 -> x1, starting transfers between devices: 14.5 us -> 14.1 us  [spread(): return lax.all_to_all(jnp.broadcast_to(x[None], (n,) + x.shape), axes, 0, 0)]
  transfers between devices with their start and end apart: 15 -> 14, of which waited for: 7 -> 6; matrix products, arithmetic and copies ran while one was open for 1% -> 0% of each run, Pallas kernels for 0% -> 7%
where the time goes in v4:
time: 97.3 us; the launch traced here: 97 us
  starting transfers between devices  43 us (44%)
  waiting for transfers between devices  28.1 us (29%)
  Pallas kernels  21.8 us (22%)
  other arithmetic  1.5 us (2%)
  local copies, waits for them, and re-layouts  1.39 us (1%)
  between operations  1.11 us (1%)
    pallas_call x4, Pallas kernels, run(): pl.pallas_call(kernel, out_shape=out_shape, in_specs=specs, out_specs=jax...  21.8 us
    ppermute x6, starting transfers between devices, exchange(): a = lax.ppermute(jnp.where(even, high, low), axis, first)  18.7 us
    all_to_all x1, starting transfers between devices, spread(): return lax.all_to_all(jnp.broadcast_to(x[None], (n,) + x.shape), axes, 0, 0)  14.1 us
    ppermute x6, waiting for transfers between devices, exchange(): a = lax.ppermute(jnp.where(even, high, low), axis, first)  12.7 us
    ppermute x6, waiting for transfers between devices, exchange(): b = lax.ppermute(jnp.where(even, low, high), axis, second)  8.78 us
    ppermute x6, starting transfers between devices, exchange(): b = lax.ppermute(jnp.where(even, low, high), axis, second)  7.87 us
    all_to_all x1, waiting for transfers between devices, spread(): return lax.all_to_all(jnp.broadcast_to(x[None], (n,) + x.shape), axes, 0, 0)  6.68 us
    ppermute x1, starting transfers between devices, on_device(): other = lax.ppermute(mine, 'co', [(0, 1), (1, 0)])  2.34 us
  transfers between devices with their start and end apart: 14, of which 6 were waited for; matrix products, arithmetic and copies ran while one was open for 0% of the time, Pallas kernels for 7%

profile of v4, /device:TPU:1, one launch (start us, length us, event | category | flops | bytes accessed | tf_op | source)
XLA Modules:
  0.0 97.0 jit_solution(2724633238788327033)
XLA Ops:
  0.6 1.0 %pad_maximum_fusion.2.in_ref = f32[2,16,16,128]{3,2,1,0:T(8,128)S(1)} fusion(f32[1,16,16,128]{3,2,1,0:T(8,128)} %bitcast.81, f32[1,16,16,128]{3,2,1,0:T(8,128)} %bitcast.82), kind=kLoop, calls=%fused_computation.8 | loop fusion | flops 65536 | bytes 524288 | tf_op jit(solution)/shard_map/stack | solution.py:644
  1.6 0.5 shard_map.41
  2.1 0.7 collective-permute-start.1
  2.8 4.6 %collective-permute-start = (f32[4,2,16,128]{3,2,1,0:T(8,128)S(1)}, f32[4,2,16,128]{3,2,1,0:T(8,128)S(1)}, u32[]{:S(2)}, u32[]{:S(2)}) collective-permute-start(f32[4,2,16,128]{3,2,1,0:T(8,128)S(1)} %get-tuple-element.44), channel_id=1, source_target_pairs={{0,8},{8,0},{16,24},{24,16},{1,9},{9,1},{17,25},{25,17},{2,10},{10... | collective-permute-start | bytes 196616 | tf_op jit(solution)/shard_map/ppermute | solution.py:564
  7.4 0.0 collective-permute-done.1
  7.4 1.6 %collective-permute-done = f32[4,2,16,128]{3,2,1,0:T(8,128)S(1)} collective-permute-done((f32[4,2,16,128]{3,2,1,0:T(8,128)S(1)}, f32[4,2,16,128]{3,2,1,0:T(8,128)S(1)}, u32[]{:S(2)}, u32[]{:S(2)}) %collective-permute-start) | collective-permute-done | bytes 65568 | tf_op jit(solution)/shard_map/ppermute | solution.py:564
  9.1 0.7 collective-permute-start.2
  9.8 4.6 %collective-permute-start.3 = (f32[80,8,128]{2,1,0:T(8,128)S(1)}, f32[80,8,128]{2,1,0:T(8,128)S(1)}, u32[]{:S(2)}, u32[]{:S(2)}) collective-permute-start(f32[80,8,128]{2,1,0:T(8,128)S(1)} %pad_maximum_fusion.1), channel_id=1, source_target_pairs={{0,1},{1,0},{2,3},{3,2},{4,5},{5,4},{6,7},{7,6},{8,9},{9,8},{10,11... | collective-permute-start | bytes 983048 | tf_op jit(solution)/shard_map/ppermute | solution.py:564
  14.4 0.0 collective-permute-done.2
  14.4 5.9 %collective-permute-done.3 = f32[80,8,128]{2,1,0:T(8,128)S(1)} collective-permute-done((f32[80,8,128]{2,1,0:T(8,128)S(1)}, f32[80,8,128]{2,1,0:T(8,128)S(1)}, u32[]{:S(2)}, u32[]{:S(2)}) %collective-permute-start.3) | collective-permute-done | bytes 327712 | tf_op jit(solution)/shard_map/ppermute | solution.py:564
  20.4 0.1 pad_maximum_fusion.e
  20.5 0.1 slice_bitcast_fusion
  21.0 0.1 broadcast_select_fusion.2
  21.0 2.8 %collective-permute-start.5 = (f32[160,8,128]{2,1,0:T(8,128)S(1)}, f32[160,8,128]{2,1,0:T(8,128)S(1)}, u32[]{:S(2)}, u32[]{:S(2)}) collective-permute-start(f32[160,8,128]{2,1,0:T(8,128)S(1)} %get-tuple-element.18), channel_id=1, source_target_pairs={{0,32},{32,0},{64,96},{96,64},{128,160},{160,128},{192,224},{224,1... | collective-permute-start | bytes 1966088 | tf_op jit(solution)/shard_map/ppermute | solution.py:564
  23.9 3.1 %collective-permute-start.4 = (f32[160,8,128]{2,1,0:T(8,128)S(1)}, f32[160,8,128]{2,1,0:T(8,128)S(1)}, u32[]{:S(2)}, u32[]{:S(2)}) collective-permute-start(f32[160,8,128]{2,1,0:T(8,128)S(1)} %get-tuple-element.19), channel_id=1, source_target_pairs={{32,64},{96,128},{160,192},{64,32},{128,96},{192,160},{33,65},{97,... | collective-permute-start | bytes 1966088 | tf_op jit(solution)/shard_map/ppermute | solution.py:565
  27.0 0.0 collective-permute-done.5
  27.0 8.8 %collective-permute-done.4 = f32[160,8,128]{2,1,0:T(8,128)S(1)} collective-permute-done((f32[160,8,128]{2,1,0:T(8,128)S(1)}, f32[160,8,128]{2,1,0:T(8,128)S(1)}, u32[]{:S(2)}, u32[]{:S(2)}) %collective-permute-start.4) | collective-permute-done | bytes 655392 | tf_op jit(solution)/shard_map/ppermute | solution.py:565
  35.8 0.1 broadcast_select_fusion
  36.1 8.9 %shard_map.42 = (f32[5,26,32,128]{3,2,1,0:T(8,128)S(1)}, f32[22,24,128]{2,1,0:T(8,128)S(1)}, f32[8,8,128]{2,1,0:T(8,128)S(1)}, f32[8,128]{1,0:T(8,128)S(1)}) custom-call(f32[2,16,48,128]{3,2,1,0:T(8,128)S(1)} %pad_maximum_fusion.e, f32[4,2,48,128]{3,2,1,0:T(8,128)S(1)} %pad_maximum_fusion.3.b, f32[5,48,128]{2,1,0:T(8,128)S(1)} %bitcast.53, ...), custom_call_target="tpu_custom_call" | custom-call | flops 4000000 | bytes 12000000 | tf_op jit(solution)/shard_map/pallas_call | solution.py:280
  44.9 0.9 broadcast_in_dim.2
  45.8 14.1 %all-to-all-start = ((f32[128,8,128]{2,1,0:T(8,128)}), f32[128,8,128]{2,1,0:T(8,128)S(1)}, u32[]{:S(2)}, u32[]{:S(2)}) async-start(f32[128,8,128]{2,1,0:T(8,128)} %broadcast_in_dim.2), calls=%async_computation | async-start | bytes 1048576 | tf_op jit(solution)/shard_map/all_to_all | solution.py:621
  59.9 0.7 collective-permute-start.7
  60.6 3.1 %collective-permute-start.6 = (f32[8,8,128]{2,1,0:T(8,128)S(1)}, f32[8,8,128]{2,1,0:T(8,128)S(1)}, u32[]{:S(2)}, u32[]{:S(2)}) collective-permute-start(f32[8,8,128]{2,1,0:T(8,128)S(1)} %get-tuple-element.14), channel_id=1, source_target_pairs={{0,8},{8,0},{16,24},{24,16},{1,9},{9,1},{17,25},{25,17},{2,10},{10... | collective-permute-start | bytes 98312 | tf_op jit(solution)/shard_map/ppermute | solution.py:564
  63.7 0.0 collective-permute-done.7
  63.7 1.9 %collective-permute-done.6 = f32[8,8,128]{2,1,0:T(8,128)S(1)} collective-permute-done((f32[8,8,128]{2,1,0:T(8,128)S(1)}, f32[8,8,128]{2,1,0:T(8,128)S(1)}, u32[]{:S(2)}, u32[]{:S(2)}) %collective-permute-start.6) | collective-permute-done | bytes 32800 | tf_op jit(solution)/shard_map/ppermute | solution.py:564
  65.6 0.7 collective-permute-start.8
  66.3 3.5 %collective-permute-start.9 = (f32[2,8,8,128]{3,2,1,0:T(8,128)S(1)}, f32[2,8,8,128]{3,2,1,0:T(8,128)S(1)}, u32[]{:S(2)}, u32[]{:S(2)}) collective-permute-start(f32[2,8,8,128]{3,2,1,0:T(8,128)S(1)} %pad_maximum_fusion.5), channel_id=1, source_target_pairs={{0,1},{1,0},{2,3},{3,2},{4,5},{5,4},{6,7},{7,6},{8,9},{9,8},{10,11... | collective-permute-start | bytes 196616 | tf_op jit(solution)/shard_map/ppermute | solution.py:564
  69.8 0.0 collective-permute-done.8
  69.8 3.2 %collective-permute-done.9 = f32[2,8,8,128]{3,2,1,0:T(8,128)S(1)} collective-permute-done((f32[2,8,8,128]{3,2,1,0:T(8,128)S(1)}, f32[2,8,8,128]{3,2,1,0:T(8,128)S(1)}, u32[]{:S(2)}, u32[]{:S(2)}) %collective-permute-start.9) | collective-permute-done | bytes 65568 | tf_op jit(solution)/shard_map/ppermute | solution.py:564
  73.0 6.7 %all-to-all-done = f32[128,8,128]{2,1,0:T(8,128)S(1)} async-done(((f32[128,8,128]{2,1,0:T(8,128)}), f32[128,8,128]{2,1,0:T(8,128)S(1)}, u32[]{:S(2)}, u32[]{:S(2)}) %all-to-all-start) | async-done | bytes 524320 | tf_op jit(solution)/shard_map/all_to_all | solution.py:621
  79.7 0.1 copy.4
  79.8 2.3 %collective-permute-start.12 = (f32[128,8,128]{2,1,0:T(8,128)S(1)}, f32[128,8,128]{2,1,0:T(8,128)S(1)}, u32[]{:S(2)}, u32[]{:S(2)}) collective-permute-start(f32[128,8,128]{2,1,0:T(8,128)S(1)} %bitcast.46), channel_id=1, source_target_pairs={{0,32},{32,0},{1,33},{33,1},{2,34},{34,2},{3,35},{35,3},{4,36},{36... | collective-permute-start | bytes 1572872 | tf_op jit(solution)/shard_map/ppermute | solution.py:656
  82.2 0.1 collective-permute-start.10
  82.3 2.1 %collective-permute-start.11 = (f32[2,7,24,128]{3,2,1,0:T(8,128)S(1)}, f32[2,7,24,128]{3,2,1,0:T(8,128)S(1)}, u32[]{:S(2)}, u32[]{:S(2)}) collective-permute-start(f32[2,7,24,128]{3,2,1,0:T(8,128)S(1)} %get-tuple-element.36), channel_id=1, source_target_pairs={{32,64},{96,128},{160,192},{64,32},{128,96},{192,160},{33,65},{97,... | collective-permute-start | bytes 516104 | tf_op jit(solution)/shard_map/ppermute | solution.py:565
  84.4 0.1 pad_add_fusion.where_ref
  84.5 0.0 collective-permute-done.12.other_ref
  84.5 6.7 %shard_map.43.win = f32[2,12,16,128]{3,2,1,0:T(8,128)S(1)} custom-call(s32[3]{0:T(128)S(1)} %pad_add_fusion.where_ref, f32[128,8,128]{2,1,0:T(8,128)S(1)} %bitcast.47, f32[128,8,128]{2,1,0:T(8,128)S(1)} %collective-permute-done.12.other_ref), custom_call_target="tpu_custom_call" | custom-call | flops 10000000 | bytes 30000000 | tf_op jit(solution)/shard_map/pallas_call | solution.py:280
  91.2 0.0 collective-permute-done.10.ma
  91.2 0.0 collective-permute-done.11.mb
  91.2 5.8 %shard_map.44 = (f32[16,16,128]{2,1,0:T(8,128)}, f32[16,16,128]{2,1,0:T(8,128)}) custom-call(s32[3]{0:T(128)S(1)} %pad_add_fusion.where_ref, f32[5,26,32,128]{3,2,1,0:T(8,128)S(1)} %get-tuple-element.12.top, f32[22,24,128]{2,1,0:T(8,128)S(1)} %get-tuple-element.13.sl, f32[2,8,24,128]{3,2,1,0:T(8,128)S(1)} %pad_maximum_fusion.4.m, ...), custom_call_target="tpu_custom_call" | custom-call | flops 4000000 | bytes 12000000 | tf_op jit(solution)/shard_map/pallas_call | solution.py:280
  (46 shorter events, 0.6 us)
Async XLA Ops:
  2.1 5.3 %collective-permute-start.1 = (f32[4,2,16,128]{3,2,1,0:T(8,128)S(1)}, f32[4,2,16,128]{3,2,1,0:T(8,128)S(1)}, u32[]{:S(2)}, u32[]{:S(2)}) collective-permute-start(f32[4,2,16,128]{3,2,1,0:T(8,128)S(1)} %get-tuple-element.45), channel_id=1, source_target_pairs={{8,16},{16,8},{9,17},{17,9},{10,18},{18,10},{11,19},{19,11},{12,20... | collective-permute-start | bytes 196616 | tf_op jit(solution)/shard_map/ppermute | solution.py:565
  2.8 6.2 %collective-permute-start = (f32[4,2,16,128]{3,2,1,0:T(8,128)S(1)}, f32[4,2,16,128]{3,2,1,0:T(8,128)S(1)}, u32[]{:S(2)}, u32[]{:S(2)}) collective-permute-start(f32[4,2,16,128]{3,2,1,0:T(8,128)S(1)} %get-tuple-element.44), channel_id=1, source_target_pairs={{0,8},{8,0},{16,24},{24,16},{1,9},{9,1},{17,25},{25,17},{2,10},{10... | collective-permute-start | bytes 196616 | tf_op jit(solution)/shard_map/ppermute | solution.py:564
  9.1 5.3 %collective-permute-start.2 = (f32[80,8,128]{2,1,0:T(8,128)S(1)}, f32[80,8,128]{2,1,0:T(8,128)S(1)}, u32[]{:S(2)}, u32[]{:S(2)}) collective-permute-start(f32[80,8,128]{2,1,0:T(8,128)S(1)} %pad_maximum_fusion.1), channel_id=1, source_target_pairs={{1,2},{3,4},{5,6},{2,1},{4,3},{6,5},{9,10},{11,12},{13,14},{10,9},... | collective-permute-start | bytes 983048 | tf_op jit(solution)/shard_map/ppermute | solution.py:565
  9.8 10.5 %collective-permute-start.3 = (f32[80,8,128]{2,1,0:T(8,128)S(1)}, f32[80,8,128]{2,1,0:T(8,128)S(1)}, u32[]{:S(2)}, u32[]{:S(2)}) collective-permute-start(f32[80,8,128]{2,1,0:T(8,128)S(1)} %pad_maximum_fusion.1), channel_id=1, source_target_pairs={{0,1},{1,0},{2,3},{3,2},{4,5},{5,4},{6,7},{7,6},{8,9},{9,8},{10,11... | collective-permute-start | bytes 983048 | tf_op jit(solution)/shard_map/ppermute | solution.py:564
  21.0 5.9 %collective-permute-start.5 = (f32[160,8,128]{2,1,0:T(8,128)S(1)}, f32[160,8,128]{2,1,0:T(8,128)S(1)}, u32[]{:S(2)}, u32[]{:S(2)}) collective-permute-start(f32[160,8,128]{2,1,0:T(8,128)S(1)} %get-tuple-element.18), channel_id=1, source_target_pairs={{0,32},{32,0},{64,96},{96,64},{128,160},{160,128},{192,224},{224,1... | collective-permute-start | bytes 1966088 | tf_op jit(solution)/shard_map/ppermute | solution.py:564
  23.9 11.9 %collective-permute-start.4 = (f32[160,8,128]{2,1,0:T(8,128)S(1)}, f32[160,8,128]{2,1,0:T(8,128)S(1)}, u32[]{:S(2)}, u32[]{:S(2)}) collective-permute-start(f32[160,8,128]{2,1,0:T(8,128)S(1)} %get-tuple-element.19), channel_id=1, source_target_pairs={{32,64},{96,128},{160,192},{64,32},{128,96},{192,160},{33,65},{97,... | collective-permute-start | bytes 1966088 | tf_op jit(solution)/shard_map/ppermute | solution.py:565
  45.8 33.9 %all-to-all-start = ((f32[128,8,128]{2,1,0:T(8,128)}), f32[128,8,128]{2,1,0:T(8,128)S(1)}, u32[]{:S(2)}, u32[]{:S(2)}) async-start(f32[128,8,128]{2,1,0:T(8,128)} %broadcast_in_dim.2), calls=%async_computation | async-start | bytes 1048576 | tf_op jit(solution)/shard_map/all_to_all | solution.py:621
  59.9 3.8 %collective-permute-start.7 = (f32[8,8,128]{2,1,0:T(8,128)S(1)}, f32[8,8,128]{2,1,0:T(8,128)S(1)}, u32[]{:S(2)}, u32[]{:S(2)}) collective-permute-start(f32[8,8,128]{2,1,0:T(8,128)S(1)} %get-tuple-element.14), channel_id=1, source_target_pairs={{8,16},{16,8},{9,17},{17,9},{10,18},{18,10},{11,19},{19,11},{12,20... | collective-permute-start | bytes 98312 | tf_op jit(solution)/shard_map/ppermute | solution.py:565
  60.6 5.0 %collective-permute-start.6 = (f32[8,8,128]{2,1,0:T(8,128)S(1)}, f32[8,8,128]{2,1,0:T(8,128)S(1)}, u32[]{:S(2)}, u32[]{:S(2)}) collective-permute-start(f32[8,8,128]{2,1,0:T(8,128)S(1)} %get-tuple-element.14), channel_id=1, source_target_pairs={{0,8},{8,0},{16,24},{24,16},{1,9},{9,1},{17,25},{25,17},{2,10},{10... | collective-permute-start | bytes 98312 | tf_op jit(solution)/shard_map/ppermute | solution.py:564
  65.6 4.2 %collective-permute-start.8 = (f32[2,8,8,128]{3,2,1,0:T(8,128)S(1)}, f32[2,8,8,128]{3,2,1,0:T(8,128)S(1)}, u32[]{:S(2)}, u32[]{:S(2)}) collective-permute-start(f32[2,8,8,128]{3,2,1,0:T(8,128)S(1)} %pad_maximum_fusion.5), channel_id=1, source_target_pairs={{1,2},{3,4},{5,6},{2,1},{4,3},{6,5},{9,10},{11,12},{13,14},{10,9},... | collective-permute-start | bytes 196616 | tf_op jit(solution)/shard_map/ppermute | solution.py:565
  66.3 6.7 %collective-permute-start.9 = (f32[2,8,8,128]{3,2,1,0:T(8,128)S(1)}, f32[2,8,8,128]{3,2,1,0:T(8,128)S(1)}, u32[]{:S(2)}, u32[]{:S(2)}) collective-permute-start(f32[2,8,8,128]{3,2,1,0:T(8,128)S(1)} %pad_maximum_fusion.5), channel_id=1, source_target_pairs={{0,1},{1,0},{2,3},{3,2},{4,5},{5,4},{6,7},{7,6},{8,9},{9,8},{10,11... | collective-permute-start | bytes 196616 | tf_op jit(solution)/shard_map/ppermute | solution.py:564
  79.8 4.7 %collective-permute-start.12 = (f32[128,8,128]{2,1,0:T(8,128)S(1)}, f32[128,8,128]{2,1,0:T(8,128)S(1)}, u32[]{:S(2)}, u32[]{:S(2)}) collective-permute-start(f32[128,8,128]{2,1,0:T(8,128)S(1)} %bitcast.46), channel_id=1, source_target_pairs={{0,32},{32,0},{1,33},{33,1},{2,34},{34,2},{3,35},{35,3},{4,36},{36... | collective-permute-start | bytes 1572872 | tf_op jit(solution)/shard_map/ppermute | solution.py:656
  82.2 9.0 %collective-permute-start.10 = (f32[2,7,24,128]{3,2,1,0:T(8,128)S(1)}, f32[2,7,24,128]{3,2,1,0:T(8,128)S(1)}, u32[]{:S(2)}, u32[]{:S(2)}) collective-permute-start(f32[2,7,24,128]{3,2,1,0:T(8,128)S(1)} %get-tuple-element.37), channel_id=1, source_target_pairs={{0,32},{32,0},{64,96},{96,64},{128,160},{160,128},{192,224},{224,1... | collective-permute-start | bytes 516104 | tf_op jit(solution)/shard_map/ppermute | solution.py:564
  82.3 8.9 %collective-permute-start.11 = (f32[2,7,24,128]{3,2,1,0:T(8,128)S(1)}, f32[2,7,24,128]{3,2,1,0:T(8,128)S(1)}, u32[]{:S(2)}, u32[]{:S(2)}) collective-permute-start(f32[2,7,24,128]{3,2,1,0:T(8,128)S(1)} %get-tuple-element.36), channel_id=1, source_target_pairs={{32,64},{96,128},{160,192},{64,32},{128,96},{192,160},{33,65},{97,... | collective-permute-start | bytes 516104 | tf_op jit(solution)/shard_map/ppermute | solution.py:565

commit v5 on v4

--- a/solution.py
+++ b/solution.py
@@ -238,7 +238,7 @@
     return (2 * k + 7) % 16
 
 
-def fill_rb(out, i, at, planes_ref, strips, k0, count, rows, step=4):
+def fill_rb(out, i, at, planes_ref, strips, k0, count, rows, step=8):
     number = rows.stop - rows.start
     lane = iota((number, LANES), 1)
     own = lane < HALF
@@ -353,9 +353,9 @@
         return carry
 
     lax.fori_loop(0, X0, top_body, 0)
-    couplings(sl, fl, cl, gl, wl, 3, X1 - 3, 4.0, step=4)
+    couplings(sl, fl, cl, gl, wl, 3, X1 - 3, 4.0, step=8)
     first_half_sweep(ul, gl, 3, X1 - 3, H1, step=8)
-    half_sweep(ul, cl, gl, 4, X1 - 4, H1 + 1, step=14)
+    half_sweep(ul, cl, gl, 4, X1 - 4, H1 + 1, step=8)
     half_sweep(ul, cl, gl, 5, X1 - 5, H1, step=12)
     half_sweep(ul, cl, gl, 6, X1 - 6, H1 + 1, step=10)
     r = residual_planes(ul, cl, gl, wl, H1, 8)
@@ -382,7 +382,7 @@
     lane = iota((8, LANES), 1)
     wide = iota((32, LANES), 1)
     zero2 = jnp.zeros((32, LANES), F32)
-    core = lax.rem(where_ref[0], 2)
+    core, chip = lax.rem(where_ref[0], 2), where_ref[0] // 2
 
     def transposed(groups):
         for s in (1, 2, 4):
@@ -400,7 +400,7 @@
             plane = 4 * (2 * xcl + c)
             groups = []
             for zi in range(8):
-                at = [((2 * xh + xcl) * 4 + iy) * 8 + zi for xh in range(2) for iy in range(4)]
+                at = [(lax.bitwise_xor(2 * xh + xcl, chip) * 4 + iy) * 8 + zi for xh in range(2) for iy in range(4)]
                 groups.append([all_ref[i] for i in at])
             for zi, tiles in enumerate(transposed(groups)):
                 rows = slice(8 * (zi // 2), 8 * (zi // 2) + 8)
@@ -506,7 +506,7 @@
 
 def ascend(where_ref, top, sl, m, ma, mb, win, u_out, r_out, c, g, w, u, d0, fl, cl, gl, wl, ul, t1, d1):
     fill_narrow(ul, fl, lax.rem(where_ref[0], 2) == 0, m, ma, mb)
-    couplings(sl, fl, cl, gl, wl, 1, X1 - 1, 4.0, step=4)
+    couplings(sl, fl, cl, gl, wl, 1, X1 - 1, 4.0, step=20)
     k, l = iota((2 * LANES, LANES), 0), iota((2 * LANES, LANES), 1)
     from_lane = jnp.where(l < 96, l >> 2, 96 + (l >> 2))
     widen = jnp.where(k == from_lane + LANES * ((l >> 1) & 1), 1.0, 0.0)
@@ -523,7 +523,7 @@
     half_sweep(ul, cl, gl, 3, X1 - 3, H1, step=16)
     half_sweep(ul, cl, gl, 4, X1 - 4, H1 + 1, step=14)
     s, f, black, red = top.at[0:2], top.at[2:4], u.at[1], u.at[0]
-    couplings_rb(s, f, c, g, w, 1, X0 - 1, 1.0, 1, 6)
+    couplings_rb(s, f, c, g, w, 1, X0 - 1, 1.0, 1, 4)
     fine = ul[4:18, 4:20]
     d0[:, pl.ds(0, 16, stride=2), :] = fine
     d0[:, pl.ds(1, 16, stride=2), :] = fine
@@ -561,8 +561,8 @@
     first = [(i, i ^ 1) for i in range(count)]
     second = [(i, i + 1) for i in range(1, count - 1, 2)]
     second += [(j, i) for i, j in second]
+    b = lax.ppermute(jnp.where(even, low, high), axis, second)
     a = lax.ppermute(jnp.where(even, high, low), axis, first)
-    b = lax.ppermute(jnp.where(even, low, high), axis, second)
     return a, b
 
 
@@ -651,8 +651,11 @@
         + [vmem(4, 2, 8, LANES), vmem(4, 8, LANES)],
     )(*extend_wide(field, lo, hi))
     narrow = extend_narrow(next1)
-    tiles = spread(tile, ("xc", "gy", "gz"), sizes)
-    mine = tiles.reshape(-1, 4, 2, 2, 4, LANES).transpose(0, 1, 3, 2, 4, 5).reshape(-1, 8, LANES)
+    line = spread(tile, ("gy", "gz"), sizes)
+    line = line.reshape(-1, 4, 2, 2, 4, LANES).transpose(0, 1, 3, 2, 4, 5).reshape(-1, 8, LANES)
+    chips = sizes["xc"]
+    mine = [line] + [lax.ppermute(line, "xc", [(i, i ^ k) for i in range(chips)]) for k in range(1, chips)]
+    mine = jnp.concatenate(mine)
     other = lax.ppermute(mine, "co", [(0, 1), (1, 0)])
     place = jnp.stack([lax.axis_index(axis_of("gx")), lax.axis_index("gy"), lax.axis_index("gz")]).astype(jnp.int32)
     window = call(

time: 97.3 us -> 94.3 us (0.969)
  waiting for transfers between devices: 28.1 us -> 25.1 us
  starting transfers between devices: 43 us -> 44.6 us
  Pallas kernels: 21.8 us -> 20.5 us
    ppermute x6, waiting for transfers between devices: 12.7 us -> 7.56 us  [exchange(): a = lax.ppermute(jnp.where(even, high, low), axis, first)]
    all_to_all x1, starting transfers between devices: 14.1 us -> 9.51 us  [spread(): return lax.all_to_all(jnp.broadcast_to(x[None], (n,) + x.shape), axes, 0, 0)]
    ppermute x0 -> x3, waiting for transfers between devices: none -> 4.14 us  [on_device(): lax.ppermute(line, 'xc', [(i, i ^ k) for i in range(chips)])]
    ppermute x0 -> x3, starting transfers between devices: none -> 3.33 us  [on_device(): lax.ppermute(line, 'xc', [(i, i ^ k) for i in range(chips)])]
    all_to_all x1, waiting for transfers between devices: 6.68 us -> 4.68 us  [spread(): return lax.all_to_all(jnp.broadcast_to(x[None], (n,) + x.shape), axes, 0, 0)]
    ppermute x1, starting transfers between devices: 2.34 us -> 4.18 us  [on_device(): other = lax.ppermute(mine, 'co', [(0, 1), (1, 0)])]
    pallas_call x4, Pallas kernels: 21.8 us -> 20.5 us  [run(): pl.pallas_call(kernel, out_shape=out_shape, in_specs=specs, out_specs=jax...]
  transfers between devices with their start and end apart: 14 -> 17, of which waited for: 6 -> 6; matrix products, arithmetic and copies ran while one was open for 0% -> 1% of each run, Pallas kernels for 7% -> 7%
where the time goes in v5:
time: 94.3 us; the launch traced here: 94 us
  starting transfers between devices  44.6 us (47%)
  waiting for transfers between devices  25.1 us (27%)
  Pallas kernels  20.5 us (22%)
  other arithmetic  1.54 us (2%)
  between operations  1.14 us (1%)
  local copies, waits for them, and re-layouts  1.12 us (1%)
    pallas_call x4, Pallas kernels, run(): pl.pallas_call(kernel, out_shape=out_shape, in_specs=specs, out_specs=jax...  20.5 us
    ppermute x6, starting transfers between devices, exchange(): a = lax.ppermute(jnp.where(even, high, low), axis, first)  18.9 us
    all_to_all x1, starting transfers between devices, spread(): return lax.all_to_all(jnp.broadcast_to(x[None], (n,) + x.shape), axes, 0, 0)  9.51 us
    ppermute x6, waiting for transfers between devices, exchange(): b = lax.ppermute(jnp.where(even, low, high), axis, second)  8.77 us
    ppermute x6, starting transfers between devices, exchange(): b = lax.ppermute(jnp.where(even, low, high), axis, second)  8.65 us
    ppermute x6, waiting for transfers between devices, exchange(): a = lax.ppermute(jnp.where(even, high, low), axis, first)  7.56 us
    all_to_all x1, waiting for transfers between devices, spread(): return lax.all_to_all(jnp.broadcast_to(x[None], (n,) + x.shape), axes, 0, 0)  4.68 us
    ppermute x1, starting transfers between devices, on_device(): other = lax.ppermute(mine, 'co', [(0, 1), (1, 0)])  4.18 us
  transfers between devices with their start and end apart: 17, of which 6 were waited for; matrix products, arithmetic and copies ran while one was open for 1% of the time, Pallas kernels for 7%

profile of v5, /device:TPU:1, one launch (start us, length us, event | category | flops | bytes accessed | tf_op | source)
XLA Modules:
  0.0 94.0 jit_solution(15862494829449315365)
XLA Ops:
  0.6 1.0 %pad_maximum_fusion.3.in_ref = f32[2,16,16,128]{3,2,1,0:T(8,128)S(1)} fusion(f32[1,16,16,128]{3,2,1,0:T(8,128)} %bitcast.83, f32[1,16,16,128]{3,2,1,0:T(8,128)} %bitcast.84), kind=kLoop, calls=%fused_computation.9 | loop fusion | flops 65536 | bytes 524288 | tf_op jit(solution)/shard_map/stack | solution.py:644
  1.6 0.5 shard_map.41
  2.1 0.7 collective-permute-start.1
  2.8 4.6 %collective-permute-start = (f32[4,2,16,128]{3,2,1,0:T(8,128)S(1)}, f32[4,2,16,128]{3,2,1,0:T(8,128)S(1)}, u32[]{:S(2)}, u32[]{:S(2)}) collective-permute-start(f32[4,2,16,128]{3,2,1,0:T(8,128)S(1)} %get-tuple-element.44), channel_id=1, source_target_pairs={{0,8},{8,0},{16,24},{24,16},{1,9},{9,1},{17,25},{25,17},{2,10},{10... | collective-permute-start | bytes 196616 | tf_op jit(solution)/shard_map/ppermute | solution.py:565
  7.4 0.0 collective-permute-done.1
  7.4 1.6 %collective-permute-done = f32[4,2,16,128]{3,2,1,0:T(8,128)S(1)} collective-permute-done((f32[4,2,16,128]{3,2,1,0:T(8,128)S(1)}, f32[4,2,16,128]{3,2,1,0:T(8,128)S(1)}, u32[]{:S(2)}, u32[]{:S(2)}) %collective-permute-start) | collective-permute-done | bytes 65568 | tf_op jit(solution)/shard_map/ppermute | solution.py:565
  9.1 0.7 collective-permute-start.2
  9.8 4.6 %collective-permute-start.3 = (f32[80,8,128]{2,1,0:T(8,128)S(1)}, f32[80,8,128]{2,1,0:T(8,128)S(1)}, u32[]{:S(2)}, u32[]{:S(2)}) collective-permute-start(f32[80,8,128]{2,1,0:T(8,128)S(1)} %pad_maximum_fusion.2), channel_id=1, source_target_pairs={{0,1},{1,0},{2,3},{3,2},{4,5},{5,4},{6,7},{7,6},{8,9},{9,8},{10,11... | collective-permute-start | bytes 983048 | tf_op jit(solution)/shard_map/ppermute | solution.py:565
  14.4 0.0 collective-permute-done.2
  14.4 5.9 %collective-permute-done.3 = f32[80,8,128]{2,1,0:T(8,128)S(1)} collective-permute-done((f32[80,8,128]{2,1,0:T(8,128)S(1)}, f32[80,8,128]{2,1,0:T(8,128)S(1)}, u32[]{:S(2)}, u32[]{:S(2)}) %collective-permute-start.3) | collective-permute-done | bytes 327712 | tf_op jit(solution)/shard_map/ppermute | solution.py:565
  20.4 0.1 pad_maximum_fusion.e
  20.5 0.1 slice_bitcast_fusion
  21.0 0.1 broadcast_select_fusion.2
  21.0 2.8 %collective-permute-start.5 = (f32[160,8,128]{2,1,0:T(8,128)S(1)}, f32[160,8,128]{2,1,0:T(8,128)S(1)}, u32[]{:S(2)}, u32[]{:S(2)}) collective-permute-start(f32[160,8,128]{2,1,0:T(8,128)S(1)} %get-tuple-element.18), channel_id=1, source_target_pairs={{0,32},{32,0},{64,96},{96,64},{128,160},{160,128},{192,224},{224,1... | collective-permute-start | bytes 1966088 | tf_op jit(solution)/shard_map/ppermute | solution.py:565
  23.9 3.1 %collective-permute-start.4 = (f32[160,8,128]{2,1,0:T(8,128)S(1)}, f32[160,8,128]{2,1,0:T(8,128)S(1)}, u32[]{:S(2)}, u32[]{:S(2)}) collective-permute-start(f32[160,8,128]{2,1,0:T(8,128)S(1)} %get-tuple-element.19), channel_id=1, source_target_pairs={{32,64},{96,128},{160,192},{64,32},{128,96},{192,160},{33,65},{97,... | collective-permute-start | bytes 1966088 | tf_op jit(solution)/shard_map/ppermute | solution.py:564
  27.0 0.0 collective-permute-done.5
  27.0 8.8 %collective-permute-done.4 = f32[160,8,128]{2,1,0:T(8,128)S(1)} collective-permute-done((f32[160,8,128]{2,1,0:T(8,128)S(1)}, f32[160,8,128]{2,1,0:T(8,128)S(1)}, u32[]{:S(2)}, u32[]{:S(2)}) %collective-permute-start.4) | collective-permute-done | bytes 655392 | tf_op jit(solution)/shard_map/ppermute | solution.py:564
  35.8 0.1 broadcast_select_fusion
  36.1 8.0 %shard_map.42 = (f32[5,26,32,128]{3,2,1,0:T(8,128)S(1)}, f32[22,24,128]{2,1,0:T(8,128)S(1)}, f32[8,8,128]{2,1,0:T(8,128)S(1)}, f32[8,128]{1,0:T(8,128)S(1)}) custom-call(f32[2,16,48,128]{3,2,1,0:T(8,128)S(1)} %pad_maximum_fusion.e, f32[4,2,48,128]{3,2,1,0:T(8,128)S(1)} %pad_maximum_fusion.4.b, f32[5,48,128]{2,1,0:T(8,128)S(1)} %bitcast.51, ...), custom_call_target="tpu_custom_call" | custom-call | flops 4000000 | bytes 12000000 | tf_op jit(solution)/shard_map/pallas_call | solution.py:280
  44.1 0.7 collective-permute-start.7
  44.8 3.0 %collective-permute-start.6 = (f32[8,8,128]{2,1,0:T(8,128)S(1)}, f32[8,8,128]{2,1,0:T(8,128)S(1)}, u32[]{:S(2)}, u32[]{:S(2)}) collective-permute-start(f32[8,8,128]{2,1,0:T(8,128)S(1)} %get-tuple-element.14), channel_id=1, source_target_pairs={{0,8},{8,0},{16,24},{24,16},{1,9},{9,1},{17,25},{25,17},{2,10},{10... | collective-permute-start | bytes 98312 | tf_op jit(solution)/shard_map/ppermute | solution.py:565
  47.8 0.7 broadcast_in_dim.2
  48.5 9.5 %all-to-all-start = ((f32[32,8,128]{2,1,0:T(8,128)}), f32[32,8,128]{2,1,0:T(8,128)S(1)}, u32[]{:S(2)}, u32[]{:S(2)}) async-start(f32[32,8,128]{2,1,0:T(8,128)} %broadcast_in_dim.2), calls=%async_computation | async-start | bytes 262144 | tf_op jit(solution)/shard_map/all_to_all | solution.py:621
  58.0 0.0 collective-permute-done.7
  58.0 0.0 collective-permute-done.6
  58.0 0.7 collective-permute-start.8
  58.7 3.7 %collective-permute-start.9 = (f32[2,8,8,128]{3,2,1,0:T(8,128)S(1)}, f32[2,8,8,128]{3,2,1,0:T(8,128)S(1)}, u32[]{:S(2)}, u32[]{:S(2)}) collective-permute-start(f32[2,8,8,128]{3,2,1,0:T(8,128)S(1)} %pad_maximum_fusion.6), channel_id=1, source_target_pairs={{0,1},{1,0},{2,3},{3,2},{4,5},{5,4},{6,7},{7,6},{8,9},{9,8},{10,11... | collective-permute-start | bytes 196616 | tf_op jit(solution)/shard_map/ppermute | solution.py:565
  62.5 4.7 %all-to-all-done = f32[32,8,128]{2,1,0:T(8,128)S(1)} async-done(((f32[32,8,128]{2,1,0:T(8,128)}), f32[32,8,128]{2,1,0:T(8,128)S(1)}, u32[]{:S(2)}, u32[]{:S(2)}) %all-to-all-start) | async-done | bytes 131104 | tf_op jit(solution)/shard_map/all_to_all | solution.py:621
  67.2 0.1 collective-permute-start.14
  67.3 3.2 %collective-permute-start.13 = (f32[32,8,128]{2,1,0:T(8,128)S(1)}, f32[32,8,128]{2,1,0:T(8,128)S(1)}, u32[]{:S(2)}, u32[]{:S(2)}) collective-permute-start(f32[32,8,128]{2,1,0:T(8,128)S(1)} %bitcast.70), channel_id=1, source_target_pairs={{0,128},{64,192},{128,0},{192,64},{1,129},{65,193},{129,1},{193,65... | collective-permute-start | bytes 393224 | tf_op jit(solution)/shard_map/ppermute | solution.py:657
  70.4 0.1 collective-permute-start.12
  70.5 0.0 collective-permute-done.8
  70.5 0.0 collective-permute-done.9
  70.5 3.9 %collective-permute-done.14 = f32[32,8,128]{2,1,0:T(8,128)S(1)} collective-permute-done((f32[32,8,128]{2,1,0:T(8,128)S(1)}, f32[32,8,128]{2,1,0:T(8,128)S(1)}, u32[]{:S(2)}, u32[]{:S(2)}) %collective-permute-start.14) | collective-permute-done | bytes 131104 | tf_op jit(solution)/shard_map/ppermute | solution.py:657
  74.5 0.0 collective-permute-done.13
  74.5 0.2 collective-permute-done.12
  74.7 4.2 %collective-permute-start.15 = (f32[128,8,128]{2,1,0:T(8,128)S(1)}, f32[128,8,128]{2,1,0:T(8,128)S(1)}, u32[]{:S(2)}, u32[]{:S(2)}) collective-permute-start(f32[128,8,128]{2,1,0:T(8,128)S(1)} %pad_maximum_fusion.1.mine_ref), channel_id=1, source_target_pairs={{0,32},{32,0},{1,33},{33,1},{2,34},{34,2},{3,35},{35,3},{4,36},{36... | collective-permute-start | bytes 1572872 | tf_op jit(solution)/shard_map/ppermute | solution.py:659
  78.9 0.1 collective-permute-start.10
  79.0 2.9 %collective-permute-start.11 = (f32[2,7,24,128]{3,2,1,0:T(8,128)S(1)}, f32[2,7,24,128]{3,2,1,0:T(8,128)S(1)}, u32[]{:S(2)}, u32[]{:S(2)}) collective-permute-start(f32[2,7,24,128]{3,2,1,0:T(8,128)S(1)} %get-tuple-element.36), channel_id=1, source_target_pairs={{32,64},{96,128},{160,192},{64,32},{128,96},{192,160},{33,65},{97,... | collective-permute-start | bytes 516104 | tf_op jit(solution)/shard_map/ppermute | solution.py:564
  81.9 0.1 pad_add_fusion.where_ref
  82.0 0.0 collective-permute-done.15.other_ref
  82.0 6.7 %shard_map.43.win = f32[2,12,16,128]{3,2,1,0:T(8,128)S(1)} custom-call(s32[3]{0:T(128)S(1)} %pad_add_fusion.where_ref, f32[128,8,128]{2,1,0:T(8,128)S(1)} %pad_maximum_fusion.1.mine_ref, f32[128,8,128]{2,1,0:T(8,128)S(1)} %collective-permute-done.15.other_ref), custom_call_target="tpu_custom_call" | custom-call | flops 10000000 | bytes 30000000 | tf_op jit(solution)/shard_map/pallas_call | solution.py:280
  88.7 0.0 collective-permute-done.10.ma
  88.7 0.0 collective-permute-done.11.mb
  88.7 5.3 %shard_map.44 = (f32[16,16,128]{2,1,0:T(8,128)}, f32[16,16,128]{2,1,0:T(8,128)}) custom-call(s32[3]{0:T(128)S(1)} %pad_add_fusion.where_ref, f32[5,26,32,128]{3,2,1,0:T(8,128)S(1)} %get-tuple-element.12.top, f32[22,24,128]{2,1,0:T(8,128)S(1)} %get-tuple-element.13.sl, f32[2,8,24,128]{3,2,1,0:T(8,128)S(1)} %pad_maximum_fusion.5.m, ...), custom_call_target="tpu_custom_call" | custom-call | flops 4000000 | bytes 12000000 | tf_op jit(solution)/shard_map/pallas_call | solution.py:280
  (48 shorter events, 0.6 us)
Async XLA Ops:
  2.1 5.3 %collective-permute-start.1 = (f32[4,2,16,128]{3,2,1,0:T(8,128)S(1)}, f32[4,2,16,128]{3,2,1,0:T(8,128)S(1)}, u32[]{:S(2)}, u32[]{:S(2)}) collective-permute-start(f32[4,2,16,128]{3,2,1,0:T(8,128)S(1)} %get-tuple-element.45), channel_id=1, source_target_pairs={{8,16},{16,8},{9,17},{17,9},{10,18},{18,10},{11,19},{19,11},{12,20... | collective-permute-start | bytes 196616 | tf_op jit(solution)/shard_map/ppermute | solution.py:564
  2.8 6.2 %collective-permute-start = (f32[4,2,16,128]{3,2,1,0:T(8,128)S(1)}, f32[4,2,16,128]{3,2,1,0:T(8,128)S(1)}, u32[]{:S(2)}, u32[]{:S(2)}) collective-permute-start(f32[4,2,16,128]{3,2,1,0:T(8,128)S(1)} %get-tuple-element.44), channel_id=1, source_target_pairs={{0,8},{8,0},{16,24},{24,16},{1,9},{9,1},{17,25},{25,17},{2,10},{10... | collective-permute-start | bytes 196616 | tf_op jit(solution)/shard_map/ppermute | solution.py:565
  9.1 5.3 %collective-permute-start.2 = (f32[80,8,128]{2,1,0:T(8,128)S(1)}, f32[80,8,128]{2,1,0:T(8,128)S(1)}, u32[]{:S(2)}, u32[]{:S(2)}) collective-permute-start(f32[80,8,128]{2,1,0:T(8,128)S(1)} %pad_maximum_fusion.2), channel_id=1, source_target_pairs={{1,2},{3,4},{5,6},{2,1},{4,3},{6,5},{9,10},{11,12},{13,14},{10,9},... | collective-permute-start | bytes 983048 | tf_op jit(solution)/shard_map/ppermute | solution.py:564
  9.8 10.5 %collective-permute-start.3 = (f32[80,8,128]{2,1,0:T(8,128)S(1)}, f32[80,8,128]{2,1,0:T(8,128)S(1)}, u32[]{:S(2)}, u32[]{:S(2)}) collective-permute-start(f32[80,8,128]{2,1,0:T(8,128)S(1)} %pad_maximum_fusion.2), channel_id=1, source_target_pairs={{0,1},{1,0},{2,3},{3,2},{4,5},{5,4},{6,7},{7,6},{8,9},{9,8},{10,11... | collective-permute-start | bytes 983048 | tf_op jit(solution)/shard_map/ppermute | solution.py:565
  21.0 6.0 %collective-permute-start.5 = (f32[160,8,128]{2,1,0:T(8,128)S(1)}, f32[160,8,128]{2,1,0:T(8,128)S(1)}, u32[]{:S(2)}, u32[]{:S(2)}) collective-permute-start(f32[160,8,128]{2,1,0:T(8,128)S(1)} %get-tuple-element.18), channel_id=1, source_target_pairs={{0,32},{32,0},{64,96},{96,64},{128,160},{160,128},{192,224},{224,1... | collective-permute-start | bytes 1966088 | tf_op jit(solution)/shard_map/ppermute | solution.py:565
  23.9 11.9 %collective-permute-start.4 = (f32[160,8,128]{2,1,0:T(8,128)S(1)}, f32[160,8,128]{2,1,0:T(8,128)S(1)}, u32[]{:S(2)}, u32[]{:S(2)}) collective-permute-start(f32[160,8,128]{2,1,0:T(8,128)S(1)} %get-tuple-element.19), channel_id=1, source_target_pairs={{32,64},{96,128},{160,192},{64,32},{128,96},{192,160},{33,65},{97,... | collective-permute-start | bytes 1966088 | tf_op jit(solution)/shard_map/ppermute | solution.py:564
  44.1 13.9 %collective-permute-start.7 = (f32[8,8,128]{2,1,0:T(8,128)S(1)}, f32[8,8,128]{2,1,0:T(8,128)S(1)}, u32[]{:S(2)}, u32[]{:S(2)}) collective-permute-start(f32[8,8,128]{2,1,0:T(8,128)S(1)} %get-tuple-element.14), channel_id=1, source_target_pairs={{8,16},{16,8},{9,17},{17,9},{10,18},{18,10},{11,19},{19,11},{12,20... | collective-permute-start | bytes 98312 | tf_op jit(solution)/shard_map/ppermute | solution.py:564
  44.8 13.2 %collective-permute-start.6 = (f32[8,8,128]{2,1,0:T(8,128)S(1)}, f32[8,8,128]{2,1,0:T(8,128)S(1)}, u32[]{:S(2)}, u32[]{:S(2)}) collective-permute-start(f32[8,8,128]{2,1,0:T(8,128)S(1)} %get-tuple-element.14), channel_id=1, source_target_pairs={{0,8},{8,0},{16,24},{24,16},{1,9},{9,1},{17,25},{25,17},{2,10},{10... | collective-permute-start | bytes 98312 | tf_op jit(solution)/shard_map/ppermute | solution.py:565
  48.5 18.7 %all-to-all-start = ((f32[32,8,128]{2,1,0:T(8,128)}), f32[32,8,128]{2,1,0:T(8,128)S(1)}, u32[]{:S(2)}, u32[]{:S(2)}) async-start(f32[32,8,128]{2,1,0:T(8,128)} %broadcast_in_dim.2), calls=%async_computation | async-start | bytes 262144 | tf_op jit(solution)/shard_map/all_to_all | solution.py:621
  58.0 12.5 %collective-permute-start.8 = (f32[2,8,8,128]{3,2,1,0:T(8,128)S(1)}, f32[2,8,8,128]{3,2,1,0:T(8,128)S(1)}, u32[]{:S(2)}, u32[]{:S(2)}) collective-permute-start(f32[2,8,8,128]{3,2,1,0:T(8,128)S(1)} %pad_maximum_fusion.6), channel_id=1, source_target_pairs={{1,2},{3,4},{5,6},{2,1},{4,3},{6,5},{9,10},{11,12},{13,14},{10,9},... | collective-permute-start | bytes 196616 | tf_op jit(solution)/shard_map/ppermute | solution.py:564
  58.7 11.8 %collective-permute-start.9 = (f32[2,8,8,128]{3,2,1,0:T(8,128)S(1)}, f32[2,8,8,128]{3,2,1,0:T(8,128)S(1)}, u32[]{:S(2)}, u32[]{:S(2)}) collective-permute-start(f32[2,8,8,128]{3,2,1,0:T(8,128)S(1)} %pad_maximum_fusion.6), channel_id=1, source_target_pairs={{0,1},{1,0},{2,3},{3,2},{4,5},{5,4},{6,7},{7,6},{8,9},{9,8},{10,11... | collective-permute-start | bytes 196616 | tf_op jit(solution)/shard_map/ppermute | solution.py:565
  67.2 7.3 %collective-permute-start.14 = (f32[32,8,128]{2,1,0:T(8,128)S(1)}, f32[32,8,128]{2,1,0:T(8,128)S(1)}, u32[]{:S(2)}, u32[]{:S(2)}) collective-permute-start(f32[32,8,128]{2,1,0:T(8,128)S(1)} %bitcast.69), channel_id=1, source_target_pairs={{0,192},{64,128},{128,64},{192,0},{1,193},{65,129},{129,65},{193,1... | collective-permute-start | bytes 393224 | tf_op jit(solution)/shard_map/ppermute | solution.py:657
  67.3 7.2 %collective-permute-start.13 = (f32[32,8,128]{2,1,0:T(8,128)S(1)}, f32[32,8,128]{2,1,0:T(8,128)S(1)}, u32[]{:S(2)}, u32[]{:S(2)}) collective-permute-start(f32[32,8,128]{2,1,0:T(8,128)S(1)} %bitcast.70), channel_id=1, source_target_pairs={{0,128},{64,192},{128,0},{192,64},{1,129},{65,193},{129,1},{193,65... | collective-permute-start | bytes 393224 | tf_op jit(solution)/shard_map/ppermute | solution.py:657
  70.4 4.2 %collective-permute-start.12 = (f32[32,8,128]{2,1,0:T(8,128)S(1)}, f32[32,8,128]{2,1,0:T(8,128)S(1)}, u32[]{:S(2)}, u32[]{:S(2)}) collective-permute-start(f32[32,8,128]{2,1,0:T(8,128)S(1)} %bitcast.71), channel_id=1, source_target_pairs={{0,64},{64,0},{128,192},{192,128},{1,65},{65,1},{129,193},{193,129... | collective-permute-start | bytes 393224 | tf_op jit(solution)/shard_map/ppermute | solution.py:657
  74.7 7.3 %collective-permute-start.15 = (f32[128,8,128]{2,1,0:T(8,128)S(1)}, f32[128,8,128]{2,1,0:T(8,128)S(1)}, u32[]{:S(2)}, u32[]{:S(2)}) collective-permute-start(f32[128,8,128]{2,1,0:T(8,128)S(1)} %pad_maximum_fusion.1.mine_ref), channel_id=1, source_target_pairs={{0,32},{32,0},{1,33},{33,1},{2,34},{34,2},{3,35},{35,3},{4,36},{36... | collective-permute-start | bytes 1572872 | tf_op jit(solution)/shard_map/ppermute | solution.py:659
  78.9 9.8 %collective-permute-start.10 = (f32[2,7,24,128]{3,2,1,0:T(8,128)S(1)}, f32[2,7,24,128]{3,2,1,0:T(8,128)S(1)}, u32[]{:S(2)}, u32[]{:S(2)}) collective-permute-start(f32[2,7,24,128]{3,2,1,0:T(8,128)S(1)} %get-tuple-element.37), channel_id=1, source_target_pairs={{0,32},{32,0},{64,96},{96,64},{128,160},{160,128},{192,224},{224,1... | collective-permute-start | bytes 516104 | tf_op jit(solution)/shard_map/ppermute | solution.py:565
  79.0 9.7 %collective-permute-start.11 = (f32[2,7,24,128]{3,2,1,0:T(8,128)S(1)}, f32[2,7,24,128]{3,2,1,0:T(8,128)S(1)}, u32[]{:S(2)}, u32[]{:S(2)}) collective-permute-start(f32[2,7,24,128]{3,2,1,0:T(8,128)S(1)} %get-tuple-element.36), channel_id=1, source_target_pairs={{32,64},{96,128},{160,192},{64,32},{128,96},{192,160},{33,65},{97,... | collective-permute-start | bytes 516104 | tf_op jit(solution)/shard_map/ppermute | solution.py:564

commit v6 on v5

--- a/solution.py
+++ b/solution.py
@@ -326,33 +326,36 @@
     half_sweep_rb(black, red, c, g, 1, 5, XD - 5, 0, 12)
 
     def residual_body(i, carry):
-        r = residuals_rb(u, c, g, w, 6, 6 + 8 * i, 8, 0)
-        for k in range(4):
-            q[0, 4 * i + k + 3] = (r[0][2 * k] + r[0][2 * k + 1]) + (r[1][2 * k] + r[1][2 * k + 1])
+        r = residuals_rb(u, c, g, w, 6, 6 + 16 * i, 16, 0)
+        for k in range(8):
+            both = (r[0][2 * k] + r[0][2 * k + 1]) + (r[1][2 * k] + r[1][2 * k + 1])
+            q[0, 8 * i + k + 3, 8 : ZD - 8] = both[8 : ZD - 8]
+            q[0, 8 * i + k + 3, :8] = q[0, 8 * i + k + 3, ZD - 8 :] = jnp.zeros((8, LANES), F32)
         return carry
 
-    lax.fori_loop(0, 4, residual_body, 0)
+    lax.fori_loop(0, 2, residual_body, 0)
     nothing = jnp.zeros((ZD, LANES), F32)
     for i in (0, 1, 2, 19, 20, 21):
         q[0, i] = nothing
 
-    def coefficient_body(i, carry):
-        q[1, i] = (s[0, 2 * i] + s[0, 2 * i + 1]) + (s[1, 2 * i] + s[1, 2 * i + 1])
-        return carry
-
-    lax.fori_loop(0, X1, coefficient_body, 0)
+    def coefficients(x, n):
+        for i in range(n):
+            a, b = 2 * (x + i), 2 * (x + i) + 1
+            q[1, x + i] = (s[0, a] + s[0, b]) + (s[1, a] + s[1, b])
+
+    stepped(coefficients, 0, X1, 11)
     sl = s1_out
     for i, ref in enumerate((fl, sl)):
         ref[...] = 0.125 * (q[i, :, pl.ds(0, Z1, stride=2), :] + q[i, :, pl.ds(1, Z1, stride=2), :])
 
-    def top_body(i, carry):
-        for col in range(2):
-            top_out[col, i] = s[col, HD - H0 + i, 8 : ZD - 8]
-            top_out[2 + col, i] = f[col, HD - H0 + i, 8 : ZD - 8]
-        top_out[4, i] = black[HD - H0 + i, 8 : ZD - 8]
-        return carry
-
-    lax.fori_loop(0, X0, top_body, 0)
+    def keep(x, n):
+        for i in range(n):
+            for col in range(2):
+                top_out[col, x + i] = s[col, HD - H0 + x + i, 8 : ZD - 8]
+                top_out[2 + col, x + i] = f[col, HD - H0 + x + i, 8 : ZD - 8]
+            top_out[4, x + i] = black[HD - H0 + x + i, 8 : ZD - 8]
+
+    stepped(keep, 0, X0, 13)
     couplings(sl, fl, cl, gl, wl, 3, X1 - 3, 4.0, step=8)
     first_half_sweep(ul, gl, 3, X1 - 3, H1, step=8)
     half_sweep(ul, cl, gl, 4, X1 - 4, H1 + 1, step=8)

time: 94.3 us -> 93.7 us (level)
  no operation moved by 1% of the time
where the time goes in v6:
time: 93.7 us; the launch traced here: 93.4 us
  starting transfers between devices  44.6 us (48%)
  waiting for transfers between devices  25.1 us (27%)
  Pallas kernels  19.9 us (21%)
  other arithmetic  1.54 us (2%)
  between operations  1.14 us (1%)
  local copies, waits for them, and re-layouts  1.12 us (1%)
    pallas_call x4, Pallas kernels, run(): pl.pallas_call(kernel, out_shape=out_shape, in_specs=specs, out_specs=jax...  19.9 us
    ppermute x6, starting transfers between devices, exchange(): a = lax.ppermute(jnp.where(even, high, low), axis, first)  18.9 us
    all_to_all x1, starting transfers between devices, spread(): return lax.all_to_all(jnp.broadcast_to(x[None], (n,) + x.shape), axes, 0, 0)  9.51 us
    ppermute x6, waiting for transfers between devices, exchange(): b = lax.ppermute(jnp.where(even, low, high), axis, second)  8.77 us
    ppermute x6, starting transfers between devices, exchange(): b = lax.ppermute(jnp.where(even, low, high), axis, second)  8.65 us
    ppermute x6, waiting for transfers between devices, exchange(): a = lax.ppermute(jnp.where(even, high, low), axis, first)  7.56 us
    all_to_all x1, waiting for transfers between devices, spread(): return lax.all_to_all(jnp.broadcast_to(x[None], (n,) + x.shape), axes, 0, 0)  4.68 us
    ppermute x1, starting transfers between devices, on_device(): other = lax.ppermute(mine, 'co', [(0, 1), (1, 0)])  4.18 us
  transfers between devices with their start and end apart: 17, of which 6 were waited for; matrix products, arithmetic and copies ran while one was open for 1% of the time, Pallas kernels for 7%

profile of v6, /device:TPU:1, one launch (start us, length us, event | category | flops | bytes accessed | tf_op | source)
XLA Modules:
  0.0 93.4 jit_solution(7161968505221171215)
XLA Ops:
  0.6 1.0 %pad_maximum_fusion.3.in_ref = f32[2,16,16,128]{3,2,1,0:T(8,128)S(1)} fusion(f32[1,16,16,128]{3,2,1,0:T(8,128)} %bitcast.83, f32[1,16,16,128]{3,2,1,0:T(8,128)} %bitcast.84), kind=kLoop, calls=%fused_computation.9 | loop fusion | flops 65536 | bytes 524288 | tf_op jit(solution)/shard_map/stack | solution.py:647
  1.6 0.5 shard_map.41
  2.1 0.7 collective-permute-start.1
  2.8 4.6 %collective-permute-start = (f32[4,2,16,128]{3,2,1,0:T(8,128)S(1)}, f32[4,2,16,128]{3,2,1,0:T(8,128)S(1)}, u32[]{:S(2)}, u32[]{:S(2)}) collective-permute-start(f32[4,2,16,128]{3,2,1,0:T(8,128)S(1)} %get-tuple-element.44), channel_id=1, source_target_pairs={{0,8},{8,0},{16,24},{24,16},{1,9},{9,1},{17,25},{25,17},{2,10},{10... | collective-permute-start | bytes 196616 | tf_op jit(solution)/shard_map/ppermute | solution.py:568
  7.4 0.0 collective-permute-done.1
  7.4 1.6 %collective-permute-done = f32[4,2,16,128]{3,2,1,0:T(8,128)S(1)} collective-permute-done((f32[4,2,16,128]{3,2,1,0:T(8,128)S(1)}, f32[4,2,16,128]{3,2,1,0:T(8,128)S(1)}, u32[]{:S(2)}, u32[]{:S(2)}) %collective-permute-start) | collective-permute-done | bytes 65568 | tf_op jit(solution)/shard_map/ppermute | solution.py:568
  9.1 0.7 collective-permute-start.2
  9.8 4.6 %collective-permute-start.3 = (f32[80,8,128]{2,1,0:T(8,128)S(1)}, f32[80,8,128]{2,1,0:T(8,128)S(1)}, u32[]{:S(2)}, u32[]{:S(2)}) collective-permute-start(f32[80,8,128]{2,1,0:T(8,128)S(1)} %pad_maximum_fusion.2), channel_id=1, source_target_pairs={{0,1},{1,0},{2,3},{3,2},{4,5},{5,4},{6,7},{7,6},{8,9},{9,8},{10,11... | collective-permute-start | bytes 983048 | tf_op jit(solution)/shard_map/ppermute | solution.py:568
  14.4 0.0 collective-permute-done.2
  14.4 5.9 %collective-permute-done.3 = f32[80,8,128]{2,1,0:T(8,128)S(1)} collective-permute-done((f32[80,8,128]{2,1,0:T(8,128)S(1)}, f32[80,8,128]{2,1,0:T(8,128)S(1)}, u32[]{:S(2)}, u32[]{:S(2)}) %collective-permute-start.3) | collective-permute-done | bytes 327712 | tf_op jit(solution)/shard_map/ppermute | solution.py:568
  20.4 0.1 pad_maximum_fusion.e
  20.5 0.1 slice_bitcast_fusion
  21.0 0.1 broadcast_select_fusion.2
  21.0 2.8 %collective-permute-start.5 = (f32[160,8,128]{2,1,0:T(8,128)S(1)}, f32[160,8,128]{2,1,0:T(8,128)S(1)}, u32[]{:S(2)}, u32[]{:S(2)}) collective-permute-start(f32[160,8,128]{2,1,0:T(8,128)S(1)} %get-tuple-element.18), channel_id=1, source_target_pairs={{0,32},{32,0},{64,96},{96,64},{128,160},{160,128},{192,224},{224,1... | collective-permute-start | bytes 1966088 | tf_op jit(solution)/shard_map/ppermute | solution.py:568
  23.9 3.1 %collective-permute-start.4 = (f32[160,8,128]{2,1,0:T(8,128)S(1)}, f32[160,8,128]{2,1,0:T(8,128)S(1)}, u32[]{:S(2)}, u32[]{:S(2)}) collective-permute-start(f32[160,8,128]{2,1,0:T(8,128)S(1)} %get-tuple-element.19), channel_id=1, source_target_pairs={{32,64},{96,128},{160,192},{64,32},{128,96},{192,160},{33,65},{97,... | collective-permute-start | bytes 1966088 | tf_op jit(solution)/shard_map/ppermute | solution.py:567
  27.0 0.0 collective-permute-done.5
  27.0 8.8 %collective-permute-done.4 = f32[160,8,128]{2,1,0:T(8,128)S(1)} collective-permute-done((f32[160,8,128]{2,1,0:T(8,128)S(1)}, f32[160,8,128]{2,1,0:T(8,128)S(1)}, u32[]{:S(2)}, u32[]{:S(2)}) %collective-permute-start.4) | collective-permute-done | bytes 655392 | tf_op jit(solution)/shard_map/ppermute | solution.py:567
  35.8 0.1 broadcast_select_fusion
  36.1 7.4 %shard_map.42 = (f32[5,26,32,128]{3,2,1,0:T(8,128)S(1)}, f32[22,24,128]{2,1,0:T(8,128)S(1)}, f32[8,8,128]{2,1,0:T(8,128)S(1)}, f32[8,128]{1,0:T(8,128)S(1)}) custom-call(f32[2,16,48,128]{3,2,1,0:T(8,128)S(1)} %pad_maximum_fusion.e, f32[4,2,48,128]{3,2,1,0:T(8,128)S(1)} %pad_maximum_fusion.4.b, f32[5,48,128]{2,1,0:T(8,128)S(1)} %bitcast.51, ...), custom_call_target="tpu_custom_call" | custom-call | flops 4000000 | bytes 12000000 | tf_op jit(solution)/shard_map/pallas_call | solution.py:280
  43.5 0.7 collective-permute-start.7
  44.2 3.0 %collective-permute-start.6 = (f32[8,8,128]{2,1,0:T(8,128)S(1)}, f32[8,8,128]{2,1,0:T(8,128)S(1)}, u32[]{:S(2)}, u32[]{:S(2)}) collective-permute-start(f32[8,8,128]{2,1,0:T(8,128)S(1)} %get-tuple-element.14), channel_id=1, source_target_pairs={{0,8},{8,0},{16,24},{24,16},{1,9},{9,1},{17,25},{25,17},{2,10},{10... | collective-permute-start | bytes 98312 | tf_op jit(solution)/shard_map/ppermute | solution.py:568
  47.2 0.7 broadcast_in_dim.2
  47.9 9.5 %all-to-all-start = ((f32[32,8,128]{2,1,0:T(8,128)}), f32[32,8,128]{2,1,0:T(8,128)S(1)}, u32[]{:S(2)}, u32[]{:S(2)}) async-start(f32[32,8,128]{2,1,0:T(8,128)} %broadcast_in_dim.2), calls=%async_computation | async-start | bytes 262144 | tf_op jit(solution)/shard_map/all_to_all | solution.py:624
  57.4 0.0 collective-permute-done.7
  57.4 0.0 collective-permute-done.6
  57.4 0.7 collective-permute-start.8
  58.1 3.7 %collective-permute-start.9 = (f32[2,8,8,128]{3,2,1,0:T(8,128)S(1)}, f32[2,8,8,128]{3,2,1,0:T(8,128)S(1)}, u32[]{:S(2)}, u32[]{:S(2)}) collective-permute-start(f32[2,8,8,128]{3,2,1,0:T(8,128)S(1)} %pad_maximum_fusion.6), channel_id=1, source_target_pairs={{0,1},{1,0},{2,3},{3,2},{4,5},{5,4},{6,7},{7,6},{8,9},{9,8},{10,11... | collective-permute-start | bytes 196616 | tf_op jit(solution)/shard_map/ppermute | solution.py:568
  61.9 4.7 %all-to-all-done = f32[32,8,128]{2,1,0:T(8,128)S(1)} async-done(((f32[32,8,128]{2,1,0:T(8,128)}), f32[32,8,128]{2,1,0:T(8,128)S(1)}, u32[]{:S(2)}, u32[]{:S(2)}) %all-to-all-start) | async-done | bytes 131104 | tf_op jit(solution)/shard_map/all_to_all | solution.py:624
  66.6 0.1 collective-permute-start.14
  66.7 3.2 %collective-permute-start.13 = (f32[32,8,128]{2,1,0:T(8,128)S(1)}, f32[32,8,128]{2,1,0:T(8,128)S(1)}, u32[]{:S(2)}, u32[]{:S(2)}) collective-permute-start(f32[32,8,128]{2,1,0:T(8,128)S(1)} %bitcast.70), channel_id=1, source_target_pairs={{0,128},{64,192},{128,0},{192,64},{1,129},{65,193},{129,1},{193,65... | collective-permute-start | bytes 393224 | tf_op jit(solution)/shard_map/ppermute | solution.py:660
  69.8 0.1 collective-permute-start.12
  69.9 0.0 collective-permute-done.8
  69.9 0.0 collective-permute-done.9
  69.9 3.9 %collective-permute-done.14 = f32[32,8,128]{2,1,0:T(8,128)S(1)} collective-permute-done((f32[32,8,128]{2,1,0:T(8,128)S(1)}, f32[32,8,128]{2,1,0:T(8,128)S(1)}, u32[]{:S(2)}, u32[]{:S(2)}) %collective-permute-start.14) | collective-permute-done | bytes 131104 | tf_op jit(solution)/shard_map/ppermute | solution.py:660
  73.9 0.0 collective-permute-done.13
  73.9 0.2 collective-permute-done.12
  74.1 4.2 %collective-permute-start.15 = (f32[128,8,128]{2,1,0:T(8,128)S(1)}, f32[128,8,128]{2,1,0:T(8,128)S(1)}, u32[]{:S(2)}, u32[]{:S(2)}) collective-permute-start(f32[128,8,128]{2,1,0:T(8,128)S(1)} %pad_maximum_fusion.1.mine_ref), channel_id=1, source_target_pairs={{0,32},{32,0},{1,33},{33,1},{2,34},{34,2},{3,35},{35,3},{4,36},{36... | collective-permute-start | bytes 1572872 | tf_op jit(solution)/shard_map/ppermute | solution.py:662
  78.3 0.1 collective-permute-start.10
  78.4 2.9 %collective-permute-start.11 = (f32[2,7,24,128]{3,2,1,0:T(8,128)S(1)}, f32[2,7,24,128]{3,2,1,0:T(8,128)S(1)}, u32[]{:S(2)}, u32[]{:S(2)}) collective-permute-start(f32[2,7,24,128]{3,2,1,0:T(8,128)S(1)} %get-tuple-element.36), channel_id=1, source_target_pairs={{32,64},{96,128},{160,192},{64,32},{128,96},{192,160},{33,65},{97,... | collective-permute-start | bytes 516104 | tf_op jit(solution)/shard_map/ppermute | solution.py:567
  81.3 0.1 pad_add_fusion.where_ref
  81.4 0.0 collective-permute-done.15.other_ref
  81.4 6.7 %shard_map.43.win = f32[2,12,16,128]{3,2,1,0:T(8,128)S(1)} custom-call(s32[3]{0:T(128)S(1)} %pad_add_fusion.where_ref, f32[128,8,128]{2,1,0:T(8,128)S(1)} %pad_maximum_fusion.1.mine_ref, f32[128,8,128]{2,1,0:T(8,128)S(1)} %collective-permute-done.15.other_ref), custom_call_target="tpu_custom_call" | custom-call | flops 10000000 | bytes 30000000 | tf_op jit(solution)/shard_map/pallas_call | solution.py:280
  88.1 0.0 collective-permute-done.10.ma
  88.1 0.0 collective-permute-done.11.mb
  88.1 5.3 %shard_map.44 = (f32[16,16,128]{2,1,0:T(8,128)}, f32[16,16,128]{2,1,0:T(8,128)}) custom-call(s32[3]{0:T(128)S(1)} %pad_add_fusion.where_ref, f32[5,26,32,128]{3,2,1,0:T(8,128)S(1)} %get-tuple-element.12.top, f32[22,24,128]{2,1,0:T(8,128)S(1)} %get-tuple-element.13.sl, f32[2,8,24,128]{3,2,1,0:T(8,128)S(1)} %pad_maximum_fusion.5.m, ...), custom_call_target="tpu_custom_call" | custom-call | flops 4000000 | bytes 12000000 | tf_op jit(solution)/shard_map/pallas_call | solution.py:280
  (48 shorter events, 0.6 us)
Async XLA Ops:
  2.1 5.3 %collective-permute-start.1 = (f32[4,2,16,128]{3,2,1,0:T(8,128)S(1)}, f32[4,2,16,128]{3,2,1,0:T(8,128)S(1)}, u32[]{:S(2)}, u32[]{:S(2)}) collective-permute-start(f32[4,2,16,128]{3,2,1,0:T(8,128)S(1)} %get-tuple-element.45), channel_id=1, source_target_pairs={{8,16},{16,8},{9,17},{17,9},{10,18},{18,10},{11,19},{19,11},{12,20... | collective-permute-start | bytes 196616 | tf_op jit(solution)/shard_map/ppermute | solution.py:567
  2.8 6.2 %collective-permute-start = (f32[4,2,16,128]{3,2,1,0:T(8,128)S(1)}, f32[4,2,16,128]{3,2,1,0:T(8,128)S(1)}, u32[]{:S(2)}, u32[]{:S(2)}) collective-permute-start(f32[4,2,16,128]{3,2,1,0:T(8,128)S(1)} %get-tuple-element.44), channel_id=1, source_target_pairs={{0,8},{8,0},{16,24},{24,16},{1,9},{9,1},{17,25},{25,17},{2,10},{10... | collective-permute-start | bytes 196616 | tf_op jit(solution)/shard_map/ppermute | solution.py:568
  9.1 5.3 %collective-permute-start.2 = (f32[80,8,128]{2,1,0:T(8,128)S(1)}, f32[80,8,128]{2,1,0:T(8,128)S(1)}, u32[]{:S(2)}, u32[]{:S(2)}) collective-permute-start(f32[80,8,128]{2,1,0:T(8,128)S(1)} %pad_maximum_fusion.2), channel_id=1, source_target_pairs={{1,2},{3,4},{5,6},{2,1},{4,3},{6,5},{9,10},{11,12},{13,14},{10,9},... | collective-permute-start | bytes 983048 | tf_op jit(solution)/shard_map/ppermute | solution.py:567
  9.8 10.5 %collective-permute-start.3 = (f32[80,8,128]{2,1,0:T(8,128)S(1)}, f32[80,8,128]{2,1,0:T(8,128)S(1)}, u32[]{:S(2)}, u32[]{:S(2)}) collective-permute-start(f32[80,8,128]{2,1,0:T(8,128)S(1)} %pad_maximum_fusion.2), channel_id=1, source_target_pairs={{0,1},{1,0},{2,3},{3,2},{4,5},{5,4},{6,7},{7,6},{8,9},{9,8},{10,11... | collective-permute-start | bytes 983048 | tf_op jit(solution)/shard_map/ppermute | solution.py:568
  21.0 6.0 %collective-permute-start.5 = (f32[160,8,128]{2,1,0:T(8,128)S(1)}, f32[160,8,128]{2,1,0:T(8,128)S(1)}, u32[]{:S(2)}, u32[]{:S(2)}) collective-permute-start(f32[160,8,128]{2,1,0:T(8,128)S(1)} %get-tuple-element.18), channel_id=1, source_target_pairs={{0,32},{32,0},{64,96},{96,64},{128,160},{160,128},{192,224},{224,1... | collective-permute-start | bytes 1966088 | tf_op jit(solution)/shard_map/ppermute | solution.py:568
  23.9 11.9 %collective-permute-start.4 = (f32[160,8,128]{2,1,0:T(8,128)S(1)}, f32[160,8,128]{2,1,0:T(8,128)S(1)}, u32[]{:S(2)}, u32[]{:S(2)}) collective-permute-start(f32[160,8,128]{2,1,0:T(8,128)S(1)} %get-tuple-element.19), channel_id=1, source_target_pairs={{32,64},{96,128},{160,192},{64,32},{128,96},{192,160},{33,65},{97,... | collective-permute-start | bytes 1966088 | tf_op jit(solution)/shard_map/ppermute | solution.py:567
  43.5 13.9 %collective-permute-start.7 = (f32[8,8,128]{2,1,0:T(8,128)S(1)}, f32[8,8,128]{2,1,0:T(8,128)S(1)}, u32[]{:S(2)}, u32[]{:S(2)}) collective-permute-start(f32[8,8,128]{2,1,0:T(8,128)S(1)} %get-tuple-element.14), channel_id=1, source_target_pairs={{8,16},{16,8},{9,17},{17,9},{10,18},{18,10},{11,19},{19,11},{12,20... | collective-permute-start | bytes 98312 | tf_op jit(solution)/shard_map/ppermute | solution.py:567
  44.2 13.2 %collective-permute-start.6 = (f32[8,8,128]{2,1,0:T(8,128)S(1)}, f32[8,8,128]{2,1,0:T(8,128)S(1)}, u32[]{:S(2)}, u32[]{:S(2)}) collective-permute-start(f32[8,8,128]{2,1,0:T(8,128)S(1)} %get-tuple-element.14), channel_id=1, source_target_pairs={{0,8},{8,0},{16,24},{24,16},{1,9},{9,1},{17,25},{25,17},{2,10},{10... | collective-permute-start | bytes 98312 | tf_op jit(solution)/shard_map/ppermute | solution.py:568
  47.9 18.7 %all-to-all-start = ((f32[32,8,128]{2,1,0:T(8,128)}), f32[32,8,128]{2,1,0:T(8,128)S(1)}, u32[]{:S(2)}, u32[]{:S(2)}) async-start(f32[32,8,128]{2,1,0:T(8,128)} %broadcast_in_dim.2), calls=%async_computation | async-start | bytes 262144 | tf_op jit(solution)/shard_map/all_to_all | solution.py:624
  57.4 12.5 %collective-permute-start.8 = (f32[2,8,8,128]{3,2,1,0:T(8,128)S(1)}, f32[2,8,8,128]{3,2,1,0:T(8,128)S(1)}, u32[]{:S(2)}, u32[]{:S(2)}) collective-permute-start(f32[2,8,8,128]{3,2,1,0:T(8,128)S(1)} %pad_maximum_fusion.6), channel_id=1, source_target_pairs={{1,2},{3,4},{5,6},{2,1},{4,3},{6,5},{9,10},{11,12},{13,14},{10,9},... | collective-permute-start | bytes 196616 | tf_op jit(solution)/shard_map/ppermute | solution.py:567
  58.1 11.8 %collective-permute-start.9 = (f32[2,8,8,128]{3,2,1,0:T(8,128)S(1)}, f32[2,8,8,128]{3,2,1,0:T(8,128)S(1)}, u32[]{:S(2)}, u32[]{:S(2)}) collective-permute-start(f32[2,8,8,128]{3,2,1,0:T(8,128)S(1)} %pad_maximum_fusion.6), channel_id=1, source_target_pairs={{0,1},{1,0},{2,3},{3,2},{4,5},{5,4},{6,7},{7,6},{8,9},{9,8},{10,11... | collective-permute-start | bytes 196616 | tf_op jit(solution)/shard_map/ppermute | solution.py:568
  66.6 7.3 %collective-permute-start.14 = (f32[32,8,128]{2,1,0:T(8,128)S(1)}, f32[32,8,128]{2,1,0:T(8,128)S(1)}, u32[]{:S(2)}, u32[]{:S(2)}) collective-permute-start(f32[32,8,128]{2,1,0:T(8,128)S(1)} %bitcast.69), channel_id=1, source_target_pairs={{0,192},{64,128},{128,64},{192,0},{1,193},{65,129},{129,65},{193,1... | collective-permute-start | bytes 393224 | tf_op jit(solution)/shard_map/ppermute | solution.py:660
  66.7 7.2 %collective-permute-start.13 = (f32[32,8,128]{2,1,0:T(8,128)S(1)}, f32[32,8,128]{2,1,0:T(8,128)S(1)}, u32[]{:S(2)}, u32[]{:S(2)}) collective-permute-start(f32[32,8,128]{2,1,0:T(8,128)S(1)} %bitcast.70), channel_id=1, source_target_pairs={{0,128},{64,192},{128,0},{192,64},{1,129},{65,193},{129,1},{193,65... | collective-permute-start | bytes 393224 | tf_op jit(solution)/shard_map/ppermute | solution.py:660
  69.8 4.2 %collective-permute-start.12 = (f32[32,8,128]{2,1,0:T(8,128)S(1)}, f32[32,8,128]{2,1,0:T(8,128)S(1)}, u32[]{:S(2)}, u32[]{:S(2)}) collective-permute-start(f32[32,8,128]{2,1,0:T(8,128)S(1)} %bitcast.71), channel_id=1, source_target_pairs={{0,64},{64,0},{128,192},{192,128},{1,65},{65,1},{129,193},{193,129... | collective-permute-start | bytes 393224 | tf_op jit(solution)/shard_map/ppermute | solution.py:660
  74.1 7.3 %collective-permute-start.15 = (f32[128,8,128]{2,1,0:T(8,128)S(1)}, f32[128,8,128]{2,1,0:T(8,128)S(1)}, u32[]{:S(2)}, u32[]{:S(2)}) collective-permute-start(f32[128,8,128]{2,1,0:T(8,128)S(1)} %pad_maximum_fusion.1.mine_ref), channel_id=1, source_target_pairs={{0,32},{32,0},{1,33},{33,1},{2,34},{34,2},{3,35},{35,3},{4,36},{36... | collective-permute-start | bytes 1572872 | tf_op jit(solution)/shard_map/ppermute | solution.py:662
  78.3 9.8 %collective-permute-start.10 = (f32[2,7,24,128]{3,2,1,0:T(8,128)S(1)}, f32[2,7,24,128]{3,2,1,0:T(8,128)S(1)}, u32[]{:S(2)}, u32[]{:S(2)}) collective-permute-start(f32[2,7,24,128]{3,2,1,0:T(8,128)S(1)} %get-tuple-element.37), channel_id=1, source_target_pairs={{0,32},{32,0},{64,96},{96,64},{128,160},{160,128},{192,224},{224,1... | collective-permute-start | bytes 516104 | tf_op jit(solution)/shard_map/ppermute | solution.py:568
  78.4 9.7 %collective-permute-start.11 = (f32[2,7,24,128]{3,2,1,0:T(8,128)S(1)}, f32[2,7,24,128]{3,2,1,0:T(8,128)S(1)}, u32[]{:S(2)}, u32[]{:S(2)}) collective-permute-start(f32[2,7,24,128]{3,2,1,0:T(8,128)S(1)} %get-tuple-element.36), channel_id=1, source_target_pairs={{32,64},{96,128},{160,192},{64,32},{128,96},{192,160},{33,65},{97,... | collective-permute-start | bytes 516104 | tf_op jit(solution)/shard_map/ppermute | solution.py:567
